TPU v7x, 32 devices: a whole 2x2x4 slice. The times are simulated.
32 devices in a mesh: grp: 2 (over y), row: 8 (over z, x), col: 2 (over core).
Axes of the slice: x: 2, y: 2, z: 4, core: 2. Of those that a mesh axis runs over, the one named last changes fastest.
Arguments:
- feats: bfloat16 [128, 128, 256], P(('grp', 'row'), 'col'), parts along dimension 0, may hold values from -6 to 6
- weight: bfloat16 [256, 256], replicated, may hold values from -0.375 to 0.375
- degree: int32 [128, 128], P(('grp', 'row'), 'col'), parts along dimension 0, may hold values from 0 to 63
- tile_cols: int32 [128, 16], P(('grp', 'row')), parts along dimension 0, may hold values from -1 to 63, as said below
- adjacency: int32 [2048, 128, 128], P(('grp', 'row'), 'col'), parts along dimension 0, may hold values 0 or 1
- cotangent: bfloat16 [128, 128, 256], P(('grp', 'row'), 'col'), parts along dimension 0, may hold values from -6 to 6
Outputs:
- output: bfloat16 [128, 128, 256], P(('grp', 'row'), 'col'), parts along dimension 0
- grad_feats: bfloat16 [128, 128, 256], P(('grp', 'row'), 'col'), parts along dimension 0
There are 2 independent parts, one for each index of `grp`. A program takes and returns all parts, laid end to end along the dimension named above; an argument that names none is the same for every part. Nothing has to cross between parts.
Inputs may be any that keep to these rules, and one draw needn't show every extreme that they name: `tile_cols`: in each row block's list the live slots (not -1) come first, at least one of them. Among the live slots of the 8 row blocks of one index of row, at most 16 have column blocks c with the same c // 8.
All inputs are finite; a program needn't handle non-finite values. No bound on the sum of `adjacency` on one device may be relied on, other than what follows from the above.
Results may differ from a plain program's by a relative error of at most 0.0063.
Values may be sent and summed in bfloat16 or wider, within the bound.
No kernel may reach another device: no remote copies, remote signals or barrier semaphores. Data moves between devices by JAX's collectives and lax.ppermute only.
A program may use at most 64 MiB of HBM per device.

v0:
```python
import jax
import jax.numpy as jnp
from jax import lax
from jax.sharding import PartitionSpec as P


def shards(feats, weight, degree, tile_cols, adjacency, cotangent):
    blocks, half_rows, feat_width = feats.shape
    slots_per = tile_cols.shape[1]
    tile_side = adjacency.shape[2]
    peer_count = lax.axis_size("row")
    tile_count = blocks * slots_per
    per_peer = (tile_count + peer_count - 1) // peer_count
    capacity = peer_count * per_peer
    columns = tile_cols.reshape(tile_count)
    is_live = columns >= 0
    owners = jnp.where(is_live, columns // blocks, -1)
    local_block = jnp.where(is_live, columns % blocks, -1)
    earlier = jnp.arange(tile_count)[:, None] > jnp.arange(tile_count)[None, :]
    same_owner = (owners[:, None] == owners[None, :]) & earlier & is_live[None, :]
    tile_rank = jnp.sum(same_owner.astype(jnp.int32), axis=1)
    target_slot = jnp.where(is_live, owners * per_peer + tile_rank, capacity)
    wanted = jnp.zeros((capacity,), jnp.int32).at[target_slot].set(local_block + 1, mode="drop")
    wanted = wanted.reshape(peer_count, per_peer)
    received = lax.all_to_all(wanted, "row", split_axis=0, concat_axis=0, tiled=True)
    incoming = received - 1
    scaling = lax.rsqrt(degree.astype(jnp.float32) + 1.0)[..., None]
    projected = jnp.dot(
        feats.reshape(blocks * half_rows, feat_width), weight, preferred_element_type=jnp.float32
    )
    sent_rows = (scaling * projected.reshape(blocks, half_rows, feat_width)).astype(jnp.bfloat16)
    tiles_bf = adjacency.astype(jnp.bfloat16).reshape(blocks, slots_per, half_rows, tile_side)
    pick_index = jnp.where(incoming < 0, blocks, incoming)
    replies = jnp.take(sent_rows, pick_index, axis=0, mode="fill", fill_value=0)
    fetched = lax.all_to_all(replies, "row", split_axis=0, concat_axis=0, tiled=True).reshape(
        capacity, half_rows, feat_width
    )
    tile_feats = jnp.take(fetched, target_slot, axis=0, mode="fill", fill_value=0)
    tile_feats = tile_feats.reshape(blocks, slots_per, half_rows, feat_width)
    gathered = lax.dot_general(
        tiles_bf, tile_feats, (((1, 2), (1, 2)), ((0,), (0,))), preferred_element_type=jnp.float32
    )
    own_rows = lax.psum_scatter(gathered, "col", scatter_dimension=1, tiled=True)
    mixed = scaling * (own_rows + sent_rows.astype(jnp.float32))
    sigmoid_z = jax.nn.sigmoid(mixed)
    output = (mixed * sigmoid_z).astype(jnp.bfloat16)
    silu_slope = sigmoid_z * (1.0 + mixed * (1.0 - sigmoid_z))
    back_sent = (scaling * cotangent.astype(jnp.float32) * silu_slope).astype(jnp.bfloat16)
    full_rows = lax.all_gather(back_sent, "col", axis=1, tiled=True)
    partials = lax.dot_general(
        tiles_bf, full_rows, (((3,), (1,)), ((0,), (0,))), preferred_element_type=jnp.float32
    )
    outgoing = jnp.zeros((capacity, half_rows, feat_width), jnp.float32)
    outgoing = outgoing.at[target_slot].set(
        partials.reshape(tile_count, half_rows, feat_width), mode="drop"
    )
    outgoing = outgoing.reshape(peer_count, per_peer, half_rows, feat_width)
    arrived = lax.all_to_all(outgoing, "row", split_axis=0, concat_axis=0, tiled=True).reshape(
        capacity, half_rows, feat_width
    )
    selector = (incoming.reshape(capacity)[:, None] == jnp.arange(blocks)[None, :]).astype(
        jnp.float32
    )
    returned = jnp.einsum("sl,sjf->ljf", selector, arrived, precision=lax.Precision.HIGHEST)
    combined = (scaling * (returned + back_sent.astype(jnp.float32))).astype(jnp.bfloat16)
    grad_rows = jnp.dot(
        combined.reshape(blocks * half_rows, feat_width),
        weight.T,
        preferred_element_type=jnp.float32,
    )
    return (output, grad_rows.astype(jnp.bfloat16).reshape(blocks, half_rows, feat_width))


def solution(mesh):
    in_specs = (
        P(("grp", "row"), "col", None),
        P(),
        P(("grp", "row"), "col"),
        P(("grp", "row"), None),
        P(("grp", "row"), "col", None),
        P(("grp", "row"), "col", None),
    )
    out_specs = (P(("grp", "row"), "col", None), P(("grp", "row"), "col", None))
    return jax.shard_map(shards, mesh=mesh, in_specs=in_specs, out_specs=out_specs, check_vma=False)
```

profile of v0, /device:TPU:0, one launch (start us, length us, event | category | flops | bytes accessed | tf_op | source)
XLA Modules:
  0.0 400.4 jit_solution(153186850545571925)
XLA Ops:
  7.2 0.8 reshape.243
  8.0 0.8 reshape.244
  8.8 0.2 convert_reduce_fusion
  9.0 1.0 scatter_custom_fusion
  10.0 0.7 all_to_all.12
  10.6 7.3 %all-to-all-start = ((s32[8,1,16]{2,1,0:T(1,128)}), s32[8,1,16]{2,1,0:T(1,128)S(1)}, u32[]{:S(2)}, u32[]{:S(2)}) async-start(s32[8,1,16]{2,1,0:T(1,128)} %bitcast.2), calls=%async_computation | async-start | bytes 8192 | tf_op jit(solution)/shard_map/all_to_all | solution.py:25
  17.9 0.7 add_rsqrt_fusion
  18.6 1.1 fusion.7
  19.7 4.6 %all-to-all-done = s32[8,1,16]{2,1,0:T(1,128)S(1)} async-done(((s32[8,1,16]{2,1,0:T(1,128)}), s32[8,1,16]{2,1,0:T(1,128)S(1)}, u32[]{:S(2)}, u32[]{:S(2)}) %all-to-all-start) | async-done | bytes 544 | tf_op jit(solution)/shard_map/all_to_all | solution.py:25
  24.3 0.1 reshape.254
  24.4 2.8 gather_fusion
  27.2 4.5 %broadcast_select_fusion = bf16[8,16,64,256]{3,2,1,0:T(8,128)(2,1)} fusion(bf16[8,16,64,256]{3,2,1,0:T(8,128)(2,1)} %bitcast.55, pred[8,16]{1,0:T(8,128)(4,1)S(1)} %compare_and_fusion), kind=kLoop, calls=%fused_computation.6 | loop fusion | flops 2097152 | bytes 8388736 | tf_op jit(solution)/shard_map/jit(_take)/select_n | solution.py:34
  31.7 4.5 %all-to-all-start.1 = ((bf16[8,16,64,256]{3,2,1,0:T(8,128)(2,1)}), bf16[8,16,64,256]{3,2,1,0:T(8,128)(2,1)}, u32[]{:S(2)}, u32[]{:S(2)}) async-start(bf16[8,16,64,256]{3,2,1,0:T(8,128)(2,1)} %broadcast_select_fusion), calls=%async_computation.1 | async-start | bytes 8388608 | tf_op jit(solution)/shard_map/all_to_all | solution.py:35
  36.3 0.1 reduce_sum.14
  36.4 2.7 convert_element_type.37
  39.2 89.1 %all-to-all-done.1 = bf16[8,16,64,256]{3,2,1,0:T(8,128)(2,1)} async-done(((bf16[8,16,64,256]{3,2,1,0:T(8,128)(2,1)}), bf16[8,16,64,256]{3,2,1,0:T(8,128)(2,1)}, u32[]{:S(2)}, u32[]{:S(2)}) %all-to-all-start.1) | async-done | bytes 4194336 | tf_op jit(solution)/shard_map/all_to_all | solution.py:35
  128.3 5.0 %gather_fusion.1 = bf16[128,64,256]{2,1,0:T(8,128)(2,1)} fusion(bf16[128,64,256]{2,1,0:T(8,128)(2,1)} %bitcast.8, s32[1024]{0:T(1024)S(1)} %pad_clamp_fusion), kind=kCustom, calls=%fused_computation.1 | custom fusion | bytes 8389120 | tf_op jit(solution)/shard_map/jit(_take)/gather | solution.py:38
  133.2 4.3 %fusion.4 = f32[8,128,256]{2,1,0:T(8,128)} fusion(bf16[8,16,64,128]{3,2,1,0:T(8,128)(2,1)S(1)} %bitcast.56, bf16[8,16,64,256]{3,2,1,0:T(8,128)(2,1)} %bitcast.58, pred[8,16]{1,0:T(8,128)(4,1)S(1)} %compare_and_fusion.1), kind=kOutput, calls=%fused_computation.9 | convolution fusion | flops 538968064 | bytes 7340160 | tf_op jit(solution)/shard_map/dot_general | solution.py:40
  137.5 7.8 %reduce-scatter.2.cloned.1.call-done = f32[8,64,256]{2,1,0:T(8,128)} async-done(((f32[8,128,256]{2,1,0:T(8,128)}), f32[8,64,256]{2,1,0:T(8,128)}) %reduce-scatter.2.cloned.1.call-update) | async-done | bytes 524304 | tf_op jit(solution)/shard_map/reduce_scatter | solution.py:43
  145.3 2.1 multiply_convert_fusion
  147.4 2.2 all_gather.3
  149.6 4.5 %fusion.8 = f32[8,256,16,64]{1,3,2,0:T(8,128)} fusion(bf16[8,16,64,128]{3,2,1,0:T(8,128)(2,1)S(1)} %bitcast.57, bf16[8,128,256]{2,1,0:T(8,128)(2,1)S(1)} %all_gather.3), kind=kOutput, calls=%fused_computation.13 | convolution fusion | flops 536870912 | bytes 11010048 | tf_op jit(solution)/shard_map/dot_general | solution.py:50
  154.0 4.3 %broadcast_in_dim.51 = f32[128,64,256]{2,1,0:T(8,128)} broadcast(f32[]{:T(128)} %constant.70.clone.1), dimensions={} | broadcast | bytes 8388612 | tf_op jit(solution)/shard_map/broadcast_in_dim | solution.py:53
  158.3 26.1 %scatter_fusion = f32[128,64,256]{2,1,0:T(8,128)} fusion(f32[128,64,256]{2,1,0:T(8,128)} %broadcast_in_dim.51, s32[128]{0:T(128)S(1)} %fusion.28, f32[128,64,256]{2,1,0:T(8,128)} %bitcast.53), kind=kCustom, calls=%fused_computation.3 | custom fusion | bytes 25166336 | tf_op jit(solution)/shard_map/scatter | solution.py:54
  184.4 11.4 %copy.22 = f32[8,16,64,256]{3,1,2,0:T(8,128)} copy(f32[8,16,64,256]{3,2,1,0:T(8,128)} %bitcast.52) | data formatting | bytes 16777216 | tf_op jit(solution)/shard_map/reshape | solution.py:57
  195.8 5.6 %all-to-all-start.2 = ((f32[8,16,64,256]{3,1,2,0:T(8,128)}), f32[8,16,64,256]{3,1,2,0:T(8,128)}, u32[]{:S(2)}, u32[]{:S(2)}) async-start(f32[8,16,64,256]{3,1,2,0:T(8,128)} %copy.22), calls=%async_computation.3 | async-start | bytes 16777216 | tf_op jit(solution)/shard_map/all_to_all | solution.py:58
  201.4 0.1 sub.29
  201.5 183.6 %all-to-all-done.2 = f32[8,16,64,256]{3,1,2,0:T(8,128)} async-done(((f32[8,16,64,256]{3,1,2,0:T(8,128)}), f32[8,16,64,256]{3,1,2,0:T(8,128)}, u32[]{:S(2)}, u32[]{:S(2)}) %all-to-all-start.2) | async-done | bytes 8388640 | tf_op jit(solution)/shard_map/all_to_all | solution.py:58
  385.1 4.4 %copy.23 = f32[8,16,64,256]{3,1,0,2:T(8,128)S(1)} copy(f32[8,16,64,256]{3,1,2,0:T(8,128)} %all-to-all-done.2) | data formatting | bytes 16777216 | tf_op jit(solution)/shard_map/all_to_all | solution.py:58
  389.5 2.9 fusion.22
  392.4 0.2 fusion.11
  392.6 1.0 convolution_convert_fusion
  (21 shorter events, 0.2 us)
Async XLA Ops:
  7.2 11.4 %copy-start = (bf16[8,64,256]{2,1,0:T(8,128)(2,1)S(1)}, bf16[8,64,256]{2,1,0:T(8,128)(2,1)}, u32[]{:S(2)}) copy-start(bf16[8,64,256]{2,1,0:T(8,128)(2,1)} %param.6) | copy-start | bytes 786436
  10.6 13.6 %all-to-all-start = ((s32[8,1,16]{2,1,0:T(1,128)}), s32[8,1,16]{2,1,0:T(1,128)S(1)}, u32[]{:S(2)}, u32[]{:S(2)}) async-start(s32[8,1,16]{2,1,0:T(1,128)} %bitcast.2), calls=%async_computation | async-start | bytes 8192 | tf_op jit(solution)/shard_map/all_to_all | solution.py:25
  31.7 96.6 %all-to-all-start.1 = ((bf16[8,16,64,256]{3,2,1,0:T(8,128)(2,1)}), bf16[8,16,64,256]{3,2,1,0:T(8,128)(2,1)}, u32[]{:S(2)}, u32[]{:S(2)}) async-start(bf16[8,16,64,256]{3,2,1,0:T(8,128)(2,1)} %broadcast_select_fusion), calls=%async_computation.1 | async-start | bytes 8388608 | tf_op jit(solution)/shard_map/all_to_all | solution.py:35
  36.2 2.9 copy-start.4
  36.2 109.1 %reduce-scatter.2.cloned.1.call-start = ((), (), s32[]{:S(2)}) async-start(), calls=%async_computation.4 | async-start | bytes 1572864 | tf_op jit(solution)/shard_map/reduce_scatter | solution.py:43
  133.2 12.1 %copy-start.3 = (bf16[8,64,256]{2,1,0:T(8,128)(2,1)S(1)}, bf16[8,64,256]{2,1,0:T(8,128)(2,1)}, u32[]{:S(2)}) copy-start(bf16[8,64,256]{2,1,0:T(8,128)(2,1)} %param.11) | copy-start | bytes 786436
  195.8 189.3 %all-to-all-start.2 = ((f32[8,16,64,256]{3,1,2,0:T(8,128)}), f32[8,16,64,256]{3,1,2,0:T(8,128)}, u32[]{:S(2)}, u32[]{:S(2)}) async-start(f32[8,16,64,256]{3,1,2,0:T(8,128)} %copy.22), calls=%async_computation.3 | async-start | bytes 16777216 | tf_op jit(solution)/shard_map/all_to_all | solution.py:58
  389.5 4.1 %copy-start.1 = (bf16[8,64,256]{2,1,0:T(8,128)(2,1)S(1)}, bf16[8,64,256]{2,1,0:T(8,128)(2,1)}, u32[]{:S(2)}) copy-start(bf16[8,64,256]{2,1,0:T(8,128)(2,1)} %param.6) | copy-start | bytes 786436
  389.5 3.1 copy-start.2
Sparse Core Ops, SparseCore 0:
  137.7 7.5 reduce-scatter.1
where the time goes:
time: 401 us; the launch traced here: 400 us
  waiting for transfers between devices  285 us (71%)
  local copies, waits for them, and re-layouts  57.4 us (14%)
  starting transfers between devices  17.4 us (4%)
  between operations  14.2 us (4%)
  matrix products  13.7 us (3%)
  other arithmetic  10.5 us (3%)
    all_to_all x1, waiting for transfers between devices, shards(): lax.all_to_all(outgoing, 'row', split_axis=0, concat_axis=0, tiled=True)  184 us
    all_to_all x1, waiting for transfers between devices, shards(): lax.all_to_all(replies, 'row', split_axis=0, concat_axis=0, tiled=True)  89.1 us
    scatter x1, local copies, waits for them, and re-layouts, shards(): outgoing.at[target_slot]  26.1 us
    reshape x1, local copies, waits for them, and re-layouts, shards(): outgoing = outgoing.reshape(peer_count, per_peer, half_rows, feat_width)  11.4 us
  transfers between devices with their start and end apart: 4, of which 4 were waited for; matrix products, arithmetic and copies ran while one was open for 1% of the time, Pallas kernels for 0%

commit v1 on v0

v1 whole, which is shorter than its diff:
```python
import functools

import jax
import jax.numpy as jnp
from jax import lax
from jax.experimental import pallas as pl
from jax.experimental.pallas import tpu as pltpu
from jax.sharding import PartitionSpec as P

F32 = jnp.float32
BF16 = jnp.bfloat16


def sparse_plan(feats, weight, degree, tile_cols, adjacency, cotangent):
    blocks, half_rows, feat_width = feats.shape
    slots_per = tile_cols.shape[1]
    tile_side = adjacency.shape[2]
    peer_count = lax.axis_size("row")
    tile_count = blocks * slots_per
    per_peer = (tile_count + peer_count - 1) // peer_count
    capacity = peer_count * per_peer
    columns = tile_cols.reshape(tile_count)
    is_live = columns >= 0
    owners = jnp.where(is_live, columns // blocks, -1)
    local_block = jnp.where(is_live, columns % blocks, -1)
    earlier = jnp.arange(tile_count)[:, None] > jnp.arange(tile_count)[None, :]
    same_owner = (owners[:, None] == owners[None, :]) & earlier & is_live[None, :]
    tile_rank = jnp.sum(same_owner.astype(jnp.int32), axis=1)
    target_slot = jnp.where(is_live, owners * per_peer + tile_rank, capacity)
    wanted = jnp.zeros((capacity,), jnp.int32).at[target_slot].set(local_block + 1, mode="drop")
    wanted = wanted.reshape(peer_count, per_peer)
    received = lax.all_to_all(wanted, "row", split_axis=0, concat_axis=0, tiled=True)
    incoming = received - 1
    scaling = lax.rsqrt(degree.astype(F32) + 1.0)[..., None]
    projected = jnp.dot(
        feats.reshape(blocks * half_rows, feat_width), weight, preferred_element_type=F32
    )
    sent_rows = (scaling * projected.reshape(blocks, half_rows, feat_width)).astype(BF16)
    tiles_bf = adjacency.astype(BF16).reshape(blocks, slots_per, half_rows, tile_side)
    pick_index = jnp.where(incoming < 0, blocks, incoming)
    replies = jnp.take(sent_rows, pick_index, axis=0, mode="fill", fill_value=0)
    fetched = lax.all_to_all(replies, "row", split_axis=0, concat_axis=0, tiled=True).reshape(
        capacity, half_rows, feat_width
    )
    tile_feats = jnp.take(fetched, target_slot, axis=0, mode="fill", fill_value=0)
    tile_feats = tile_feats.reshape(blocks, slots_per, half_rows, feat_width)
    gathered = lax.dot_general(
        tiles_bf, tile_feats, (((1, 2), (1, 2)), ((0,), (0,))), preferred_element_type=F32
    )
    own_rows = lax.psum_scatter(gathered, "col", scatter_dimension=1, tiled=True)
    mixed = scaling * (own_rows + sent_rows.astype(F32))
    sigmoid_z = jax.nn.sigmoid(mixed)
    output = (mixed * sigmoid_z).astype(BF16)
    silu_slope = sigmoid_z * (1.0 + mixed * (1.0 - sigmoid_z))
    back_sent = (scaling * cotangent.astype(F32) * silu_slope).astype(BF16)
    full_rows = lax.all_gather(back_sent, "col", axis=1, tiled=True)
    partials = lax.dot_general(
        tiles_bf, full_rows, (((3,), (1,)), ((0,), (0,))), preferred_element_type=F32
    )
    outgoing = jnp.zeros((capacity, half_rows, feat_width), F32)
    outgoing = outgoing.at[target_slot].set(
        partials.reshape(tile_count, half_rows, feat_width), mode="drop"
    )
    outgoing = outgoing.reshape(peer_count, per_peer, half_rows, feat_width)
    arrived = lax.all_to_all(outgoing, "row", split_axis=0, concat_axis=0, tiled=True).reshape(
        capacity, half_rows, feat_width
    )
    selector = (incoming.reshape(capacity)[:, None] == jnp.arange(blocks)[None, :]).astype(F32)
    returned = jnp.einsum("sl,sjf->ljf", selector, arrived, precision=lax.Precision.HIGHEST)
    combined = (scaling * (returned + back_sent.astype(F32))).astype(BF16)
    grad_rows = jnp.dot(
        combined.reshape(blocks * half_rows, feat_width), weight.T, preferred_element_type=F32
    )
    return (output, grad_rows.astype(BF16).reshape(blocks, half_rows, feat_width))


VM = pl.BlockSpec(memory_space=pltpu.VMEM)
SM = pl.BlockSpec(memory_space=pltpu.SMEM)


def call(body, outs, ins, args, flops, nbytes, name, **kw):
    return pl.pallas_call(
        body,
        out_shape=outs,
        in_specs=ins,
        out_specs=jax.tree.map(lambda _: VM, outs),
        cost_estimate=pl.CostEstimate(flops=flops, bytes_accessed=nbytes, transcendentals=0),
        compiler_params=pltpu.CompilerParams(vmem_limit_bytes=24 * 2**20),
        name=name,
        **kw,
    )(*args)


def dense_plan(feats, weight, degree, tile_cols, adjacency, cotangent):
    blocks, half, width = feats.shape
    slots = tile_cols.shape[1]
    side = adjacency.shape[2]
    n = lax.axis_size("row")
    rows = blocks * half
    hrows = rows // 2
    span = blocks * side
    far = n // 2
    ring = [2 * p if p < far else 2 * (n - 1 - p) + 1 for p in range(n)]
    fwd = [(ring[p], ring[(p + 1) % n]) for p in range(n)]
    bwd = [(b, a) for a, b in fwd]
    me = lax.axis_index("row")
    z = me // 2
    pos = jnp.where(me % 2 == 0, z, n - 1 - z)
    where_ref = jnp.stack([pos, lax.axis_index("col")]).astype(jnp.int32)

    def owner(where, d):
        p = lax.rem(where[0] + (d + n), n)
        return jnp.where(p < far, 2 * p, 2 * (n - 1 - p) + 1)

    def vout(shape, dtype):
        return jax.ShapeDtypeStruct(shape, dtype)

    def project(deg, x, w, s0, s1, sc):
        proj = jnp.dot(x[...], w[...], preferred_element_type=F32)
        scale = lax.rsqrt(deg[...].astype(F32) + 1.0)
        eye = lax.broadcasted_iota(jnp.int32, (half, half), 0) == lax.broadcasted_iota(
            jnp.int32, (half, half), 1
        )
        for b in range(blocks):
            line = jnp.broadcast_to(scale[b : b + 1, :], (half, half))
            col = jnp.sum(jnp.where(eye, line, 0.0), axis=1, keepdims=True)
            sc[b * half : (b + 1) * half, :] = jnp.broadcast_to(col, (half, 128))
            out = (col * proj[b * half : (b + 1) * half, :]).astype(BF16)
            if b < blocks // 2:
                s0[b * half : (b + 1) * half, :] = out
            else:
                s1[b * half - hrows : (b + 1) * half - hrows, :] = out

    s0, s1, scale = call(
        project,
        (vout((hrows, width), BF16), vout((hrows, width), BF16), vout((rows, 128), F32)),
        [VM] * 3,
        (degree, feats.reshape(rows, width), weight),
        2 * rows * width * width,
        2 * rows * width * 2,
        "project",
    )

    def densify(cols, adj, dense):
        b = pl.program_id(0)
        at = pl.multiple_of(b * side, side)
        dense[:, pl.ds(at, side)] = jnp.zeros((n * rows, side), BF16)

        def add(k, _):
            c = cols[b, k]

            @pl.when(c >= 0)
            def _():
                place = (pl.ds(pl.multiple_of(c * half, half), half), pl.ds(at, side))
                dense[place] = dense[place] + adj[k].astype(F32).astype(BF16)

            return 0

        lax.fori_loop(0, slots, add, 0)

    dense = pl.pallas_call(
        densify,
        out_shape=pltpu.VMEM((n * rows, span), BF16),
        grid=(blocks,),
        in_specs=[SM, pl.BlockSpec((slots, half, side), lambda b: (b, 0, 0))],
        out_specs=VM,
        cost_estimate=pl.CostEstimate(
            flops=0, bytes_accessed=adjacency.size * 4 + 2 * n * rows * span, transcendentals=0
        ),
        compiler_params=pltpu.CompilerParams(
            vmem_limit_bytes=24 * 2**20, dimension_semantics=("arbitrary",)
        ),
        name="densify",
    )(tile_cols, adjacency)

    def shift(x, perm):
        return lax.ppermute(x, "row", perm)

    f0, f1, b0, b1 = [s0], [s1], [s0], [s1]
    for step in range(far):
        f0.append(shift(f0[-1], fwd))
        b1.append(shift(b1[-1], bwd))
        if step < far - 1:
            f1.append(shift(f1[-1], fwd))
            b0.append(shift(b0[-1], bwd))

    def accumulate(where, dense, items, total):
        for d, h, ref in items:
            at = pl.multiple_of(owner(where, d) * rows + h * hrows, hrows)
            term = lax.dot_general(
                ref[...], dense[pl.ds(at, hrows), :], (((0,), (0,)), ((), ())),
                preferred_element_type=F32,
            )
            total = term if total is None else total + term
        return total

    early = [(0, 0, s0), (0, 1, s1)]
    for d in range(1, far):
        early += [(-d, 0, f0[d]), (d, 1, b1[d])]
        if d < far - 1:
            early += [(-d, 1, f1[d]), (d, 0, b0[d])]
    late = [(-(far - 1), 1, f1[far - 1]), (far - 1, 0, b0[far - 1])]
    late += [(-far, 0, f0[far]), (far, 1, b1[far])]

    def gather_early(where, dense, *refs):
        total = refs[-1]
        first = True
        for (d, h, _), ref in zip(early, refs[:-1]):
            term = accumulate(where, dense, [(d, h, ref)], None)
            total[...] = term if first else total[...] + term
            first = False

    def flops_of(items):
        return 2 * hrows * span * width * items

    part = call(
        gather_early,
        vout((width, span), F32),
        [SM] + [VM] * (1 + len(early)),
        (where_ref, dense, *[e[2] for e in early]),
        flops_of(len(early)),
        len(early) * hrows * span * 2,
        "gather_early",
    )

    def gather_late(where, dense, part, *refs):
        keep, give, whole = refs[-3:]
        total = accumulate(where, dense, [(d, h, r) for (d, h, _), r in zip(late, refs)], part[...])
        whole[...] = total.T.reshape(blocks, 2, half, width)
        keep[...] = whole[:, where[1]]
        give[...] = whole[:, 1 - where[1]]

    keep, give = call(
        gather_late,
        (vout((blocks, half, width), F32), vout((blocks, half, width), F32)),
        [SM] + [VM] * (2 + len(late)),
        (where_ref, dense, part, *[e[2] for e in late]),
        flops_of(len(late)),
        len(late) * hrows * span * 2,
        "gather_late",
        scratch_shapes=[pltpu.VMEM((blocks, 2, half, width), F32)],
    )
    other = [(0, 1), (1, 0)]
    got = lax.ppermute(give, "col", other)

    def mix(keep, got, s0, s1, sc, cot, out, back):
        for b in range(blocks):
            own = s0 if b < blocks // 2 else s1
            at = (b * half) % hrows
            s = jnp.tile(sc[b * half : (b + 1) * half, :], (1, width // 128))
            sent = own[at : at + half, :].astype(F32)
            mixed = s * (keep[b] + got[b] + sent)
            sig = jax.nn.sigmoid(mixed)
            out[b] = (mixed * sig).astype(BF16)
            slope = sig * (1.0 + mixed * (1.0 - sig))
            back[b] = (s * cot[b].astype(F32) * slope).astype(BF16)

    output, back = call(
        mix,
        (vout((blocks, half, width), BF16), vout((blocks, half, width), BF16)),
        [VM] * 6,
        (keep, got, s0, s1, scale, cotangent),
        rows * width * 20,
        rows * width * 16,
        "mix",
    )
    peer_back = lax.ppermute(back, "col", other)

    def chunk(where, dense, full, d):
        at = pl.multiple_of(owner(where, d) * rows, rows)
        return jnp.dot(dense[pl.ds(at, rows), :], full, preferred_element_type=F32)

    def return_far(where, dense, back, peer, full, c0, c1):
        q = where[1]
        full[:, q] = back[...]
        full[:, 1 - q] = peer[...]
        out = chunk(where, dense, full[...].reshape(span, width), far).astype(BF16)
        c0[...] = out[:hrows]
        c1[...] = out[hrows:]

    full, far0, far1 = call(
        return_far,
        (
            vout((blocks, 2, half, width), BF16),
            vout((hrows, width), BF16),
            vout((hrows, width), BF16),
        ),
        [SM] + [VM] * 3,
        (where_ref, dense, back, peer_back),
        flops_of(2),
        2 * hrows * span * 2,
        "return_far",
    )
    full = full.reshape(span, width)

    def return_next(where, dense, full, up0, up1, down0, down1):
        up = chunk(where, dense, full[...], far - 1)
        up0[...] = up[:hrows]
        up1[...] = up[hrows:].astype(BF16)
        down = chunk(where, dense, full[...], 1 - far)
        down0[...] = down[:hrows].astype(BF16)
        down1[...] = down[hrows:]

    hshape = (hrows, width)
    up0, up1, down0, down1 = call(
        return_next,
        (vout(hshape, F32), vout(hshape, BF16), vout(hshape, BF16), vout(hshape, F32)),
        [SM] + [VM] * 2,
        (where_ref, dense, full),
        flops_of(4),
        4 * hrows * span * 2,
        "return_next",
    )
    near = [d for d in range(2 - far, far - 1)]

    def return_near(where, dense, full, *outs):
        for d, out in zip(near, outs):
            out[...] = chunk(where, dense, full[...], d)

    chunks = call(
        return_near,
        tuple(vout((rows, width), F32) for _ in near),
        [SM] + [VM] * 2,
        (where_ref, dense, full),
        flops_of(2 * len(near)),
        2 * len(near) * hrows * span * 2,
        "return_near",
    )
    chunks = dict(zip(near, chunks))

    g0, r1 = far0, far1
    g1, r0 = up1, down0
    for step in range(far):
        g0 = shift(g0, fwd)
        r1 = shift(r1, bwd)
        if step < far - 1:
            g1 = shift(g1, fwd)
            r0 = shift(r0, bwd)
        d = far - 1 - step
        if d > 0:
            add0 = up0 if step == 0 else chunks[d][:hrows]
            add1 = down1 if step == 0 else chunks[-d][hrows:]
            g0 = (g0.astype(F32) + add0).astype(BF16)
            r1 = (r1.astype(F32) + add1).astype(BF16)
        if 0 < d - 1:
            g1 = (g1.astype(F32) + chunks[d - 1][hrows:]).astype(BF16)
            r0 = (r0.astype(F32) + chunks[1 - d][:hrows]).astype(BF16)

    def finish(own, g0, g1, r0, r1, back, sc, w, out):
        for h, (g, r) in enumerate(((g0, r0), (g1, r1))):
            at = slice(h * hrows, (h + 1) * hrows)
            total = own[at, :] + g[...].astype(F32) + r[...].astype(F32)
            s = jnp.tile(sc[at, :], (1, width // 128))
            comb = (s * (total + back[at, :].astype(F32))).astype(BF16)
            out[at, :] = lax.dot_general(
                comb, w[...], (((1,), (1,)), ((), ())), preferred_element_type=F32
            ).astype(BF16)

    grad = call(
        finish,
        vout((rows, width), BF16),
        [VM] * 8,
        (chunks[0], g0, g1, r0, r1, back.reshape(rows, width), scale, weight),
        2 * rows * width * width,
        rows * width * 8,
        "finish",
    )
    return output, grad.reshape(blocks, half, width)


def shards(feats, weight, degree, tile_cols, adjacency, cotangent):
    n = lax.axis_size("row")
    blocks, half, width = feats.shape
    dense = (
        n * blocks <= blocks * tile_cols.shape[1]
        and n % 2 == 0
        and n >= 6
        and blocks % 2 == 0
        and half % 16 == 0
        and width % 128 == 0
        and adjacency.shape[2] == 2 * half
        and lax.axis_size("col") == 2
    )
    plan = dense_plan if dense else sparse_plan
    return plan(feats, weight, degree, tile_cols, adjacency, cotangent)


def solution(mesh):
    in_specs = (
        P(("grp", "row"), "col", None),
        P(),
        P(("grp", "row"), "col"),
        P(("grp", "row"), None),
        P(("grp", "row"), "col", None),
        P(("grp", "row"), "col", None),
    )
    out_specs = (P(("grp", "row"), "col", None), P(("grp", "row"), "col", None))
    return jax.shard_map(shards, mesh=mesh, in_specs=in_specs, out_specs=out_specs, check_vma=False)
```

time: 401 us -> 72.7 us (0.18)
  waiting for transfers between devices: 285 us -> 20.7 us
  local copies, waits for them, and re-layouts: 57.4 us -> 5.42 us
  Pallas kernels: 0 us -> 15.2 us
  matrix products: 13.7 us -> 0 us
  between operations: 14.2 us -> 0.76 us
  starting transfers between devices: 17.4 us -> 29.9 us
  other arithmetic: 10.5 us -> 0.42 us
    all_to_all x3 -> x0, waiting for transfers between devices: 277 us -> none  [the longest x1 184 us: shards(): lax.all_to_all(outgoing, 'row', split_axis=0, concat_axis=0, tiled=True)]
    ppermute x0 -> x30, starting transfers between devices: none -> 29.9 us  [the longest x28 29.7 us: shift(): return lax.ppermute(x, 'row', perm)]
    scatter x2 -> x0, local copies, waits for them, and re-layouts: 27.1 us -> none  [the longest x1 26.1 us: shards(): outgoing.at[target_slot]]
    ppermute x0 -> x30, waiting for transfers between devices: none -> 20.7 us  [the longest x28 17.4 us: shift(): return lax.ppermute(x, 'row', perm)]
    all_to_all x3 -> x0, starting transfers between devices: 17.4 us -> none  [the longest x1 7.25 us: shards(): lax.all_to_all(wanted, 'row', split_axis=0, concat_axis=0, tiled=True)]
    pallas_call x0 -> x9, Pallas kernels: none -> 15.2 us  [the longest x8 10.3 us: call(): pl.pallas_call(body, out_shape=outs, in_specs=ins, out_specs=jax.tree.map...]
    dot_general x5 -> x0, matrix products: 13.7 us -> none  [the longest x1 4.46 us: shards(): lax.dot_general(tiles_bf, full_rows, (((3,), (1,)), ((0,), (0,))), prefer...]
    reshape x3 -> x0, local copies, waits for them, and re-layouts: 13 us -> none  [the longest x1 11.4 us: shards(): outgoing = outgoing.reshape(peer_count, per_peer, half_rows, feat_width)]
  transfers between devices with their start and end apart: 4 -> 30, of which waited for: 4 -> 18; matrix products, arithmetic and copies ran while one was open for 1% -> 1% of each run, Pallas kernels for 0% -> 15%
where the time goes in v1:
time: 72.7 us; the launch traced here: 72.4 us
  starting transfers between devices  29.9 us (41%)
  waiting for transfers between devices  20.7 us (28%)
  Pallas kernels  15.2 us (21%)
  local copies, waits for them, and re-layouts  5.42 us (7%)
  between operations  0.76 us (1%)
    ppermute x28, starting transfers between devices, shift(): return lax.ppermute(x, 'row', perm)  29.7 us
    ppermute x28, waiting for transfers between devices, shift(): return lax.ppermute(x, 'row', perm)  17.4 us
    pallas_call x8, Pallas kernels, call(): pl.pallas_call(body, out_shape=outs, in_specs=ins, out_specs=jax.tree.map...  10.3 us
    unnamed x14, local copies, waits for them, and re-layouts  5.42 us
    pallas_call x1, Pallas kernels, dense_plan(): pl.pallas_call(densify, out_shape=pltpu.VMEM((n * rows, span), BF16), gri...  4.9 us
    ppermute x1, waiting for transfers between devices, dense_plan(): got = lax.ppermute(give, 'col', other)  1.9 us
  transfers between devices with their start and end apart: 30, of which 18 were waited for; matrix products, arithmetic and copies ran while one was open for 1% of the time, Pallas kernels for 15%

profile of v1, /device:TPU:0, one launch (start us, length us, event | category | flops | bytes accessed | tf_op | source)
XLA Modules:
  0.0 72.4 jit_solution(12876947316709865922)
XLA Ops:
  3.4 3.1 %collective-permute-start = (bf16[256,256]{1,0:T(8,128)(2,1)S(1)}, bf16[256,256]{1,0:T(8,128)(2,1)S(1)}, u32[]{:S(2)}, u32[]{:S(2)}) collective-permute-start(bf16[256,256]{1,0:T(8,128)(2,1)S(1)} %get-tuple-element.21.refs_0_.s0), channel_id=1, source_target_pairs={{0,4},{4,8},{8,12},{12,14},{14,10},{10,6},{6,2},{2,0},{1,5},{5,9},... | collective-permute-start | bytes 393224 | tf_op jit(solution)/shard_map/ppermute | solution.py:177
  6.5 2.0 %collective-permute-start.2 = (bf16[256,256]{1,0:T(8,128)(2,1)S(1)}, bf16[256,256]{1,0:T(8,128)(2,1)S(1)}, u32[]{:S(2)}, u32[]{:S(2)}) collective-permute-start(bf16[256,256]{1,0:T(8,128)(2,1)S(1)} %get-tuple-element.22.refs_1_.s1), channel_id=1, source_target_pairs={{0,4},{4,8},{8,12},{12,14},{14,10},{10,6},{6,2},{2,0},{1,5},{5,9},... | collective-permute-start | bytes 393224 | tf_op jit(solution)/shard_map/ppermute | solution.py:177
  8.5 2.2 %collective-permute-done.refs_2_ = bf16[256,256]{1,0:T(8,128)(2,1)S(1)} collective-permute-done((bf16[256,256]{1,0:T(8,128)(2,1)S(1)}, bf16[256,256]{1,0:T(8,128)(2,1)S(1)}, u32[]{:S(2)}, u32[]{:S(2)}) %collective-permute-start) | collective-permute-done | bytes 131104 | tf_op jit(solution)/shard_map/ppermute | solution.py:177
  10.7 2.1 %collective-permute-start.4 = (bf16[256,256]{1,0:T(8,128)(2,1)S(1)}, bf16[256,256]{1,0:T(8,128)(2,1)S(1)}, u32[]{:S(2)}, u32[]{:S(2)}) collective-permute-start(bf16[256,256]{1,0:T(8,128)(2,1)S(1)} %collective-permute-done.refs_2_), channel_id=1, source_target_pairs={{0,4},{4,8},{8,12},{12,14},{14,10},{10,6},{6,2},{2,0},{1,5},{5,9},... | collective-permute-start | bytes 393224 | tf_op jit(solution)/shard_map/ppermute | solution.py:177
  13.5 2.2 %collective-permute-start.6 = (bf16[256,256]{1,0:T(8,128)(2,1)S(1)}, bf16[256,256]{1,0:T(8,128)(2,1)S(1)}, u32[]{:S(2)}, u32[]{:S(2)}) collective-permute-start(bf16[256,256]{1,0:T(8,128)(2,1)S(1)} %collective-permute-done.2.refs_4_), channel_id=1, source_target_pairs={{0,4},{4,8},{8,12},{12,14},{14,10},{10,6},{6,2},{2,0},{1,5},{5,9},... | collective-permute-start | bytes 393224 | tf_op jit(solution)/shard_map/ppermute | solution.py:177
  15.7 1.2 %collective-permute-done.4.refs_6_ = bf16[256,256]{1,0:T(8,128)(2,1)S(1)} collective-permute-done((bf16[256,256]{1,0:T(8,128)(2,1)S(1)}, bf16[256,256]{1,0:T(8,128)(2,1)S(1)}, u32[]{:S(2)}, u32[]{:S(2)}) %collective-permute-start.4) | collective-permute-done | bytes 131104 | tf_op jit(solution)/shard_map/ppermute | solution.py:177
  16.9 2.2 %collective-permute-start.8 = (bf16[256,256]{1,0:T(8,128)(2,1)S(1)}, bf16[256,256]{1,0:T(8,128)(2,1)S(1)}, u32[]{:S(2)}, u32[]{:S(2)}) collective-permute-start(bf16[256,256]{1,0:T(8,128)(2,1)S(1)} %collective-permute-done.4.refs_6_), channel_id=1, source_target_pairs={{0,4},{4,8},{8,12},{12,14},{14,10},{10,6},{6,2},{2,0},{1,5},{5,9},... | collective-permute-start | bytes 393224 | tf_op jit(solution)/shard_map/ppermute | solution.py:177
  19.3 2.2 %copy-done = s32[128,64,128]{2,1,0:T(8,128)S(1)} copy-done((s32[128,64,128]{2,1,0:T(8,128)S(1)}, s32[128,64,128]{2,1,0:T(8,128)}, u32[]{:S(2)}) %copy-start) | copy-done | bytes 4194328
  22.1 4.9 %densify.1.dense = bf16[4096,1024]{1,0:T(8,128)(2,1)S(1)} custom-call(s32[8,16]{1,0:T(8,128)S(1)} %copy-done.6, s32[128,64,128]{2,1,0:T(8,128)S(1)} %copy-done), custom_call_target="tpu_custom_call" | custom-call | bytes 12582912 | tf_op jit(solution)/shard_map/densify/pallas_call | solution.py:161
  27.1 1.9 %collective-permute-start.10 = (bf16[256,256]{1,0:T(8,128)(2,1)S(1)}, bf16[256,256]{1,0:T(8,128)(2,1)S(1)}, u32[]{:S(2)}, u32[]{:S(2)}) collective-permute-start(bf16[256,256]{1,0:T(8,128)(2,1)S(1)} %collective-permute-done.6.refs_8_), channel_id=1, source_target_pairs={{0,4},{4,8},{8,12},{12,14},{14,10},{10,6},{6,2},{2,0},{1,5},{5,9},... | collective-permute-start | bytes 393224 | tf_op jit(solution)/shard_map/ppermute | solution.py:177
  29.5 1.5 %collective-permute-start.12 = (bf16[256,256]{1,0:T(8,128)(2,1)S(1)}, bf16[256,256]{1,0:T(8,128)(2,1)S(1)}, u32[]{:S(2)}, u32[]{:S(2)}) collective-permute-start(bf16[256,256]{1,0:T(8,128)(2,1)S(1)} %collective-permute-done.8.refs_10_), channel_id=1, source_target_pairs={{0,4},{4,8},{8,12},{12,14},{14,10},{10,6},{6,2},{2,0},{1,5},{5,9},... | collective-permute-start | bytes 393224 | tf_op jit(solution)/shard_map/ppermute | solution.py:177
  31.5 2.4 %gather_early.1.part = f32[256,1024]{1,0:T(8,128)S(1)} custom-call(s32[2]{0:T(128)S(1)} %pad_add_fusion.where, bf16[4096,1024]{1,0:T(8,128)(2,1)S(1)} %densify.1.dense, bf16[256,256]{1,0:T(8,128)(2,1)S(1)} %get-tuple-element.21.refs_0_.s0, bf16[256,256]{1,0:T(8,128)(2,1)S(1)} %get-tuple-element.22.refs_1_.s1, ...), custom_call_target="tpu_custom_call" | custom-call | flops 1610612736 | bytes 6291456 | tf_op jit(solution)/shard_map/gather_early/pallas_call | solution.py:82
  34.5 1.5 %collective-permute-done.13.refs_3_ = bf16[256,256]{1,0:T(8,128)(2,1)S(1)} collective-permute-done((bf16[256,256]{1,0:T(8,128)(2,1)S(1)}, bf16[256,256]{1,0:T(8,128)(2,1)S(1)}, u32[]{:S(2)}, u32[]{:S(2)}) %collective-permute-start.13) | collective-permute-done | bytes 131104 | tf_op jit(solution)/shard_map/ppermute | solution.py:177
  36.0 1.5 %gather_late.1 = (f32[8,64,256]{2,1,0:T(8,128)S(1)}, f32[8,64,256]{2,1,0:T(8,128)S(1)}) custom-call(s32[2]{0:T(128)S(1)} %pad_add_fusion.where, bf16[4096,1024]{1,0:T(8,128)(2,1)S(1)} %densify.1.dense, f32[256,1024]{1,0:T(8,128)S(1)} %gather_early.1.part, bf16[256,256]{1,0:T(8,128)(2,1)S(1)} %collective-permute-done.10.refs_0_, ...), custom_call_target="tpu_custom_call" | custom-call | flops 536870912 | bytes 2097152 | tf_op jit(solution)/shard_map/gather_late/pallas_call | solution.py:82
  37.6 1.9 %collective-permute-done.14.got = f32[8,64,256]{2,1,0:T(8,128)S(1)} collective-permute-done((f32[8,64,256]{2,1,0:T(8,128)S(1)}, f32[8,64,256]{2,1,0:T(8,128)S(1)}, u32[]{:S(2)}, u32[]{:S(2)}) %collective-permute-start.14) | collective-permute-done | bytes 524320 | tf_op jit(solution)/shard_map/ppermute | solution.py:244
  40.5 1.4 %collective-permute-done.15.peer = bf16[8,64,256]{2,1,0:T(8,128)(2,1)S(1)} collective-permute-done((bf16[8,64,256]{2,1,0:T(8,128)(2,1)S(1)}, bf16[8,64,256]{2,1,0:T(8,128)(2,1)S(1)}, u32[]{:S(2)}, u32[]{:S(2)}) %collective-permute-start.15) | collective-permute-done | bytes 262176 | tf_op jit(solution)/shard_map/ppermute | solution.py:267
  41.9 1.0 %return_far.1 = (bf16[8,2,64,256]{3,2,1,0:T(8,128)(2,1)S(1)}, bf16[256,256]{1,0:T(8,128)(2,1)S(1)}, bf16[256,256]{1,0:T(8,128)(2,1)S(1)}) custom-call(s32[2]{0:T(128)S(1)} %pad_add_fusion.where, bf16[4096,1024]{1,0:T(8,128)(2,1)S(1)} %densify.1.dense, bf16[8,64,256]{2,1,0:T(8,128)(2,1)S(1)} %get-tuple-element.27.back, ...), custom_call_target="tpu_custom_call" | custom-call | flops 268435456 | bytes 1048576 | tf_op jit(solution)/shard_map/return_far/pallas_call | solution.py:82
  43.5 1.2 %return_next.1 = (f32[256,256]{1,0:T(8,128)S(1)}, bf16[256,256]{1,0:T(8,128)(2,1)S(1)}, bf16[256,256]{1,0:T(8,128)(2,1)S(1)}, f32[256,256]{1,0:T(8,128)S(1)}) custom-call(s32[2]{0:T(128)S(1)} %pad_add_fusion.where, bf16[4096,1024]{1,0:T(8,128)(2,1)S(1)} %densify.1.dense, bf16[1024,256]{1,0:T(8,128)(2,1)S(1)} %bitcast.6), custom_call_target="tpu_custom_call" | custom-call | flops 536870912 | bytes 2097152 | tf_op jit(solution)/shard_map/return_next/pallas_call | solution.py:82
  44.7 2.0 %collective-permute-start.23 = (bf16[256,256]{1,0:T(8,128)(2,1)S(1)}, bf16[256,256]{1,0:T(8,128)(2,1)S(1)}, u32[]{:S(2)}, u32[]{:S(2)}) collective-permute-start(bf16[256,256]{1,0:T(8,128)(2,1)S(1)} %get-tuple-element.35), channel_id=1, source_target_pairs={{4,0},{8,4},{12,8},{14,12},{10,14},{6,10},{2,6},{0,2},{5,1},{9,5},... | collective-permute-start | bytes 393224 | tf_op jit(solution)/shard_map/ppermute | solution.py:177
  46.8 1.5 %collective-permute-start.20 = (bf16[256,256]{1,0:T(8,128)(2,1)S(1)}, bf16[256,256]{1,0:T(8,128)(2,1)S(1)}, u32[]{:S(2)}, u32[]{:S(2)}) collective-permute-start(bf16[256,256]{1,0:T(8,128)(2,1)S(1)} %get-tuple-element.34), channel_id=1, source_target_pairs={{0,4},{4,8},{8,12},{12,14},{14,10},{10,6},{6,2},{2,0},{1,5},{5,9},... | collective-permute-start | bytes 393224 | tf_op jit(solution)/shard_map/ppermute | solution.py:177
  48.3 2.1 %return_near.1 = (f32[512,256]{1,0:T(8,128)S(1)}, f32[512,256]{1,0:T(8,128)S(1)}, f32[512,256]{1,0:T(8,128)S(1)}, f32[512,256]{1,0:T(8,128)S(1)}, f32[512,256]{1,0:T(8,128)S(1)}) custom-call(s32[2]{0:T(128)S(1)} %pad_add_fusion.where, bf16[4096,1024]{1,0:T(8,128)(2,1)S(1)} %densify.1.dense, bf16[1024,256]{1,0:T(8,128)(2,1)S(1)} %bitcast.7), custom_call_target="tpu_custom_call" | custom-call | flops 1342177280 | bytes 5242880 | tf_op jit(solution)/shard_map/return_near/pallas_call | solution.py:82
  51.0 2.1 %collective-permute-done.16 = bf16[256,256]{1,0:T(8,128)(2,1)S(1)} collective-permute-done((bf16[256,256]{1,0:T(8,128)(2,1)S(1)}, bf16[256,256]{1,0:T(8,128)(2,1)S(1)}, u32[]{:S(2)}, u32[]{:S(2)}) %collective-permute-start.16) | collective-permute-done | bytes 131104 | tf_op jit(solution)/shard_map/ppermute | solution.py:177
  53.3 2.2 %collective-permute-done.27 = bf16[256,256]{1,0:T(8,128)(2,1)S(1)} collective-permute-done((bf16[256,256]{1,0:T(8,128)(2,1)S(1)}, bf16[256,256]{1,0:T(8,128)(2,1)S(1)}, u32[]{:S(2)}, u32[]{:S(2)}) %collective-permute-start.27) | collective-permute-done | bytes 131104 | tf_op jit(solution)/shard_map/ppermute | solution.py:177
  56.1 2.0 %collective-permute-start.28 = (bf16[256,256]{1,0:T(8,128)(2,1)S(1)}, bf16[256,256]{1,0:T(8,128)(2,1)S(1)}, u32[]{:S(2)}, u32[]{:S(2)}) collective-permute-start(bf16[256,256]{1,0:T(8,128)(2,1)S(1)} %get-tuple-element.42), channel_id=1, source_target_pairs={{4,0},{8,4},{12,8},{14,12},{10,14},{6,10},{2,6},{0,2},{5,1},{9,5},... | collective-permute-start | bytes 393224 | tf_op jit(solution)/shard_map/ppermute | solution.py:177
  58.4 1.5 %collective-permute-start.21 = (bf16[256,256]{1,0:T(8,128)(2,1)S(1)}, bf16[256,256]{1,0:T(8,128)(2,1)S(1)}, u32[]{:S(2)}, u32[]{:S(2)}) collective-permute-start(bf16[256,256]{1,0:T(8,128)(2,1)S(1)} %get-tuple-element.46), channel_id=1, source_target_pairs={{0,4},{4,8},{8,12},{12,14},{14,10},{10,6},{6,2},{2,0},{1,5},{5,9},... | collective-permute-start | bytes 393224 | tf_op jit(solution)/shard_map/ppermute | solution.py:177
  60.6 1.6 %collective-permute-done.28 = bf16[256,256]{1,0:T(8,128)(2,1)S(1)} collective-permute-done((bf16[256,256]{1,0:T(8,128)(2,1)S(1)}, bf16[256,256]{1,0:T(8,128)(2,1)S(1)}, u32[]{:S(2)}, u32[]{:S(2)}) %collective-permute-start.28) | collective-permute-done | bytes 131104 | tf_op jit(solution)/shard_map/ppermute | solution.py:177
  63.1 1.6 %collective-permute-start.29 = (bf16[256,256]{1,0:T(8,128)(2,1)S(1)}, bf16[256,256]{1,0:T(8,128)(2,1)S(1)}, u32[]{:S(2)}, u32[]{:S(2)}) collective-permute-start(bf16[256,256]{1,0:T(8,128)(2,1)S(1)} %get-tuple-element.40), channel_id=1, source_target_pairs={{4,0},{8,4},{12,8},{14,12},{10,14},{6,10},{2,6},{0,2},{5,1},{9,5},... | collective-permute-start | bytes 393224 | tf_op jit(solution)/shard_map/ppermute | solution.py:177
  65.3 1.7 %collective-permute-start.22 = (bf16[256,256]{1,0:T(8,128)(2,1)S(1)}, bf16[256,256]{1,0:T(8,128)(2,1)S(1)}, u32[]{:S(2)}, u32[]{:S(2)}) collective-permute-start(bf16[256,256]{1,0:T(8,128)(2,1)S(1)} %get-tuple-element.44), channel_id=1, source_target_pairs={{0,4},{4,8},{8,12},{12,14},{14,10},{10,6},{6,2},{2,0},{1,5},{5,9},... | collective-permute-start | bytes 393224 | tf_op jit(solution)/shard_map/ppermute | solution.py:177
  67.3 1.4 %collective-permute-done.29.r1 = bf16[256,256]{1,0:T(8,128)(2,1)S(1)} collective-permute-done((bf16[256,256]{1,0:T(8,128)(2,1)S(1)}, bf16[256,256]{1,0:T(8,128)(2,1)S(1)}, u32[]{:S(2)}, u32[]{:S(2)}) %collective-permute-start.29) | collective-permute-done | bytes 131104 | tf_op jit(solution)/shard_map/ppermute | solution.py:177
  68.7 1.3 %collective-permute-done.19.g0 = bf16[256,256]{1,0:T(8,128)(2,1)S(1)} collective-permute-done((bf16[256,256]{1,0:T(8,128)(2,1)S(1)}, bf16[256,256]{1,0:T(8,128)(2,1)S(1)}, u32[]{:S(2)}, u32[]{:S(2)}) %collective-permute-start.19) | collective-permute-done | bytes 131104 | tf_op jit(solution)/shard_map/ppermute | solution.py:177
  70.0 1.4 %collective-permute-done.22.g1 = bf16[256,256]{1,0:T(8,128)(2,1)S(1)} collective-permute-done((bf16[256,256]{1,0:T(8,128)(2,1)S(1)}, bf16[256,256]{1,0:T(8,128)(2,1)S(1)}, u32[]{:S(2)}, u32[]{:S(2)}) %collective-permute-start.22) | collective-permute-done | bytes 131104 | tf_op jit(solution)/shard_map/ppermute | solution.py:177
  71.4 1.0 %finish.1 = bf16[512,256]{1,0:T(8,128)(2,1)} custom-call(f32[512,256]{1,0:T(8,128)S(1)} %get-tuple-element.29.own, bf16[256,256]{1,0:T(8,128)(2,1)S(1)} %collective-permute-done.19.g0, bf16[256,256]{1,0:T(8,128)(2,1)S(1)} %collective-permute-done.22.g1, bf16[256,256]{1,0:T(8,128)(2,1)S(1)} %collective-permute-done.25.r0, ...), custom_call_target="tpu_custom_call" | custom-call | flops 67108864 | bytes 1048576 | tf_op jit(solution)/shard_map/finish/pallas_call | solution.py:82
  (58 shorter events, 11.8 us)
Async XLA Ops:
  3.4 7.3 %collective-permute-start = (bf16[256,256]{1,0:T(8,128)(2,1)S(1)}, bf16[256,256]{1,0:T(8,128)(2,1)S(1)}, u32[]{:S(2)}, u32[]{:S(2)}) collective-permute-start(bf16[256,256]{1,0:T(8,128)(2,1)S(1)} %get-tuple-element.21.refs_0_.s0), channel_id=1, source_target_pairs={{0,4},{4,8},{8,12},{12,14},{14,10},{10,6},{6,2},{2,0},{1,5},{5,9},... | collective-permute-start | bytes 393224 | tf_op jit(solution)/shard_map/ppermute | solution.py:177
  6.5 6.4 %collective-permute-start.1 = (bf16[256,256]{1,0:T(8,128)(2,1)S(1)}, bf16[256,256]{1,0:T(8,128)(2,1)S(1)}, u32[]{:S(2)}, u32[]{:S(2)}) collective-permute-start(bf16[256,256]{1,0:T(8,128)(2,1)S(1)} %get-tuple-element.22.refs_1_.s1), channel_id=1, source_target_pairs={{4,0},{8,4},{12,8},{14,12},{10,14},{6,10},{2,6},{0,2},{5,1},{9,5},... | collective-permute-start | bytes 393224 | tf_op jit(solution)/shard_map/ppermute | solution.py:177
  6.5 7.0 %collective-permute-start.2 = (bf16[256,256]{1,0:T(8,128)(2,1)S(1)}, bf16[256,256]{1,0:T(8,128)(2,1)S(1)}, u32[]{:S(2)}, u32[]{:S(2)}) collective-permute-start(bf16[256,256]{1,0:T(8,128)(2,1)S(1)} %get-tuple-element.22.refs_1_.s1), channel_id=1, source_target_pairs={{0,4},{4,8},{8,12},{12,14},{14,10},{10,6},{6,2},{2,0},{1,5},{5,9},... | collective-permute-start | bytes 393224 | tf_op jit(solution)/shard_map/ppermute | solution.py:177
  8.5 7.2 %collective-permute-start.3 = (bf16[256,256]{1,0:T(8,128)(2,1)S(1)}, bf16[256,256]{1,0:T(8,128)(2,1)S(1)}, u32[]{:S(2)}, u32[]{:S(2)}) collective-permute-start(bf16[256,256]{1,0:T(8,128)(2,1)S(1)} %get-tuple-element.21.refs_0_.s0), channel_id=1, source_target_pairs={{4,0},{8,4},{12,8},{14,12},{10,14},{6,10},{2,6},{0,2},{5,1},{9,5},... | collective-permute-start | bytes 393224 | tf_op jit(solution)/shard_map/ppermute | solution.py:177
  10.7 6.2 %collective-permute-start.4 = (bf16[256,256]{1,0:T(8,128)(2,1)S(1)}, bf16[256,256]{1,0:T(8,128)(2,1)S(1)}, u32[]{:S(2)}, u32[]{:S(2)}) collective-permute-start(bf16[256,256]{1,0:T(8,128)(2,1)S(1)} %collective-permute-done.refs_2_), channel_id=1, source_target_pairs={{0,4},{4,8},{8,12},{12,14},{14,10},{10,6},{6,2},{2,0},{1,5},{5,9},... | collective-permute-start | bytes 393224 | tf_op jit(solution)/shard_map/ppermute | solution.py:177
  12.9 6.2 %collective-permute-start.5 = (bf16[256,256]{1,0:T(8,128)(2,1)S(1)}, bf16[256,256]{1,0:T(8,128)(2,1)S(1)}, u32[]{:S(2)}, u32[]{:S(2)}) collective-permute-start(bf16[256,256]{1,0:T(8,128)(2,1)S(1)} %collective-permute-done.1.refs_3_), channel_id=1, source_target_pairs={{4,0},{8,4},{12,8},{14,12},{10,14},{6,10},{2,6},{0,2},{5,1},{9,5},... | collective-permute-start | bytes 393224 | tf_op jit(solution)/shard_map/ppermute | solution.py:177
  13.5 13.6 %collective-permute-start.6 = (bf16[256,256]{1,0:T(8,128)(2,1)S(1)}, bf16[256,256]{1,0:T(8,128)(2,1)S(1)}, u32[]{:S(2)}, u32[]{:S(2)}) collective-permute-start(bf16[256,256]{1,0:T(8,128)(2,1)S(1)} %collective-permute-done.2.refs_4_), channel_id=1, source_target_pairs={{0,4},{4,8},{8,12},{12,14},{14,10},{10,6},{6,2},{2,0},{1,5},{5,9},... | collective-permute-start | bytes 393224 | tf_op jit(solution)/shard_map/ppermute | solution.py:177
  15.7 13.3 %collective-permute-start.7 = (bf16[256,256]{1,0:T(8,128)(2,1)S(1)}, bf16[256,256]{1,0:T(8,128)(2,1)S(1)}, u32[]{:S(2)}, u32[]{:S(2)}) collective-permute-start(bf16[256,256]{1,0:T(8,128)(2,1)S(1)} %collective-permute-done.3.refs_5_), channel_id=1, source_target_pairs={{4,0},{8,4},{12,8},{14,12},{10,14},{6,10},{2,6},{0,2},{5,1},{9,5},... | collective-permute-start | bytes 393224 | tf_op jit(solution)/shard_map/ppermute | solution.py:177
  16.9 12.6 %collective-permute-start.8 = (bf16[256,256]{1,0:T(8,128)(2,1)S(1)}, bf16[256,256]{1,0:T(8,128)(2,1)S(1)}, u32[]{:S(2)}, u32[]{:S(2)}) collective-permute-start(bf16[256,256]{1,0:T(8,128)(2,1)S(1)} %collective-permute-done.4.refs_6_), channel_id=1, source_target_pairs={{0,4},{4,8},{8,12},{12,14},{14,10},{10,6},{6,2},{2,0},{1,5},{5,9},... | collective-permute-start | bytes 393224 | tf_op jit(solution)/shard_map/ppermute | solution.py:177
  19.1 11.9 %collective-permute-start.9 = (bf16[256,256]{1,0:T(8,128)(2,1)S(1)}, bf16[256,256]{1,0:T(8,128)(2,1)S(1)}, u32[]{:S(2)}, u32[]{:S(2)}) collective-permute-start(bf16[256,256]{1,0:T(8,128)(2,1)S(1)} %collective-permute-done.5.refs_7_), channel_id=1, source_target_pairs={{4,0},{8,4},{12,8},{14,12},{10,14},{6,10},{2,6},{0,2},{5,1},{9,5},... | collective-permute-start | bytes 393224 | tf_op jit(solution)/shard_map/ppermute | solution.py:177
  27.1 12.4 %copy-start.3 = (bf16[8,64,256]{2,1,0:T(8,128)(2,1)S(1)}, bf16[8,64,256]{2,1,0:T(8,128)(2,1)}, u32[]{:S(2)}) copy-start(bf16[8,64,256]{2,1,0:T(8,128)(2,1)} %cot.1) | copy-start | bytes 786436
  27.1 6.8 %collective-permute-start.10 = (bf16[256,256]{1,0:T(8,128)(2,1)S(1)}, bf16[256,256]{1,0:T(8,128)(2,1)S(1)}, u32[]{:S(2)}, u32[]{:S(2)}) collective-permute-start(bf16[256,256]{1,0:T(8,128)(2,1)S(1)} %collective-permute-done.6.refs_8_), channel_id=1, source_target_pairs={{0,4},{4,8},{8,12},{12,14},{14,10},{10,6},{6,2},{2,0},{1,5},{5,9},... | collective-permute-start | bytes 393224 | tf_op jit(solution)/shard_map/ppermute | solution.py:177
  29.0 5.0 %collective-permute-start.11 = (bf16[256,256]{1,0:T(8,128)(2,1)S(1)}, bf16[256,256]{1,0:T(8,128)(2,1)S(1)}, u32[]{:S(2)}, u32[]{:S(2)}) collective-permute-start(bf16[256,256]{1,0:T(8,128)(2,1)S(1)} %collective-permute-done.7.refs_9_), channel_id=1, source_target_pairs={{4,0},{8,4},{12,8},{14,12},{10,14},{6,10},{2,6},{0,2},{5,1},{9,5},... | collective-permute-start | bytes 393224 | tf_op jit(solution)/shard_map/ppermute | solution.py:177
  29.5 5.0 %collective-permute-start.12 = (bf16[256,256]{1,0:T(8,128)(2,1)S(1)}, bf16[256,256]{1,0:T(8,128)(2,1)S(1)}, u32[]{:S(2)}, u32[]{:S(2)}) collective-permute-start(bf16[256,256]{1,0:T(8,128)(2,1)S(1)} %collective-permute-done.8.refs_10_), channel_id=1, source_target_pairs={{0,4},{4,8},{8,12},{12,14},{14,10},{10,6},{6,2},{2,0},{1,5},{5,9},... | collective-permute-start | bytes 393224 | tf_op jit(solution)/shard_map/ppermute | solution.py:177
  31.0 5.0 %collective-permute-start.13 = (bf16[256,256]{1,0:T(8,128)(2,1)S(1)}, bf16[256,256]{1,0:T(8,128)(2,1)S(1)}, u32[]{:S(2)}, u32[]{:S(2)}) collective-permute-start(bf16[256,256]{1,0:T(8,128)(2,1)S(1)} %collective-permute-done.9.refs_11_), channel_id=1, source_target_pairs={{4,0},{8,4},{12,8},{14,12},{10,14},{6,10},{2,6},{0,2},{5,1},{9,5},... | collective-permute-start | bytes 393224 | tf_op jit(solution)/shard_map/ppermute | solution.py:177
  37.5 2.0 %collective-permute-start.14 = (f32[8,64,256]{2,1,0:T(8,128)S(1)}, f32[8,64,256]{2,1,0:T(8,128)S(1)}, u32[]{:S(2)}, u32[]{:S(2)}) collective-permute-start(f32[8,64,256]{2,1,0:T(8,128)S(1)} %get-tuple-element.24), channel_id=1, source_target_pairs={{0,1},{1,0},{2,3},{3,2},{4,5},{5,4},{6,7},{7,6},{8,9},{9,8},{10,11... | collective-permute-start | bytes 1572872 | tf_op jit(solution)/shard_map/ppermute | solution.py:244
  40.4 1.5 %collective-permute-start.15 = (bf16[8,64,256]{2,1,0:T(8,128)(2,1)S(1)}, bf16[8,64,256]{2,1,0:T(8,128)(2,1)S(1)}, u32[]{:S(2)}, u32[]{:S(2)}) collective-permute-start(bf16[8,64,256]{2,1,0:T(8,128)(2,1)S(1)} %get-tuple-element.27.back), channel_id=1, source_target_pairs={{0,1},{1,0},{2,3},{3,2},{4,5},{5,4},{6,7},{7,6},{8,9},{9,8},{10,11... | collective-permute-start | bytes 786440 | tf_op jit(solution)/shard_map/ppermute | solution.py:267
  42.9 7.5 %collective-permute-start.26 = (bf16[256,256]{1,0:T(8,128)(2,1)S(1)}, bf16[256,256]{1,0:T(8,128)(2,1)S(1)}, u32[]{:S(2)}, u32[]{:S(2)}) collective-permute-start(bf16[256,256]{1,0:T(8,128)(2,1)S(1)} %get-tuple-element.38), channel_id=1, source_target_pairs={{4,0},{8,4},{12,8},{14,12},{10,14},{6,10},{2,6},{0,2},{5,1},{9,5},... | collective-permute-start | bytes 393224 | tf_op jit(solution)/shard_map/ppermute | solution.py:177
  44.7 26.7 %copy-start.2 = (bf16[256,256]{1,0:T(8,128)(2,1)S(1)}, bf16[256,256]{1,0:T(8,128)(2,1)}, u32[]{:S(2)}) copy-start(bf16[256,256]{1,0:T(8,128)(2,1)} %w.3) | copy-start | bytes 393220
  44.7 8.6 %collective-permute-start.23 = (bf16[256,256]{1,0:T(8,128)(2,1)S(1)}, bf16[256,256]{1,0:T(8,128)(2,1)S(1)}, u32[]{:S(2)}, u32[]{:S(2)}) collective-permute-start(bf16[256,256]{1,0:T(8,128)(2,1)S(1)} %get-tuple-element.35), channel_id=1, source_target_pairs={{4,0},{8,4},{12,8},{14,12},{10,14},{6,10},{2,6},{0,2},{5,1},{9,5},... | collective-permute-start | bytes 393224 | tf_op jit(solution)/shard_map/ppermute | solution.py:177
  46.7 6.4 %collective-permute-start.16 = (bf16[256,256]{1,0:T(8,128)(2,1)S(1)}, bf16[256,256]{1,0:T(8,128)(2,1)S(1)}, u32[]{:S(2)}, u32[]{:S(2)}) collective-permute-start(bf16[256,256]{1,0:T(8,128)(2,1)S(1)} %get-tuple-element.30), channel_id=1, source_target_pairs={{0,4},{4,8},{8,12},{12,14},{14,10},{10,6},{6,2},{2,0},{1,5},{5,9},... | collective-permute-start | bytes 393224 | tf_op jit(solution)/shard_map/ppermute | solution.py:177
  46.8 11.2 %collective-permute-start.20 = (bf16[256,256]{1,0:T(8,128)(2,1)S(1)}, bf16[256,256]{1,0:T(8,128)(2,1)S(1)}, u32[]{:S(2)}, u32[]{:S(2)}) collective-permute-start(bf16[256,256]{1,0:T(8,128)(2,1)S(1)} %get-tuple-element.34), channel_id=1, source_target_pairs={{0,4},{4,8},{8,12},{12,14},{14,10},{10,6},{6,2},{2,0},{1,5},{5,9},... | collective-permute-start | bytes 393224 | tf_op jit(solution)/shard_map/ppermute | solution.py:177
  50.4 5.0 %collective-permute-start.27 = (bf16[256,256]{1,0:T(8,128)(2,1)S(1)}, bf16[256,256]{1,0:T(8,128)(2,1)S(1)}, u32[]{:S(2)}, u32[]{:S(2)}) collective-permute-start(bf16[256,256]{1,0:T(8,128)(2,1)S(1)} %add_convert_fusion.2), channel_id=1, source_target_pairs={{4,0},{8,4},{12,8},{14,12},{10,14},{6,10},{2,6},{0,2},{5,1},{9,5},... | collective-permute-start | bytes 393224 | tf_op jit(solution)/shard_map/ppermute | solution.py:177
  53.1 5.0 %collective-permute-start.17 = (bf16[256,256]{1,0:T(8,128)(2,1)S(1)}, bf16[256,256]{1,0:T(8,128)(2,1)S(1)}, u32[]{:S(2)}, u32[]{:S(2)}) collective-permute-start(bf16[256,256]{1,0:T(8,128)(2,1)S(1)} %add_convert_fusion.9), channel_id=1, source_target_pairs={{0,4},{4,8},{8,12},{12,14},{14,10},{10,6},{6,2},{2,0},{1,5},{5,9},... | collective-permute-start | bytes 393224 | tf_op jit(solution)/shard_map/ppermute | solution.py:177
  55.5 5.0 %collective-permute-start.24 = (bf16[256,256]{1,0:T(8,128)(2,1)S(1)}, bf16[256,256]{1,0:T(8,128)(2,1)S(1)}, u32[]{:S(2)}, u32[]{:S(2)}) collective-permute-start(bf16[256,256]{1,0:T(8,128)(2,1)S(1)} %get-tuple-element.43), channel_id=1, source_target_pairs={{4,0},{8,4},{12,8},{14,12},{10,14},{6,10},{2,6},{0,2},{5,1},{9,5},... | collective-permute-start | bytes 393224 | tf_op jit(solution)/shard_map/ppermute | solution.py:177
  56.1 6.1 %collective-permute-start.28 = (bf16[256,256]{1,0:T(8,128)(2,1)S(1)}, bf16[256,256]{1,0:T(8,128)(2,1)S(1)}, u32[]{:S(2)}, u32[]{:S(2)}) collective-permute-start(bf16[256,256]{1,0:T(8,128)(2,1)S(1)} %get-tuple-element.42), channel_id=1, source_target_pairs={{4,0},{8,4},{12,8},{14,12},{10,14},{6,10},{2,6},{0,2},{5,1},{9,5},... | collective-permute-start | bytes 393224 | tf_op jit(solution)/shard_map/ppermute | solution.py:177
  58.2 6.5 %collective-permute-start.18 = (bf16[256,256]{1,0:T(8,128)(2,1)S(1)}, bf16[256,256]{1,0:T(8,128)(2,1)S(1)}, u32[]{:S(2)}, u32[]{:S(2)}) collective-permute-start(bf16[256,256]{1,0:T(8,128)(2,1)S(1)} %get-tuple-element.47), channel_id=1, source_target_pairs={{0,4},{4,8},{8,12},{12,14},{14,10},{10,6},{6,2},{2,0},{1,5},{5,9},... | collective-permute-start | bytes 393224 | tf_op jit(solution)/shard_map/ppermute | solution.py:177
  58.4 6.5 %collective-permute-start.21 = (bf16[256,256]{1,0:T(8,128)(2,1)S(1)}, bf16[256,256]{1,0:T(8,128)(2,1)S(1)}, u32[]{:S(2)}, u32[]{:S(2)}) collective-permute-start(bf16[256,256]{1,0:T(8,128)(2,1)S(1)} %get-tuple-element.46), channel_id=1, source_target_pairs={{0,4},{4,8},{8,12},{12,14},{14,10},{10,6},{6,2},{2,0},{1,5},{5,9},... | collective-permute-start | bytes 393224 | tf_op jit(solution)/shard_map/ppermute | solution.py:177
  62.2 5.0 %collective-permute-start.25 = (bf16[256,256]{1,0:T(8,128)(2,1)S(1)}, bf16[256,256]{1,0:T(8,128)(2,1)S(1)}, u32[]{:S(2)}, u32[]{:S(2)}) collective-permute-start(bf16[256,256]{1,0:T(8,128)(2,1)S(1)} %get-tuple-element.41), channel_id=1, source_target_pairs={{4,0},{8,4},{12,8},{14,12},{10,14},{6,10},{2,6},{0,2},{5,1},{9,5},... | collective-permute-start | bytes 393224 | tf_op jit(solution)/shard_map/ppermute | solution.py:177
  63.1 5.5 %collective-permute-start.29 = (bf16[256,256]{1,0:T(8,128)(2,1)S(1)}, bf16[256,256]{1,0:T(8,128)(2,1)S(1)}, u32[]{:S(2)}, u32[]{:S(2)}) collective-permute-start(bf16[256,256]{1,0:T(8,128)(2,1)S(1)} %get-tuple-element.40), channel_id=1, source_target_pairs={{4,0},{8,4},{12,8},{14,12},{10,14},{6,10},{2,6},{0,2},{5,1},{9,5},... | collective-permute-start | bytes 393224 | tf_op jit(solution)/shard_map/ppermute | solution.py:177
  65.0 5.0 %collective-permute-start.19 = (bf16[256,256]{1,0:T(8,128)(2,1)S(1)}, bf16[256,256]{1,0:T(8,128)(2,1)S(1)}, u32[]{:S(2)}, u32[]{:S(2)}) collective-permute-start(bf16[256,256]{1,0:T(8,128)(2,1)S(1)} %get-tuple-element.45), channel_id=1, source_target_pairs={{0,4},{4,8},{8,12},{12,14},{14,10},{10,6},{6,2},{2,0},{1,5},{5,9},... | collective-permute-start | bytes 393224 | tf_op jit(solution)/shard_map/ppermute | solution.py:177
  65.3 6.1 %collective-permute-start.22 = (bf16[256,256]{1,0:T(8,128)(2,1)S(1)}, bf16[256,256]{1,0:T(8,128)(2,1)S(1)}, u32[]{:S(2)}, u32[]{:S(2)}) collective-permute-start(bf16[256,256]{1,0:T(8,128)(2,1)S(1)} %get-tuple-element.44), channel_id=1, source_target_pairs={{0,4},{4,8},{8,12},{12,14},{14,10},{10,6},{6,2},{2,0},{1,5},{5,9},... | collective-permute-start | bytes 393224 | tf_op jit(solution)/shard_map/ppermute | solution.py:177
  (5 other events, 5.4 us)

commit v2 on v0

v2 whole, which is shorter than its diff:
```python
import functools

import jax
import jax.numpy as jnp
from jax import lax
from jax.experimental import pallas as pl
from jax.experimental.pallas import tpu as pltpu
from jax.sharding import PartitionSpec as P

F32 = jnp.float32
BF16 = jnp.bfloat16


def sparse_plan(feats, weight, degree, tile_cols, adjacency, cotangent):
    blocks, half_rows, feat_width = feats.shape
    slots_per = tile_cols.shape[1]
    tile_side = adjacency.shape[2]
    peer_count = lax.axis_size("row")
    tile_count = blocks * slots_per
    per_peer = (tile_count + peer_count - 1) // peer_count
    capacity = peer_count * per_peer
    columns = tile_cols.reshape(tile_count)
    is_live = columns >= 0
    owners = jnp.where(is_live, columns // blocks, -1)
    local_block = jnp.where(is_live, columns % blocks, -1)
    earlier = jnp.arange(tile_count)[:, None] > jnp.arange(tile_count)[None, :]
    same_owner = (owners[:, None] == owners[None, :]) & earlier & is_live[None, :]
    tile_rank = jnp.sum(same_owner.astype(jnp.int32), axis=1)
    target_slot = jnp.where(is_live, owners * per_peer + tile_rank, capacity)
    wanted = jnp.zeros((capacity,), jnp.int32).at[target_slot].set(local_block + 1, mode="drop")
    wanted = wanted.reshape(peer_count, per_peer)
    received = lax.all_to_all(wanted, "row", split_axis=0, concat_axis=0, tiled=True)
    incoming = received - 1
    scaling = lax.rsqrt(degree.astype(F32) + 1.0)[..., None]
    projected = jnp.dot(
        feats.reshape(blocks * half_rows, feat_width), weight, preferred_element_type=F32
    )
    sent_rows = (scaling * projected.reshape(blocks, half_rows, feat_width)).astype(BF16)
    tiles_bf = adjacency.astype(BF16).reshape(blocks, slots_per, half_rows, tile_side)
    pick_index = jnp.where(incoming < 0, blocks, incoming)
    replies = jnp.take(sent_rows, pick_index, axis=0, mode="fill", fill_value=0)
    fetched = lax.all_to_all(replies, "row", split_axis=0, concat_axis=0, tiled=True).reshape(
        capacity, half_rows, feat_width
    )
    tile_feats = jnp.take(fetched, target_slot, axis=0, mode="fill", fill_value=0)
    tile_feats = tile_feats.reshape(blocks, slots_per, half_rows, feat_width)
    gathered = lax.dot_general(
        tiles_bf, tile_feats, (((1, 2), (1, 2)), ((0,), (0,))), preferred_element_type=F32
    )
    own_rows = lax.psum_scatter(gathered, "col", scatter_dimension=1, tiled=True)
    mixed = scaling * (own_rows + sent_rows.astype(F32))
    sigmoid_z = jax.nn.sigmoid(mixed)
    output = (mixed * sigmoid_z).astype(BF16)
    silu_slope = sigmoid_z * (1.0 + mixed * (1.0 - sigmoid_z))
    back_sent = (scaling * cotangent.astype(F32) * silu_slope).astype(BF16)
    full_rows = lax.all_gather(back_sent, "col", axis=1, tiled=True)
    partials = lax.dot_general(
        tiles_bf, full_rows, (((3,), (1,)), ((0,), (0,))), preferred_element_type=F32
    )
    outgoing = jnp.zeros((capacity, half_rows, feat_width), F32)
    outgoing = outgoing.at[target_slot].set(
        partials.reshape(tile_count, half_rows, feat_width), mode="drop"
    )
    outgoing = outgoing.reshape(peer_count, per_peer, half_rows, feat_width)
    arrived = lax.all_to_all(outgoing, "row", split_axis=0, concat_axis=0, tiled=True).reshape(
        capacity, half_rows, feat_width
    )
    selector = (incoming.reshape(capacity)[:, None] == jnp.arange(blocks)[None, :]).astype(F32)
    returned = jnp.einsum("sl,sjf->ljf", selector, arrived, precision=lax.Precision.HIGHEST)
    combined = (scaling * (returned + back_sent.astype(F32))).astype(BF16)
    grad_rows = jnp.dot(
        combined.reshape(blocks * half_rows, feat_width), weight.T, preferred_element_type=F32
    )
    return (output, grad_rows.astype(BF16).reshape(blocks, half_rows, feat_width))


VM = pl.BlockSpec(memory_space=pltpu.VMEM)
ANY = pl.BlockSpec(memory_space=pl.ANY)
OTHER = [(0, 1), (1, 0)]


def call(body, outs, ins, args, flops, nbytes, name, **kw):
    return pl.pallas_call(
        body,
        out_shape=outs,
        in_specs=ins,
        out_specs=jax.tree.map(lambda _: VM, outs),
        cost_estimate=pl.CostEstimate(flops=flops, bytes_accessed=nbytes, transcendentals=0),
        compiler_params=pltpu.CompilerParams(vmem_limit_bytes=24 * 2**20),
        name=name,
        **kw,
    )(*args)


def array(shape, dtype):
    return jax.ShapeDtypeStruct(shape, dtype)


def after(value, *tokens):
    return lax.optimization_barrier((value,) + tokens)[0]


def dense_plan(feats, weight, degree, tile_cols, adjacency, cotangent):
    blocks, half, width = feats.shape
    slots = tile_cols.shape[1]
    side = adjacency.shape[2]
    n = lax.axis_size("row")
    rows = blocks * half
    hrows = rows // 2
    span = blocks * side
    far = n // 2
    ring = [2 * p if p < far else 2 * (n - 1 - p) + 1 for p in range(n)]
    fwd = [(ring[p], ring[(p + 1) % n]) for p in range(n)]
    bwd = [(b, a) for a, b in fwd]

    def half_rows_of(d, h):
        me = lax.axis_index("row")
        z = lax.shift_right_logical(me, 1)
        place = jnp.where(lax.rem(me, 2) == 0, z, n - 1 - z)
        p = lax.rem(place + (d + n), n)
        owner = jnp.where(p < far, 2 * p, 2 * (n - 1 - p) + 1)
        return pl.ds(pl.multiple_of(owner * rows + h * hrows, hrows), hrows)

    def item_cost(items):
        return 2 * hrows * span * width * items, items * hrows * span * 2

    def project(deg_hbm, x_hbm, w_hbm, s0, s1, sc, deg, x, w, sems):
        copies = [
            pltpu.make_async_copy(src, dst, sems.at[i])
            for i, (src, dst) in enumerate(((deg_hbm, deg), (x_hbm, x), (w_hbm, w)))
        ]
        for c in copies:
            c.start()
        copies[0].wait()
        scale = lax.rsqrt(deg[...].astype(F32) + 1.0)
        eye = lax.broadcasted_iota(jnp.int32, (half, half), 0) == lax.broadcasted_iota(
            jnp.int32, (half, half), 1
        )
        for b in range(blocks):
            line = jnp.broadcast_to(scale[b : b + 1, :], (half, half))
            col = jnp.sum(jnp.where(eye, line, 0.0), axis=1, keepdims=True)
            sc[b * half : (b + 1) * half, :] = jnp.broadcast_to(col, (half, 128))
        copies[1].wait()
        copies[2].wait()
        proj = jnp.dot(x[...], w[...], preferred_element_type=F32)
        out = (jnp.tile(sc[...], (1, width // 128)) * proj).astype(BF16)
        s0[...] = out[:hrows]
        s1[...] = out[hrows:]

    hshape = (hrows, width)
    s0, s1, scale = call(
        project,
        (array(hshape, BF16), array(hshape, BF16), array((rows, 128), F32)),
        [ANY] * 3,
        tuple(
            pltpu.with_memory_space_constraint(a, pltpu.HBM)
            for a in (degree, feats.reshape(rows, width), weight)
        ),
        2 * rows * width * width,
        2 * rows * width * 2,
        "project",
        scratch_shapes=[
            pltpu.VMEM(degree.shape, jnp.int32),
            pltpu.VMEM((rows, width), BF16),
            pltpu.VMEM(weight.shape, BF16),
            pltpu.SemaphoreType.DMA((3,)),
        ],
    )

    def densify(cols_hbm, adj_hbm, dense, cols, adj, sems):
        def tiles_of(b):
            return pl.ds(b * slots, slots)

        cols_copy = pltpu.make_async_copy(cols_hbm, cols, sems.at[blocks])
        cols_copy.start()
        copies = [
            pltpu.make_async_copy(adj_hbm.at[tiles_of(b)], adj.at[tiles_of(b)], sems.at[b])
            for b in range(blocks)
        ]
        for c in copies:
            c.start()
        dense[...] = jnp.zeros(dense.shape, BF16)
        cols_copy.wait()
        for b in range(blocks):
            copies[b].wait()
            lanes = slice(b * side, (b + 1) * side)
            for k in range(slots):
                c = cols[b, k]
                tile = jnp.where(c >= 0, adj[b * slots + k], 0).astype(F32).astype(BF16)
                place = pl.ds(pl.multiple_of(jnp.maximum(c, 0) * half, half), half)
                dense[place, lanes] = dense[place, lanes] + tile

    def hbm(x):
        return pltpu.with_memory_space_constraint(x, pltpu.HBM)

    dense = pl.pallas_call(
        densify,
        out_shape=pltpu.VMEM((n * rows, span), BF16),
        in_specs=[ANY, ANY],
        out_specs=VM,
        scratch_shapes=[
            pltpu.SMEM(tile_cols.shape, jnp.int32),
            pltpu.VMEM(adjacency.shape, jnp.int32),
            pltpu.SemaphoreType.DMA((blocks + 1,)),
        ],
        cost_estimate=pl.CostEstimate(
            flops=0, bytes_accessed=adjacency.size * 4, transcendentals=0
        ),
        compiler_params=pltpu.CompilerParams(vmem_limit_bytes=24 * 2**20),
        name="densify",
    )(hbm(tile_cols), hbm(adjacency))

    def shift_pair(pair):
        return lax.ppermute(pair[0], "row", fwd), lax.ppermute(pair[1], "row", bwd)

    def gather_terms(dense, items):
        total = None
        for d, h, ref in items:
            term = lax.dot_general(
                ref[...], dense[half_rows_of(d, h), :], (((0,), (0,)), ((), ())),
                preferred_element_type=F32,
            )
            total = term if total is None else total + term
        return total

    def gather(items, part, name):
        def body(dense, *refs):
            total = gather_terms(dense, [(d, h, r) for (d, h, _), r in zip(items, refs)])
            refs[-1][...] = total if part is None else refs[-2][...] + total

        extra = () if part is None else (part,)
        return call(
            body,
            array((width, span), F32),
            [VM] * (1 + len(items) + len(extra)),
            (dense, *[i[2] for i in items], *extra),
            *item_cost(len(items)),
            name,
        )

    long, short = [(s0, s1)], [(s1, s0)]
    long.append(shift_pair(long[0]))
    short.append(shift_pair(short[0]))

    def pass_on(pair, token):
        first = after(pair[0], token)
        return first, after(pair[1], first)

    long[1] = pass_on(long[1], dense)
    long.append(shift_pair(long[1]))
    short[1] = pass_on(short[1], long[1][1])
    short.append(shift_pair(short[1]))

    def long_items(hop):
        return [(-hop, 0, long[hop][0]), (hop, 1, long[hop][1])]

    def short_items(hop):
        return [(-hop, 1, short[hop][0]), (hop, 0, short[hop][1])]

    part = gather([(0, 0, s0), (0, 1, s1)] + long_items(1), None, "gather_near")
    long[2] = pass_on(long[2], part)
    long.append(shift_pair(long[2]))
    part = gather(short_items(1) + long_items(2), part, "gather_two")
    short[2] = pass_on(short[2], part)
    short.append(shift_pair(short[2]))
    long[3] = pass_on(long[3], short[2][1])
    long.append(shift_pair(long[3]))
    part = gather(short_items(2) + long_items(3), part, "gather_three")

    def turn(dense, fa, ba, part, give, keep, tgive, tkeep, dgive, dkeep, whole, wide):
        q = lax.axis_index("col")
        total = part[...] + gather_terms(dense, [(-(far - 1), 1, fa), (far - 1, 0, ba)])
        whole[...] = total.T.reshape(blocks, 2, half, width)
        for h in range(2):
            block = dense[half_rows_of(far, h), :].T
            wide[:, :, :, h * hrows : (h + 1) * hrows] = block.reshape(blocks, 2, half, hrows)
        give[...] = whole[:, 1 - q].reshape(rows, width)
        keep[...] = whole[:, q].reshape(rows, width)
        tg = wide[:, 1 - q].reshape(rows, rows)
        tk = wide[:, q].reshape(rows, rows)
        tgive[...] = tg
        tkeep[...] = tk
        dgive[...] = tg.T
        dkeep[...] = tk.T

    shape = (rows, width)
    square = (rows, rows)
    part_give, part_keep, turn_give, turn_keep, far_give, far_keep = call(
        turn,
        (array(shape, F32), array(shape, F32)) + (array(square, BF16),) * 4,
        [VM] * 4,
        (dense, *short[3], part),
        *item_cost(3),
        "turn",
        scratch_shapes=[
            pltpu.VMEM((blocks, 2, half, width), F32),
            pltpu.VMEM((blocks, 2, half, rows), BF16),
        ],
    )

    def last(part, turned, fa, ba, out):
        total = part[...] + jnp.dot(turned[:, :hrows], fa[...], preferred_element_type=F32)
        total = total + jnp.dot(turned[:, hrows:], ba[...], preferred_element_type=F32)
        out[...] = total.astype(out.dtype)

    def gather_last(part, turned, dtype, name):
        return call(
            last, array(shape, dtype), [VM] * 4, (part, turned, *long[far]), *item_cost(1), name
        )

    give = gather_last(part_give, turn_give, BF16, "gather_give")
    got = lax.ppermute(give, "col", OTHER)
    keep = gather_last(part_keep, turn_keep, F32, "gather_keep")

    def mixed_of(keep, got, s0, s1, sc, h):
        at = slice(h * hrows, (h + 1) * hrows)
        s = jnp.tile(sc[at, :], (1, width // 128))
        sent = (s0, s1)[h][...].astype(F32)
        mixed = s * (keep[at, :] + got[at, :].astype(F32) + sent)
        return at, s, mixed, jax.nn.sigmoid(mixed)

    def mix_back(keep, got, s0, s1, sc, cot, back):
        for h in range(2):
            at, s, mixed, sig = mixed_of(keep, got, s0, s1, sc, h)
            slope = sig * (1.0 + mixed * (1.0 - sig))
            back[at, :] = (s * cot[at, :].astype(F32) * slope).astype(BF16)

    def mix_out(keep, got, s0, s1, sc, out):
        for h in range(2):
            at, _, mixed, sig = mixed_of(keep, got, s0, s1, sc, h)
            out[at, :] = (mixed * sig).astype(BF16)

    mix_in = (keep, got, s0, s1, scale)
    back = call(
        mix_back,
        array(shape, BF16),
        [VM] * 6,
        mix_in + (cotangent.reshape(shape),),
        rows * width * 20,
        rows * width * 16,
        "mix_back",
    )
    peer_back = lax.ppermute(back, "col", OTHER)
    output = call(
        mix_out, array(shape, BF16), [VM] * 5, mix_in, rows * width * 10, rows * width * 12, "mix_out"
    )

    def far_own(matrix, back, out):
        out[...] = jnp.dot(matrix[...], back[...], preferred_element_type=F32)

    far_part = call(
        far_own, array(shape, F32), [VM] * 2, (far_keep, back), *item_cost(1), "return_far_own"
    )

    def far_peer(matrix, back, part, c0, c1):
        out = part[...] + jnp.dot(matrix[...], back[...], preferred_element_type=F32)
        c0[...] = out[:hrows].astype(BF16)
        c1[...] = out[hrows:].astype(BF16)

    up = call(
        far_peer,
        (array(hshape, BF16), array(hshape, BF16)),
        [VM] * 3,
        (far_give, peer_back, far_part),
        *item_cost(1),
        "return_far",
    )
    up = shift_pair(up)

    def chunk(dense, full, d, h):
        return jnp.dot(dense[half_rows_of(d, h), :], full, preferred_element_type=F32)

    def return_next(dense, back, peer, full4, first, second):
        q = lax.axis_index("col")
        full4[:, q] = back[...].reshape(blocks, half, width)
        full4[:, 1 - q] = peer[...].reshape(blocks, half, width)
        full = full4[...].reshape(span, width)
        first[...] = chunk(dense, full, far - 1, 1).astype(BF16)
        second[...] = chunk(dense, full, 1 - far, 0).astype(BF16)

    full4, *down = call(
        return_next,
        (array((blocks, 2, half, width), BF16), array(hshape, BF16), array(hshape, BF16)),
        [VM] * 3,
        (dense, back, peer_back),
        *item_cost(2),
        "return_next",
    )
    full = full4.reshape(span, width)
    down = shift_pair(down)

    def chunks(which, full, name):
        def body(dense, full, *outs):
            for (d, h), out in zip(which, outs):
                out[...] = chunk(dense, full[...], d, h)

        return call(
            body,
            tuple(array(hshape, F32) for _ in which),
            [VM] * 2,
            (dense, full),
            *item_cost(len(which)),
            name,
        )

    def add_pair(pair, terms, token):
        first = (pair[0].astype(F32) + after(terms[0], token)).astype(BF16)
        second = (pair[1].astype(F32) + after(terms[1], first)).astype(BF16)
        return first, second

    a0, a1, c0, c1 = chunks([(3, 0), (-3, 1), (2, 1), (-2, 0)], full, "return_a")
    up = add_pair(up, (a0, a1), c0)
    full_b = after(full, up[1])
    up = shift_pair(up)
    d0, d1, e0, e1 = chunks([(2, 0), (-2, 1), (1, 1), (-1, 0)], full_b, "return_b")
    down = add_pair(down, (c0, c1), d0)
    full_c = after(full, down[1])
    down = shift_pair(down)
    f0, f1, own0, own1 = chunks([(1, 0), (-1, 1), (0, 0), (0, 1)], full_c, "return_c")
    up = add_pair(up, (d0, d1), f0)
    token = up[1]
    up = shift_pair(up)
    down = add_pair(down, (e0, e1), token)
    token = down[1]
    down = shift_pair(down)
    up = shift_pair(add_pair(up, (f0, f1), token))

    def finish(own0, own1, g0, r1, g1, r0, back, sc, w, out):
        for h, (own, g, r) in enumerate(((own0, g0, r0), (own1, g1, r1))):
            at = slice(h * hrows, (h + 1) * hrows)
            total = own[...] + g[...].astype(F32) + r[...].astype(F32)
            s = jnp.tile(sc[at, :], (1, width // 128))
            comb = (s * (total + back[at, :].astype(F32))).astype(BF16)
            out[at, :] = lax.dot_general(
                comb, w[...], (((1,), (1,)), ((), ())), preferred_element_type=F32
            ).astype(BF16)

    grad = call(
        finish,
        array(shape, BF16),
        [VM] * 9,
        (own0, own1, *up, *down, back, scale, weight),
        2 * rows * width * width,
        rows * width * 8,
        "finish",
    )
    return output.reshape(feats.shape), grad.reshape(feats.shape)


def shards(feats, weight, degree, tile_cols, adjacency, cotangent):
    n = lax.axis_size("row")
    blocks, half, width = feats.shape
    dense = (
        n * blocks <= blocks * tile_cols.shape[1]
        and n % 2 == 0
        and n == 8
        and blocks % 2 == 0
        and half % 16 == 0
        and width % 128 == 0
        and adjacency.shape[2] == 2 * half
        and lax.axis_size("col") == 2
    )
    plan = dense_plan if dense else sparse_plan
    return plan(feats, weight, degree, tile_cols, adjacency, cotangent)


def solution(mesh):
    in_specs = (
        P(("grp", "row"), "col", None),
        P(),
        P(("grp", "row"), "col"),
        P(("grp", "row"), None),
        P(("grp", "row"), "col", None),
        P(("grp", "row"), "col", None),
    )
    out_specs = (P(("grp", "row"), "col", None), P(("grp", "row"), "col", None))
    return jax.shard_map(shards, mesh=mesh, in_specs=in_specs, out_specs=out_specs, check_vma=False)
```

time: 401 us -> 61.7 us (0.15)
  waiting for transfers between devices: 285 us -> 16.9 us
  local copies, waits for them, and re-layouts: 57.4 us -> 0.01 us
  matrix products: 13.7 us -> 0 us
  between operations: 14.2 us -> 0.89 us
  Pallas kernels: 0 us -> 13.2 us
  starting transfers between devices: 17.4 us -> 30.3 us
  other arithmetic: 10.5 us -> 0.27 us
    all_to_all x3 -> x0, waiting for transfers between devices: 277 us -> none  [the longest x1 184 us: shards(): lax.all_to_all(outgoing, 'row', split_axis=0, concat_axis=0, tiled=True)]
    ppermute x0 -> x30, starting transfers between devices: none -> 30.3 us  [the longest x14 21.9 us: shift_pair(): lax.ppermute(pair[0], 'row', fwd)]
    scatter x2 -> x0, local copies, waits for them, and re-layouts: 27.1 us -> none  [the longest x1 26.1 us: shards(): outgoing.at[target_slot]]
    all_to_all x3 -> x0, starting transfers between devices: 17.4 us -> none  [the longest x1 7.25 us: shards(): lax.all_to_all(wanted, 'row', split_axis=0, concat_axis=0, tiled=True)]
    ppermute x0 -> x30, waiting for transfers between devices: none -> 16.9 us  [the longest x14 8.48 us: shift_pair(): lax.ppermute(pair[1], 'row', bwd)]
    dot_general x5 -> x0, matrix products: 13.7 us -> none  [the longest x1 4.46 us: shards(): lax.dot_general(tiles_bf, full_rows, (((3,), (1,)), ((0,), (0,))), prefer...]
    pallas_call x0 -> x17, Pallas kernels: none -> 13.2 us  [the longest x16 10.8 us: call(): pl.pallas_call(body, out_shape=outs, in_specs=ins, out_specs=jax.tree.map...]
    reshape x3 -> x0, local copies, waits for them, and re-layouts: 13 us -> none  [the longest x1 11.4 us: shards(): outgoing = outgoing.reshape(peer_count, per_peer, half_rows, feat_width)]
  transfers between devices with their start and end apart: 4 -> 30, of which waited for: 4 -> 15; matrix products, arithmetic and copies ran while one was open for 1% -> 0% of each run, Pallas kernels for 0% -> 16%
where the time goes in v2:
time: 61.7 us; the launch traced here: 61.5 us
  starting transfers between devices  30.3 us (49%)
  waiting for transfers between devices  16.9 us (27%)
  Pallas kernels  13.2 us (21%)
  between operations  0.89 us (1%)
    ppermute x14, starting transfers between devices, shift_pair(): lax.ppermute(pair[0], 'row', fwd)  21.9 us
    pallas_call x16, Pallas kernels, call(): pl.pallas_call(body, out_shape=outs, in_specs=ins, out_specs=jax.tree.map...  10.8 us
    ppermute x14, waiting for transfers between devices, shift_pair(): lax.ppermute(pair[1], 'row', bwd)  8.48 us
    ppermute x14, starting transfers between devices, shift_pair(): lax.ppermute(pair[1], 'row', bwd)  8.14 us
    ppermute x14, waiting for transfers between devices, shift_pair(): lax.ppermute(pair[0], 'row', fwd)  6.1 us
    pallas_call x1, Pallas kernels, dense_plan(): pl.pallas_call(densify, out_shape=pltpu.VMEM((n * rows, span), BF16), in_...  2.35 us
  transfers between devices with their start and end apart: 30, of which 15 were waited for; matrix products, arithmetic and copies ran while one was open for 0% of the time, Pallas kernels for 16%

profile of v2, /device:TPU:0, one launch (start us, length us, event | category | flops | bytes accessed | tf_op | source)
XLA Modules:
  0.0 61.5 jit_solution(14669941918992900198)
XLA Ops:
  0.6 1.3 %project.1 = (bf16[256,256]{1,0:T(8,128)(2,1)S(1)}, bf16[256,256]{1,0:T(8,128)(2,1)S(1)}, f32[512,128]{1,0:T(8,128)S(1)}) custom-call(s32[8,64]{1,0:T(8,128)} %deg_hbm.1, bf16[512,256]{1,0:T(8,128)(2,1)} %bitcast.10, bf16[256,256]{1,0:T(8,128)(2,1)} %w.1), custom_call_target="tpu_custom_call" | custom-call | flops 67108864 | bytes 524288 | tf_op jit(solution)/shard_map/project/pallas_call | solution.py:83
  1.9 3.1 %collective-permute-start.2 = (bf16[256,256]{1,0:T(8,128)(2,1)S(1)}, bf16[256,256]{1,0:T(8,128)(2,1)S(1)}, u32[]{:S(2)}, u32[]{:S(2)}) collective-permute-start(bf16[256,256]{1,0:T(8,128)(2,1)S(1)} %get-tuple-element.51.refs_0_.s0), channel_id=1, source_target_pairs={{0,4},{4,8},{8,12},{12,14},{14,10},{10,6},{6,2},{2,0},{1,5},{5,9},... | collective-permute-start | bytes 393224 | tf_op jit(solution)/shard_map/ppermute | solution.py:214
  5.0 2.0 %collective-permute-start = (bf16[256,256]{1,0:T(8,128)(2,1)S(1)}, bf16[256,256]{1,0:T(8,128)(2,1)S(1)}, u32[]{:S(2)}, u32[]{:S(2)}) collective-permute-start(bf16[256,256]{1,0:T(8,128)(2,1)S(1)} %get-tuple-element.50.refs_1_.s1), channel_id=1, source_target_pairs={{0,4},{4,8},{8,12},{12,14},{14,10},{10,6},{6,2},{2,0},{1,5},{5,9},... | collective-permute-start | bytes 393224 | tf_op jit(solution)/shard_map/ppermute | solution.py:214
  7.0 2.3 %densify.1.dense = bf16[4096,1024]{1,0:T(8,128)(2,1)S(1)} custom-call(s32[8,16]{1,0:T(8,128)} %cols_hbm.1, s32[128,64,128]{2,1,0:T(8,128)} %adj_hbm.1), custom_call_target="tpu_custom_call" | custom-call | bytes 4194304 | tf_op jit(solution)/shard_map/densify/pallas_call | solution.py:196
  9.4 2.1 %collective-permute-start.5 = (bf16[256,256]{1,0:T(8,128)(2,1)S(1)}, bf16[256,256]{1,0:T(8,128)(2,1)S(1)}, u32[]{:S(2)}, u32[]{:S(2)}) collective-permute-start(bf16[256,256]{1,0:T(8,128)(2,1)S(1)} %collective-permute-done.2.refs_2_), channel_id=1, source_target_pairs={{0,4},{4,8},{8,12},{12,14},{14,10},{10,6},{6,2},{2,0},{1,5},{5,9},... | collective-permute-start | bytes 393224 | tf_op jit(solution)/shard_map/ppermute | solution.py:214
  11.4 2.0 %collective-permute-start.3 = (bf16[256,256]{1,0:T(8,128)(2,1)S(1)}, bf16[256,256]{1,0:T(8,128)(2,1)S(1)}, u32[]{:S(2)}, u32[]{:S(2)}) collective-permute-start(bf16[256,256]{1,0:T(8,128)(2,1)S(1)} %collective-permute-done.refs_0_), channel_id=1, source_target_pairs={{0,4},{4,8},{8,12},{12,14},{14,10},{10,6},{6,2},{2,0},{1,5},{5,9},... | collective-permute-start | bytes 393224 | tf_op jit(solution)/shard_map/ppermute | solution.py:214
  14.3 1.4 %collective-permute-done.5.refs_2_ = bf16[256,256]{1,0:T(8,128)(2,1)S(1)} collective-permute-done((bf16[256,256]{1,0:T(8,128)(2,1)S(1)}, bf16[256,256]{1,0:T(8,128)(2,1)S(1)}, u32[]{:S(2)}, u32[]{:S(2)}) %collective-permute-start.5) | collective-permute-done | bytes 131104 | tf_op jit(solution)/shard_map/ppermute | solution.py:214
  15.7 1.9 %collective-permute-start.10 = (bf16[256,256]{1,0:T(8,128)(2,1)S(1)}, bf16[256,256]{1,0:T(8,128)(2,1)S(1)}, u32[]{:S(2)}, u32[]{:S(2)}) collective-permute-start(bf16[256,256]{1,0:T(8,128)(2,1)S(1)} %collective-permute-done.5.refs_2_), channel_id=1, source_target_pairs={{0,4},{4,8},{8,12},{12,14},{14,10},{10,6},{6,2},{2,0},{1,5},{5,9},... | collective-permute-start | bytes 393224 | tf_op jit(solution)/shard_map/ppermute | solution.py:214
  18.6 1.5 %collective-permute-done.8.refs_1_ = bf16[256,256]{1,0:T(8,128)(2,1)S(1)} collective-permute-done((bf16[256,256]{1,0:T(8,128)(2,1)S(1)}, bf16[256,256]{1,0:T(8,128)(2,1)S(1)}, u32[]{:S(2)}, u32[]{:S(2)}) %collective-permute-start.8) | collective-permute-done | bytes 131104 | tf_op jit(solution)/shard_map/ppermute | solution.py:214
  20.6 1.5 %collective-permute-start.7 = (bf16[256,256]{1,0:T(8,128)(2,1)S(1)}, bf16[256,256]{1,0:T(8,128)(2,1)S(1)}, u32[]{:S(2)}, u32[]{:S(2)}) collective-permute-start(bf16[256,256]{1,0:T(8,128)(2,1)S(1)} %collective-permute-done.3.refs_0_), channel_id=1, source_target_pairs={{0,4},{4,8},{8,12},{12,14},{14,10},{10,6},{6,2},{2,0},{1,5},{5,9},... | collective-permute-start | bytes 393224 | tf_op jit(solution)/shard_map/ppermute | solution.py:214
  22.1 0.8 %collective-permute-done.11.refs_3_ = bf16[256,256]{1,0:T(8,128)(2,1)S(1)} collective-permute-done((bf16[256,256]{1,0:T(8,128)(2,1)S(1)}, bf16[256,256]{1,0:T(8,128)(2,1)S(1)}, u32[]{:S(2)}, u32[]{:S(2)}) %collective-permute-start.11) | collective-permute-done | bytes 131104 | tf_op jit(solution)/shard_map/ppermute | solution.py:214
  23.0 0.8 %collective-permute-start.13 = (bf16[256,256]{1,0:T(8,128)(2,1)S(1)}, bf16[256,256]{1,0:T(8,128)(2,1)S(1)}, u32[]{:S(2)}, u32[]{:S(2)}) collective-permute-start(bf16[256,256]{1,0:T(8,128)(2,1)S(1)} %collective-permute-done.11.refs_3_), channel_id=1, source_target_pairs={{4,0},{8,4},{12,8},{14,12},{10,14},{6,10},{2,6},{0,2},{5,1},{9,5},... | collective-permute-start | bytes 393224 | tf_op jit(solution)/shard_map/ppermute | solution.py:214
  23.7 1.2 %collective-permute-start.12 = (bf16[256,256]{1,0:T(8,128)(2,1)S(1)}, bf16[256,256]{1,0:T(8,128)(2,1)S(1)}, u32[]{:S(2)}, u32[]{:S(2)}) collective-permute-start(bf16[256,256]{1,0:T(8,128)(2,1)S(1)} %collective-permute-done.10.refs_2_), channel_id=1, source_target_pairs={{0,4},{4,8},{8,12},{12,14},{14,10},{10,6},{6,2},{2,0},{1,5},{5,9},... | collective-permute-start | bytes 393224 | tf_op jit(solution)/shard_map/ppermute | solution.py:214
  25.7 1.6 %turn.1 = (f32[512,256]{1,0:T(8,128)S(1)}, f32[512,256]{1,0:T(8,128)S(1)}, bf16[512,512]{1,0:T(8,128)(2,1)S(1)}, bf16[512,512]{1,0:T(8,128)(2,1)S(1)}, bf16[512,...) custom-call(bf16[4096,1024]{1,0:T(8,128)(2,1)S(1)} %densify.1.dense, bf16[256,256]{1,0:T(8,128)(2,1)S(1)} %collective-permute-done.7.fa, ...), custom_call_target="tpu_custom_call" | custom-call | flops 402653184 | bytes 1572864 | tf_op jit(solution)/shard_map/turn/pallas_call | solution.py:83
  27.9 0.8 %collective-permute-done.12.fa = bf16[256,256]{1,0:T(8,128)(2,1)S(1)} collective-permute-done((bf16[256,256]{1,0:T(8,128)(2,1)S(1)}, bf16[256,256]{1,0:T(8,128)(2,1)S(1)}, u32[]{:S(2)}, u32[]{:S(2)}) %collective-permute-start.12) | collective-permute-done | bytes 131104 | tf_op jit(solution)/shard_map/ppermute | solution.py:214
  29.4 1.2 %collective-permute-done.14.got = bf16[512,256]{1,0:T(8,128)(2,1)S(1)} collective-permute-done((bf16[512,256]{1,0:T(8,128)(2,1)S(1)}, bf16[512,256]{1,0:T(8,128)(2,1)S(1)}, u32[]{:S(2)}, u32[]{:S(2)}) %collective-permute-start.14) | collective-permute-done | bytes 262176 | tf_op jit(solution)/shard_map/ppermute | solution.py:312
  31.4 1.1 %collective-permute-done.15.peer.back = bf16[512,256]{1,0:T(8,128)(2,1)S(1)} collective-permute-done((bf16[512,256]{1,0:T(8,128)(2,1)S(1)}, bf16[512,256]{1,0:T(8,128)(2,1)S(1)}, u32[]{:S(2)}, u32[]{:S(2)}) %collective-permute-start.15) | collective-permute-done | bytes 262176 | tf_op jit(solution)/shard_map/ppermute | solution.py:343
  32.8 1.3 %collective-permute-start.19 = (bf16[256,256]{1,0:T(8,128)(2,1)S(1)}, bf16[256,256]{1,0:T(8,128)(2,1)S(1)}, u32[]{:S(2)}, u32[]{:S(2)}) collective-permute-start(bf16[256,256]{1,0:T(8,128)(2,1)S(1)} %get-tuple-element.76), channel_id=1, source_target_pairs={{0,4},{4,8},{8,12},{12,14},{14,10},{10,6},{6,2},{2,0},{1,5},{5,9},... | collective-permute-start | bytes 393224 | tf_op jit(solution)/shard_map/ppermute | solution.py:214
  34.1 0.8 %collective-permute-start.18 = (bf16[256,256]{1,0:T(8,128)(2,1)S(1)}, bf16[256,256]{1,0:T(8,128)(2,1)S(1)}, u32[]{:S(2)}, u32[]{:S(2)}) collective-permute-start(bf16[256,256]{1,0:T(8,128)(2,1)S(1)} %get-tuple-element.74), channel_id=1, source_target_pairs={{4,0},{8,4},{12,8},{14,12},{10,14},{6,10},{2,6},{0,2},{5,1},{9,5},... | collective-permute-start | bytes 393224 | tf_op jit(solution)/shard_map/ppermute | solution.py:214
  35.3 1.6 %collective-permute-start.16 = (bf16[256,256]{1,0:T(8,128)(2,1)S(1)}, bf16[256,256]{1,0:T(8,128)(2,1)S(1)}, u32[]{:S(2)}, u32[]{:S(2)}) collective-permute-start(bf16[256,256]{1,0:T(8,128)(2,1)S(1)} %get-tuple-element.68), channel_id=1, source_target_pairs={{4,0},{8,4},{12,8},{14,12},{10,14},{6,10},{2,6},{0,2},{5,1},{9,5},... | collective-permute-start | bytes 393224 | tf_op jit(solution)/shard_map/ppermute | solution.py:214
  38.4 2.0 %collective-permute-done.18 = bf16[256,256]{1,0:T(8,128)(2,1)S(1)} collective-permute-done((bf16[256,256]{1,0:T(8,128)(2,1)S(1)}, bf16[256,256]{1,0:T(8,128)(2,1)S(1)}, u32[]{:S(2)}, u32[]{:S(2)}) %collective-permute-start.18) | collective-permute-done | bytes 131104 | tf_op jit(solution)/shard_map/ppermute | solution.py:214
  41.2 1.3 %collective-permute-start.20 = (bf16[256,256]{1,0:T(8,128)(2,1)S(1)}, bf16[256,256]{1,0:T(8,128)(2,1)S(1)}, u32[]{:S(2)}, u32[]{:S(2)}) collective-permute-start(bf16[256,256]{1,0:T(8,128)(2,1)S(1)} %add_convert_fusion.9), channel_id=1, source_target_pairs={{0,4},{4,8},{8,12},{12,14},{14,10},{10,6},{6,2},{2,0},{1,5},{5,9},... | collective-permute-start | bytes 393224 | tf_op jit(solution)/shard_map/ppermute | solution.py:214
  44.1 1.3 %collective-permute-start.23 = (bf16[256,256]{1,0:T(8,128)(2,1)S(1)}, bf16[256,256]{1,0:T(8,128)(2,1)S(1)}, u32[]{:S(2)}, u32[]{:S(2)}) collective-permute-start(bf16[256,256]{1,0:T(8,128)(2,1)S(1)} %add_convert_fusion.7), channel_id=1, source_target_pairs={{0,4},{4,8},{8,12},{12,14},{14,10},{10,6},{6,2},{2,0},{1,5},{5,9},... | collective-permute-start | bytes 393224 | tf_op jit(solution)/shard_map/ppermute | solution.py:214
  46.2 1.4 %collective-permute-done.20 = bf16[256,256]{1,0:T(8,128)(2,1)S(1)} collective-permute-done((bf16[256,256]{1,0:T(8,128)(2,1)S(1)}, bf16[256,256]{1,0:T(8,128)(2,1)S(1)}, u32[]{:S(2)}, u32[]{:S(2)}) %collective-permute-start.20) | collective-permute-done | bytes 131104 | tf_op jit(solution)/shard_map/ppermute | solution.py:214
  47.6 1.4 %collective-permute-start.21 = (bf16[256,256]{1,0:T(8,128)(2,1)S(1)}, bf16[256,256]{1,0:T(8,128)(2,1)S(1)}, u32[]{:S(2)}, u32[]{:S(2)}) collective-permute-start(bf16[256,256]{1,0:T(8,128)(2,1)S(1)} %add_convert_fusion.5), channel_id=1, source_target_pairs={{0,4},{4,8},{8,12},{12,14},{14,10},{10,6},{6,2},{2,0},{1,5},{5,9},... | collective-permute-start | bytes 393224 | tf_op jit(solution)/shard_map/ppermute | solution.py:214
  50.1 1.6 %collective-permute-start.29 = (bf16[256,256]{1,0:T(8,128)(2,1)S(1)}, bf16[256,256]{1,0:T(8,128)(2,1)S(1)}, u32[]{:S(2)}, u32[]{:S(2)}) collective-permute-start(bf16[256,256]{1,0:T(8,128)(2,1)S(1)} %add_convert_fusion.2), channel_id=1, source_target_pairs={{4,0},{8,4},{12,8},{14,12},{10,14},{6,10},{2,6},{0,2},{5,1},{9,5},... | collective-permute-start | bytes 393224 | tf_op jit(solution)/shard_map/ppermute | solution.py:214
  52.2 1.8 %collective-permute-done.21 = bf16[256,256]{1,0:T(8,128)(2,1)S(1)} collective-permute-done((bf16[256,256]{1,0:T(8,128)(2,1)S(1)}, bf16[256,256]{1,0:T(8,128)(2,1)S(1)}, u32[]{:S(2)}, u32[]{:S(2)}) %collective-permute-start.21) | collective-permute-done | bytes 131104 | tf_op jit(solution)/shard_map/ppermute | solution.py:214
  54.0 1.4 %collective-permute-done.26 = bf16[256,256]{1,0:T(8,128)(2,1)S(1)} collective-permute-done((bf16[256,256]{1,0:T(8,128)(2,1)S(1)}, bf16[256,256]{1,0:T(8,128)(2,1)S(1)}, u32[]{:S(2)}, u32[]{:S(2)}) %collective-permute-start.26) | collective-permute-done | bytes 131104 | tf_op jit(solution)/shard_map/ppermute | solution.py:214
  55.6 1.9 %collective-permute-start.25 = (bf16[256,256]{1,0:T(8,128)(2,1)S(1)}, bf16[256,256]{1,0:T(8,128)(2,1)S(1)}, u32[]{:S(2)}, u32[]{:S(2)}) collective-permute-start(bf16[256,256]{1,0:T(8,128)(2,1)S(1)} %add_convert_fusion.1), channel_id=1, source_target_pairs={{0,4},{4,8},{8,12},{12,14},{14,10},{10,6},{6,2},{2,0},{1,5},{5,9},... | collective-permute-start | bytes 393224 | tf_op jit(solution)/shard_map/ppermute | solution.py:214
  57.5 0.9 %mix_out.1 = bf16[512,256]{1,0:T(8,128)(2,1)} custom-call(f32[512,256]{1,0:T(8,128)S(1)} %gather_keep.1.keep, bf16[512,256]{1,0:T(8,128)(2,1)S(1)} %collective-permute-done.14.got, bf16[256,256]{1,0:T(8,128)(2,1)S(1)} %get-tuple-element.51.refs_0_.s0, bf16[256,256]{1,0:T(8,128)(2,1)S(1)} %get-tuple-element.50.refs_1_.s1, f32[512,128]{1,0:T(8,128)S(1)} %get-tuple-element.66.sc), custom_call_target="tpu_custom_call" | custom-call | flops 1310720 | bytes 1572864 | tf_op jit(solution)/shard_map/mix_out/pallas_call | solution.py:83
  58.4 2.1 %collective-permute-done.27.r1 = bf16[256,256]{1,0:T(8,128)(2,1)S(1)} collective-permute-done((bf16[256,256]{1,0:T(8,128)(2,1)S(1)}, bf16[256,256]{1,0:T(8,128)(2,1)S(1)}, u32[]{:S(2)}, u32[]{:S(2)}) %collective-permute-start.27) | collective-permute-done | bytes 131104 | tf_op jit(solution)/shard_map/ppermute | solution.py:214
  60.6 1.0 %finish.1 = bf16[512,256]{1,0:T(8,128)(2,1)} custom-call(f32[256,256]{1,0:T(8,128)S(1)} %get-tuple-element.85.own0, f32[256,256]{1,0:T(8,128)S(1)} %get-tuple-element.86.own1, bf16[256,256]{1,0:T(8,128)(2,1)S(1)} %collective-permute-done.25.g0, bf16[256,256]{1,0:T(8,128)(2,1)S(1)} %collective-permute-done.27.r1, ...), custom_call_target="tpu_custom_call" | custom-call | flops 67108864 | bytes 1048576 | tf_op jit(solution)/shard_map/finish/pallas_call | solution.py:83
  (59 shorter events, 12.2 us)
Async XLA Ops:
  1.9 7.5 %collective-permute-start.2 = (bf16[256,256]{1,0:T(8,128)(2,1)S(1)}, bf16[256,256]{1,0:T(8,128)(2,1)S(1)}, u32[]{:S(2)}, u32[]{:S(2)}) collective-permute-start(bf16[256,256]{1,0:T(8,128)(2,1)S(1)} %get-tuple-element.51.refs_0_.s0), channel_id=1, source_target_pairs={{0,4},{4,8},{8,12},{12,14},{14,10},{10,6},{6,2},{2,0},{1,5},{5,9},... | collective-permute-start | bytes 393224 | tf_op jit(solution)/shard_map/ppermute | solution.py:214
  5.0 6.5 %collective-permute-start.1 = (bf16[256,256]{1,0:T(8,128)(2,1)S(1)}, bf16[256,256]{1,0:T(8,128)(2,1)S(1)}, u32[]{:S(2)}, u32[]{:S(2)}) collective-permute-start(bf16[256,256]{1,0:T(8,128)(2,1)S(1)} %get-tuple-element.50.refs_1_.s1), channel_id=1, source_target_pairs={{4,0},{8,4},{12,8},{14,12},{10,14},{6,10},{2,6},{0,2},{5,1},{9,5},... | collective-permute-start | bytes 393224 | tf_op jit(solution)/shard_map/ppermute | solution.py:214
  5.0 6.5 %collective-permute-start = (bf16[256,256]{1,0:T(8,128)(2,1)S(1)}, bf16[256,256]{1,0:T(8,128)(2,1)S(1)}, u32[]{:S(2)}, u32[]{:S(2)}) collective-permute-start(bf16[256,256]{1,0:T(8,128)(2,1)S(1)} %get-tuple-element.50.refs_1_.s1), channel_id=1, source_target_pairs={{0,4},{4,8},{8,12},{12,14},{14,10},{10,6},{6,2},{2,0},{1,5},{5,9},... | collective-permute-start | bytes 393224 | tf_op jit(solution)/shard_map/ppermute | solution.py:214
  7.0 6.5 %collective-permute-start.4 = (bf16[256,256]{1,0:T(8,128)(2,1)S(1)}, bf16[256,256]{1,0:T(8,128)(2,1)S(1)}, u32[]{:S(2)}, u32[]{:S(2)}) collective-permute-start(bf16[256,256]{1,0:T(8,128)(2,1)S(1)} %get-tuple-element.51.refs_0_.s0), channel_id=1, source_target_pairs={{4,0},{8,4},{12,8},{14,12},{10,14},{6,10},{2,6},{0,2},{5,1},{9,5},... | collective-permute-start | bytes 393224 | tf_op jit(solution)/shard_map/ppermute | solution.py:214
  9.4 6.3 %collective-permute-start.5 = (bf16[256,256]{1,0:T(8,128)(2,1)S(1)}, bf16[256,256]{1,0:T(8,128)(2,1)S(1)}, u32[]{:S(2)}, u32[]{:S(2)}) collective-permute-start(bf16[256,256]{1,0:T(8,128)(2,1)S(1)} %collective-permute-done.2.refs_2_), channel_id=1, source_target_pairs={{0,4},{4,8},{8,12},{12,14},{14,10},{10,6},{6,2},{2,0},{1,5},{5,9},... | collective-permute-start | bytes 393224 | tf_op jit(solution)/shard_map/ppermute | solution.py:214
  11.4 6.1 %collective-permute-start.6 = (bf16[256,256]{1,0:T(8,128)(2,1)S(1)}, bf16[256,256]{1,0:T(8,128)(2,1)S(1)}, u32[]{:S(2)}, u32[]{:S(2)}) collective-permute-start(bf16[256,256]{1,0:T(8,128)(2,1)S(1)} %collective-permute-done.1.refs_3_), channel_id=1, source_target_pairs={{4,0},{8,4},{12,8},{14,12},{10,14},{6,10},{2,6},{0,2},{5,1},{9,5},... | collective-permute-start | bytes 393224 | tf_op jit(solution)/shard_map/ppermute | solution.py:214
  11.4 7.1 %collective-permute-start.3 = (bf16[256,256]{1,0:T(8,128)(2,1)S(1)}, bf16[256,256]{1,0:T(8,128)(2,1)S(1)}, u32[]{:S(2)}, u32[]{:S(2)}) collective-permute-start(bf16[256,256]{1,0:T(8,128)(2,1)S(1)} %collective-permute-done.refs_0_), channel_id=1, source_target_pairs={{0,4},{4,8},{8,12},{12,14},{14,10},{10,6},{6,2},{2,0},{1,5},{5,9},... | collective-permute-start | bytes 393224 | tf_op jit(solution)/shard_map/ppermute | solution.py:214
  13.5 6.6 %collective-permute-start.8 = (bf16[256,256]{1,0:T(8,128)(2,1)S(1)}, bf16[256,256]{1,0:T(8,128)(2,1)S(1)}, u32[]{:S(2)}, u32[]{:S(2)}) collective-permute-start(bf16[256,256]{1,0:T(8,128)(2,1)S(1)} %collective-permute-done.4.refs_1_), channel_id=1, source_target_pairs={{4,0},{8,4},{12,8},{14,12},{10,14},{6,10},{2,6},{0,2},{5,1},{9,5},... | collective-permute-start | bytes 393224 | tf_op jit(solution)/shard_map/ppermute | solution.py:214
  15.7 6.4 %collective-permute-start.10 = (bf16[256,256]{1,0:T(8,128)(2,1)S(1)}, bf16[256,256]{1,0:T(8,128)(2,1)S(1)}, u32[]{:S(2)}, u32[]{:S(2)}) collective-permute-start(bf16[256,256]{1,0:T(8,128)(2,1)S(1)} %collective-permute-done.5.refs_2_), channel_id=1, source_target_pairs={{0,4},{4,8},{8,12},{12,14},{14,10},{10,6},{6,2},{2,0},{1,5},{5,9},... | collective-permute-start | bytes 393224 | tf_op jit(solution)/shard_map/ppermute | solution.py:214
  17.6 5.4 %collective-permute-start.11 = (bf16[256,256]{1,0:T(8,128)(2,1)S(1)}, bf16[256,256]{1,0:T(8,128)(2,1)S(1)}, u32[]{:S(2)}, u32[]{:S(2)}) collective-permute-start(bf16[256,256]{1,0:T(8,128)(2,1)S(1)} %collective-permute-done.6.refs_3_), channel_id=1, source_target_pairs={{4,0},{8,4},{12,8},{14,12},{10,14},{6,10},{2,6},{0,2},{5,1},{9,5},... | collective-permute-start | bytes 393224 | tf_op jit(solution)/shard_map/ppermute | solution.py:214
  20.1 5.6 %collective-permute-start.9 = (bf16[256,256]{1,0:T(8,128)(2,1)S(1)}, bf16[256,256]{1,0:T(8,128)(2,1)S(1)}, u32[]{:S(2)}, u32[]{:S(2)}) collective-permute-start(bf16[256,256]{1,0:T(8,128)(2,1)S(1)} %collective-permute-done.8.refs_1_), channel_id=1, source_target_pairs={{4,0},{8,4},{12,8},{14,12},{10,14},{6,10},{2,6},{0,2},{5,1},{9,5},... | collective-permute-start | bytes 393224 | tf_op jit(solution)/shard_map/ppermute | solution.py:214
  20.6 5.1 %collective-permute-start.7 = (bf16[256,256]{1,0:T(8,128)(2,1)S(1)}, bf16[256,256]{1,0:T(8,128)(2,1)S(1)}, u32[]{:S(2)}, u32[]{:S(2)}) collective-permute-start(bf16[256,256]{1,0:T(8,128)(2,1)S(1)} %collective-permute-done.3.refs_0_), channel_id=1, source_target_pairs={{0,4},{4,8},{8,12},{12,14},{14,10},{10,6},{6,2},{2,0},{1,5},{5,9},... | collective-permute-start | bytes 393224 | tf_op jit(solution)/shard_map/ppermute | solution.py:214
  23.0 5.0 %collective-permute-start.13 = (bf16[256,256]{1,0:T(8,128)(2,1)S(1)}, bf16[256,256]{1,0:T(8,128)(2,1)S(1)}, u32[]{:S(2)}, u32[]{:S(2)}) collective-permute-start(bf16[256,256]{1,0:T(8,128)(2,1)S(1)} %collective-permute-done.11.refs_3_), channel_id=1, source_target_pairs={{4,0},{8,4},{12,8},{14,12},{10,14},{6,10},{2,6},{0,2},{5,1},{9,5},... | collective-permute-start | bytes 393224 | tf_op jit(solution)/shard_map/ppermute | solution.py:214
  23.7 5.0 %collective-permute-start.12 = (bf16[256,256]{1,0:T(8,128)(2,1)S(1)}, bf16[256,256]{1,0:T(8,128)(2,1)S(1)}, u32[]{:S(2)}, u32[]{:S(2)}) collective-permute-start(bf16[256,256]{1,0:T(8,128)(2,1)S(1)} %collective-permute-done.10.refs_2_), channel_id=1, source_target_pairs={{0,4},{4,8},{8,12},{12,14},{14,10},{10,6},{6,2},{2,0},{1,5},{5,9},... | collective-permute-start | bytes 393224 | tf_op jit(solution)/shard_map/ppermute | solution.py:214
  25.7 4.9 %copy-start.1 = (bf16[8,64,256]{2,1,0:T(8,128)(2,1)S(1)}, bf16[8,64,256]{2,1,0:T(8,128)(2,1)}, u32[]{:S(2)}) copy-start(bf16[8,64,256]{2,1,0:T(8,128)(2,1)} %param.11) | copy-start | bytes 786436
  29.0 1.6 %collective-permute-start.14 = (bf16[512,256]{1,0:T(8,128)(2,1)S(1)}, bf16[512,256]{1,0:T(8,128)(2,1)S(1)}, u32[]{:S(2)}, u32[]{:S(2)}) collective-permute-start(bf16[512,256]{1,0:T(8,128)(2,1)S(1)} %gather_give.1), channel_id=1, source_target_pairs={{0,1},{1,0},{2,3},{3,2},{4,5},{5,4},{6,7},{7,6},{8,9},{9,8},{10,11... | collective-permute-start | bytes 786440 | tf_op jit(solution)/shard_map/ppermute | solution.py:312
  30.9 1.6 %collective-permute-start.15 = (bf16[512,256]{1,0:T(8,128)(2,1)S(1)}, bf16[512,256]{1,0:T(8,128)(2,1)S(1)}, u32[]{:S(2)}, u32[]{:S(2)}) collective-permute-start(bf16[512,256]{1,0:T(8,128)(2,1)S(1)} %mix_back.1.back), channel_id=1, source_target_pairs={{0,1},{1,0},{2,3},{3,2},{4,5},{5,4},{6,7},{7,6},{8,9},{9,8},{10,11... | collective-permute-start | bytes 786440 | tf_op jit(solution)/shard_map/ppermute | solution.py:343
  32.8 5.6 %collective-permute-start.19 = (bf16[256,256]{1,0:T(8,128)(2,1)S(1)}, bf16[256,256]{1,0:T(8,128)(2,1)S(1)}, u32[]{:S(2)}, u32[]{:S(2)}) collective-permute-start(bf16[256,256]{1,0:T(8,128)(2,1)S(1)} %get-tuple-element.76), channel_id=1, source_target_pairs={{0,4},{4,8},{8,12},{12,14},{14,10},{10,6},{6,2},{2,0},{1,5},{5,9},... | collective-permute-start | bytes 393224 | tf_op jit(solution)/shard_map/ppermute | solution.py:214
  34.1 6.4 %collective-permute-start.18 = (bf16[256,256]{1,0:T(8,128)(2,1)S(1)}, bf16[256,256]{1,0:T(8,128)(2,1)S(1)}, u32[]{:S(2)}, u32[]{:S(2)}) collective-permute-start(bf16[256,256]{1,0:T(8,128)(2,1)S(1)} %get-tuple-element.74), channel_id=1, source_target_pairs={{4,0},{8,4},{12,8},{14,12},{10,14},{6,10},{2,6},{0,2},{5,1},{9,5},... | collective-permute-start | bytes 393224 | tf_op jit(solution)/shard_map/ppermute | solution.py:214
  35.3 8.0 %collective-permute-start.16 = (bf16[256,256]{1,0:T(8,128)(2,1)S(1)}, bf16[256,256]{1,0:T(8,128)(2,1)S(1)}, u32[]{:S(2)}, u32[]{:S(2)}) collective-permute-start(bf16[256,256]{1,0:T(8,128)(2,1)S(1)} %get-tuple-element.68), channel_id=1, source_target_pairs={{4,0},{8,4},{12,8},{14,12},{10,14},{6,10},{2,6},{0,2},{5,1},{9,5},... | collective-permute-start | bytes 393224 | tf_op jit(solution)/shard_map/ppermute | solution.py:214
  37.0 6.3 %collective-permute-start.17 = (bf16[256,256]{1,0:T(8,128)(2,1)S(1)}, bf16[256,256]{1,0:T(8,128)(2,1)S(1)}, u32[]{:S(2)}, u32[]{:S(2)}) collective-permute-start(bf16[256,256]{1,0:T(8,128)(2,1)S(1)} %get-tuple-element.70), channel_id=1, source_target_pairs={{0,4},{4,8},{8,12},{12,14},{14,10},{10,6},{6,2},{2,0},{1,5},{5,9},... | collective-permute-start | bytes 393224 | tf_op jit(solution)/shard_map/ppermute | solution.py:214
  40.5 8.5 %collective-permute-start.24 = (bf16[256,256]{1,0:T(8,128)(2,1)S(1)}, bf16[256,256]{1,0:T(8,128)(2,1)S(1)}, u32[]{:S(2)}, u32[]{:S(2)}) collective-permute-start(bf16[256,256]{1,0:T(8,128)(2,1)S(1)} %add_convert_fusion.8), channel_id=1, source_target_pairs={{4,0},{8,4},{12,8},{14,12},{10,14},{6,10},{2,6},{0,2},{5,1},{9,5},... | collective-permute-start | bytes 393224 | tf_op jit(solution)/shard_map/ppermute | solution.py:214
  41.2 6.3 %collective-permute-start.20 = (bf16[256,256]{1,0:T(8,128)(2,1)S(1)}, bf16[256,256]{1,0:T(8,128)(2,1)S(1)}, u32[]{:S(2)}, u32[]{:S(2)}) collective-permute-start(bf16[256,256]{1,0:T(8,128)(2,1)S(1)} %add_convert_fusion.9), channel_id=1, source_target_pairs={{0,4},{4,8},{8,12},{12,14},{14,10},{10,6},{6,2},{2,0},{1,5},{5,9},... | collective-permute-start | bytes 393224 | tf_op jit(solution)/shard_map/ppermute | solution.py:214
  43.3 17.3 %copy-start = (bf16[256,256]{1,0:T(8,128)(2,1)S(1)}, bf16[256,256]{1,0:T(8,128)(2,1)}, u32[]{:S(2)}) copy-start(bf16[256,256]{1,0:T(8,128)(2,1)} %w.1) | copy-start | bytes 393220
  43.4 6.7 %collective-permute-start.22 = (bf16[256,256]{1,0:T(8,128)(2,1)S(1)}, bf16[256,256]{1,0:T(8,128)(2,1)S(1)}, u32[]{:S(2)}, u32[]{:S(2)}) collective-permute-start(bf16[256,256]{1,0:T(8,128)(2,1)S(1)} %add_convert_fusion.6), channel_id=1, source_target_pairs={{4,0},{8,4},{12,8},{14,12},{10,14},{6,10},{2,6},{0,2},{5,1},{9,5},... | collective-permute-start | bytes 393224 | tf_op jit(solution)/shard_map/ppermute | solution.py:214
  44.1 5.9 %collective-permute-start.23 = (bf16[256,256]{1,0:T(8,128)(2,1)S(1)}, bf16[256,256]{1,0:T(8,128)(2,1)S(1)}, u32[]{:S(2)}, u32[]{:S(2)}) collective-permute-start(bf16[256,256]{1,0:T(8,128)(2,1)S(1)} %add_convert_fusion.7), channel_id=1, source_target_pairs={{0,4},{4,8},{8,12},{12,14},{14,10},{10,6},{6,2},{2,0},{1,5},{5,9},... | collective-permute-start | bytes 393224 | tf_op jit(solution)/shard_map/ppermute | solution.py:214
  47.6 6.4 %collective-permute-start.21 = (bf16[256,256]{1,0:T(8,128)(2,1)S(1)}, bf16[256,256]{1,0:T(8,128)(2,1)S(1)}, u32[]{:S(2)}, u32[]{:S(2)}) collective-permute-start(bf16[256,256]{1,0:T(8,128)(2,1)S(1)} %add_convert_fusion.5), channel_id=1, source_target_pairs={{0,4},{4,8},{8,12},{12,14},{14,10},{10,6},{6,2},{2,0},{1,5},{5,9},... | collective-permute-start | bytes 393224 | tf_op jit(solution)/shard_map/ppermute | solution.py:214
  49.0 6.4 %collective-permute-start.26 = (bf16[256,256]{1,0:T(8,128)(2,1)S(1)}, bf16[256,256]{1,0:T(8,128)(2,1)S(1)}, u32[]{:S(2)}, u32[]{:S(2)}) collective-permute-start(bf16[256,256]{1,0:T(8,128)(2,1)S(1)} %add_convert_fusion.4), channel_id=1, source_target_pairs={{4,0},{8,4},{12,8},{14,12},{10,14},{6,10},{2,6},{0,2},{5,1},{9,5},... | collective-permute-start | bytes 393224 | tf_op jit(solution)/shard_map/ppermute | solution.py:214
  50.1 8.3 %collective-permute-start.29 = (bf16[256,256]{1,0:T(8,128)(2,1)S(1)}, bf16[256,256]{1,0:T(8,128)(2,1)S(1)}, u32[]{:S(2)}, u32[]{:S(2)}) collective-permute-start(bf16[256,256]{1,0:T(8,128)(2,1)S(1)} %add_convert_fusion.2), channel_id=1, source_target_pairs={{4,0},{8,4},{12,8},{14,12},{10,14},{6,10},{2,6},{0,2},{5,1},{9,5},... | collective-permute-start | bytes 393224 | tf_op jit(solution)/shard_map/ppermute | solution.py:214
  51.7 6.6 %collective-permute-start.28 = (bf16[256,256]{1,0:T(8,128)(2,1)S(1)}, bf16[256,256]{1,0:T(8,128)(2,1)S(1)}, u32[]{:S(2)}, u32[]{:S(2)}) collective-permute-start(bf16[256,256]{1,0:T(8,128)(2,1)S(1)} %add_convert_fusion.3), channel_id=1, source_target_pairs={{0,4},{4,8},{8,12},{12,14},{14,10},{10,6},{6,2},{2,0},{1,5},{5,9},... | collective-permute-start | bytes 393224 | tf_op jit(solution)/shard_map/ppermute | solution.py:214
  55.4 5.0 %collective-permute-start.27 = (bf16[256,256]{1,0:T(8,128)(2,1)S(1)}, bf16[256,256]{1,0:T(8,128)(2,1)S(1)}, u32[]{:S(2)}, u32[]{:S(2)}) collective-permute-start(bf16[256,256]{1,0:T(8,128)(2,1)S(1)} %add_convert_fusion), channel_id=1, source_target_pairs={{4,0},{8,4},{12,8},{14,12},{10,14},{6,10},{2,6},{0,2},{5,1},{9,5},... | collective-permute-start | bytes 393224 | tf_op jit(solution)/shard_map/ppermute | solution.py:214
  55.6 5.0 %collective-permute-start.25 = (bf16[256,256]{1,0:T(8,128)(2,1)S(1)}, bf16[256,256]{1,0:T(8,128)(2,1)S(1)}, u32[]{:S(2)}, u32[]{:S(2)}) collective-permute-start(bf16[256,256]{1,0:T(8,128)(2,1)S(1)} %add_convert_fusion.1), channel_id=1, source_target_pairs={{0,4},{4,8},{8,12},{12,14},{14,10},{10,6},{6,2},{2,0},{1,5},{5,9},... | collective-permute-start | bytes 393224 | tf_op jit(solution)/shard_map/ppermute | solution.py:214

commit v3 on v2

v3 whole, which is shorter than its diff:
```python
import functools

import jax
import jax.numpy as jnp
from jax import lax
from jax.experimental import pallas as pl
from jax.experimental.pallas import tpu as pltpu
from jax.sharding import PartitionSpec as P

F32 = jnp.float32
BF16 = jnp.bfloat16


def sparse_plan(feats, weight, degree, tile_cols, adjacency, cotangent):
    blocks, half_rows, feat_width = feats.shape
    slots_per = tile_cols.shape[1]
    tile_side = adjacency.shape[2]
    peer_count = lax.axis_size("row")
    tile_count = blocks * slots_per
    per_peer = (tile_count + peer_count - 1) // peer_count
    capacity = peer_count * per_peer
    columns = tile_cols.reshape(tile_count)
    is_live = columns >= 0
    owners = jnp.where(is_live, columns // blocks, -1)
    local_block = jnp.where(is_live, columns % blocks, -1)
    earlier = jnp.arange(tile_count)[:, None] > jnp.arange(tile_count)[None, :]
    same_owner = (owners[:, None] == owners[None, :]) & earlier & is_live[None, :]
    tile_rank = jnp.sum(same_owner.astype(jnp.int32), axis=1)
    target_slot = jnp.where(is_live, owners * per_peer + tile_rank, capacity)
    wanted = jnp.zeros((capacity,), jnp.int32).at[target_slot].set(local_block + 1, mode="drop")
    wanted = wanted.reshape(peer_count, per_peer)
    received = lax.all_to_all(wanted, "row", split_axis=0, concat_axis=0, tiled=True)
    incoming = received - 1
    scaling = lax.rsqrt(degree.astype(F32) + 1.0)[..., None]
    projected = jnp.dot(
        feats.reshape(blocks * half_rows, feat_width), weight, preferred_element_type=F32
    )
    sent_rows = (scaling * projected.reshape(blocks, half_rows, feat_width)).astype(BF16)
    tiles_bf = adjacency.astype(BF16).reshape(blocks, slots_per, half_rows, tile_side)
    pick_index = jnp.where(incoming < 0, blocks, incoming)
    replies = jnp.take(sent_rows, pick_index, axis=0, mode="fill", fill_value=0)
    fetched = lax.all_to_all(replies, "row", split_axis=0, concat_axis=0, tiled=True).reshape(
        capacity, half_rows, feat_width
    )
    tile_feats = jnp.take(fetched, target_slot, axis=0, mode="fill", fill_value=0)
    tile_feats = tile_feats.reshape(blocks, slots_per, half_rows, feat_width)
    gathered = lax.dot_general(
        tiles_bf, tile_feats, (((1, 2), (1, 2)), ((0,), (0,))), preferred_element_type=F32
    )
    own_rows = lax.psum_scatter(gathered, "col", scatter_dimension=1, tiled=True)
    mixed = scaling * (own_rows + sent_rows.astype(F32))
    sigmoid_z = jax.nn.sigmoid(mixed)
    output = (mixed * sigmoid_z).astype(BF16)
    silu_slope = sigmoid_z * (1.0 + mixed * (1.0 - sigmoid_z))
    back_sent = (scaling * cotangent.astype(F32) * silu_slope).astype(BF16)
    full_rows = lax.all_gather(back_sent, "col", axis=1, tiled=True)
    partials = lax.dot_general(
        tiles_bf, full_rows, (((3,), (1,)), ((0,), (0,))), preferred_element_type=F32
    )
    outgoing = jnp.zeros((capacity, half_rows, feat_width), F32)
    outgoing = outgoing.at[target_slot].set(
        partials.reshape(tile_count, half_rows, feat_width), mode="drop"
    )
    outgoing = outgoing.reshape(peer_count, per_peer, half_rows, feat_width)
    arrived = lax.all_to_all(outgoing, "row", split_axis=0, concat_axis=0, tiled=True).reshape(
        capacity, half_rows, feat_width
    )
    selector = (incoming.reshape(capacity)[:, None] == jnp.arange(blocks)[None, :]).astype(F32)
    returned = jnp.einsum("sl,sjf->ljf", selector, arrived, precision=lax.Precision.HIGHEST)
    combined = (scaling * (returned + back_sent.astype(F32))).astype(BF16)
    grad_rows = jnp.dot(
        combined.reshape(blocks * half_rows, feat_width), weight.T, preferred_element_type=F32
    )
    return (output, grad_rows.astype(BF16).reshape(blocks, half_rows, feat_width))


VM = pl.BlockSpec(memory_space=pltpu.VMEM)
ANY = pl.BlockSpec(memory_space=pl.ANY)
OTHER = [(0, 1), (1, 0)]


def call(body, outs, ins, args, name, **kw):
    return pl.pallas_call(
        body,
        out_shape=outs,
        in_specs=ins,
        out_specs=jax.tree.map(lambda _: VM, outs),
        cost_estimate=pl.CostEstimate(flops=0, bytes_accessed=0, transcendentals=0),
        compiler_params=pltpu.CompilerParams(vmem_limit_bytes=24 * 2**20),
        name=name,
        **kw,
    )(*args)


def array(shape, dtype):
    return jax.ShapeDtypeStruct(shape, dtype)


def after(value, *tokens):
    return lax.optimization_barrier((value,) + tokens)[0]


def dense_plan(feats, weight, degree, tile_cols, adjacency, cotangent):
    blocks, half, width = feats.shape
    slots = tile_cols.shape[1]
    side = adjacency.shape[2]
    n = lax.axis_size("row")
    rows = blocks * half
    hrows = rows // 2
    span = blocks * side
    far = n // 2
    ring = [2 * p if p < far else 2 * (n - 1 - p) + 1 for p in range(n)]
    fwd = [(ring[p], ring[(p + 1) % n]) for p in range(n)]
    bwd = [(b, a) for a, b in fwd]

    def half_rows_of(d, h):
        me = lax.axis_index("row")
        z = lax.shift_right_logical(me, 1)
        place = jnp.where(lax.rem(me, 2) == 0, z, n - 1 - z)
        p = lax.rem(place + (d + n), n)
        owner = jnp.where(p < far, 2 * p, 2 * (n - 1 - p) + 1)
        return pl.ds(pl.multiple_of(owner * rows + h * hrows, hrows), hrows)

    def scale_columns(degree_values):
        scale = lax.rsqrt(degree_values.astype(F32) + 1.0)
        eye = lax.broadcasted_iota(jnp.int32, (half, half), 0) == lax.broadcasted_iota(
            jnp.int32, (half, half), 1
        )
        for b in range(blocks):
            line = jnp.broadcast_to(scale[b : b + 1, :], (half, half))
            column = jnp.sum(jnp.where(eye, line, 0.0), axis=1, keepdims=True)
            yield b, jnp.broadcast_to(column, (half, 128))

    def over(scale):
        return jnp.tile(scale, (1, width // 128))

    def project(deg_hbm, x_hbm, w_hbm, s0, s1, sc, deg, x, w, sems):
        deg_copy = pltpu.make_async_copy(deg_hbm, deg, sems.at[0])
        deg_copy.start()
        copies = []
        for src, dst, parts in ((x_hbm, x, 4), (w_hbm, w, 2)):
            step = src.shape[0] // parts
            for i in range(parts):
                at = pl.ds(i * step, step)
                copies.append(
                    pltpu.make_async_copy(src.at[at], dst.at[at], sems.at[1 + len(copies)])
                )
                copies[-1].start()
        deg_copy.wait()
        for b, column in scale_columns(deg[...]):
            sc[b * half : (b + 1) * half, :] = column
        for c in copies:
            c.wait()
        proj = jnp.dot(x[...], w[...], preferred_element_type=F32)
        out = (over(sc[...]) * proj).astype(BF16)
        s0[...] = out[:hrows]
        s1[...] = out[hrows:]

    hshape = (hrows, width)
    s0, s1, scale = call(
        project,
        (array(hshape, BF16), array(hshape, BF16), array((rows, 128), F32)),
        [ANY] * 3,
        tuple(
            pltpu.with_memory_space_constraint(a, pltpu.HBM)
            for a in (degree, feats.reshape(rows, width), weight)
        ),
        "project",
        scratch_shapes=[
            pltpu.VMEM(degree.shape, jnp.int32),
            pltpu.VMEM((rows, width), BF16),
            pltpu.VMEM(weight.shape, BF16),
            pltpu.SemaphoreType.DMA((7,)),
        ],
    )

    def densify(cols_hbm, adj_hbm, deg_hbm, cot_hbm, dense, pack, cols, adj, deg, sems):
        def tiles_of(b):
            return pl.ds(b * slots, slots)

        cols_copy = pltpu.make_async_copy(cols_hbm, cols, sems.at[blocks])
        deg_copy = pltpu.make_async_copy(deg_hbm, deg, sems.at[blocks + 1])
        cot_copy = pltpu.make_async_copy(cot_hbm, pack.at[pl.ds(0, rows)], sems.at[blocks + 2])
        cols_copy.start()
        deg_copy.start()
        copies = [
            pltpu.make_async_copy(adj_hbm.at[tiles_of(b)], adj.at[tiles_of(b)], sems.at[b])
            for b in range(blocks)
        ]
        for c in copies:
            c.start()
        cot_copy.start()
        dense[...] = jnp.zeros(dense.shape, BF16)
        pack[rows:, :] = jnp.zeros((16, width), BF16)
        deg_copy.wait()
        padded = jnp.concatenate([deg[...], jnp.zeros((16 - blocks, half), jnp.int32)], axis=0)
        pack[rows:, :half] = padded.astype(F32).astype(BF16)
        cols_copy.wait()
        for b in range(blocks):
            copies[b].wait()
            lanes = slice(b * side, (b + 1) * side)
            for k in range(slots):
                c = cols[b, k]
                tile = jnp.where(c >= 0, adj[b * slots + k], 0).astype(F32).astype(BF16)
                place = pl.ds(pl.multiple_of(jnp.maximum(c, 0) * half, half), half)
                dense[place, lanes] = dense[place, lanes] + tile
        cot_copy.wait()

    def hbm(x):
        return pltpu.with_memory_space_constraint(x, pltpu.HBM)

    shape = (rows, width)
    dense, pack = pl.pallas_call(
        densify,
        out_shape=(pltpu.VMEM((n * rows, span), BF16), array((rows + 16, width), BF16)),
        in_specs=[ANY] * 4,
        out_specs=(VM, VM),
        scratch_shapes=[
            pltpu.SMEM(tile_cols.shape, jnp.int32),
            pltpu.VMEM(adjacency.shape, jnp.int32),
            pltpu.VMEM(degree.shape, jnp.int32),
            pltpu.SemaphoreType.DMA((blocks + 3,)),
        ],
        cost_estimate=pl.CostEstimate(flops=0, bytes_accessed=0, transcendentals=0),
        compiler_params=pltpu.CompilerParams(vmem_limit_bytes=24 * 2**20),
        name="densify",
    )(hbm(tile_cols), hbm(adjacency), hbm(degree), hbm(cotangent.reshape(shape)))

    def shift_pair(pair):
        return lax.ppermute(pair[0], "row", fwd), lax.ppermute(pair[1], "row", bwd)

    def gather_terms(dense, items):
        total = None
        for d, h, ref in items:
            term = lax.dot_general(
                ref[...], dense[half_rows_of(d, h), :], (((0,), (0,)), ((), ())),
                preferred_element_type=F32,
            )
            total = term if total is None else total + term
        return total

    def gather(items, part, name):
        def body(dense, *refs):
            total = gather_terms(dense, [(d, h, r) for (d, h, _), r in zip(items, refs)])
            refs[-1][...] = total if part is None else refs[-2][...] + total

        extra = () if part is None else (part,)
        return call(
            body,
            array((width, span), F32),
            [VM] * (1 + len(items) + len(extra)),
            (dense, *[i[2] for i in items], *extra),
            name,
        )

    long, short = [(s0, s1)], [(s1, s0)]
    long.append(shift_pair(long[0]))
    short.append(shift_pair(short[0]))

    long[1] = tuple(after(x, dense) for x in long[1])
    long.append(shift_pair(long[1]))
    short.append(shift_pair(short[1]))
    long.append(shift_pair(long[2]))
    def long_items(hop):
        return [(-hop, 0, long[hop][0]), (hop, 1, long[hop][1])]

    def short_items(hop):
        return [(-hop, 1, short[hop][0]), (hop, 0, short[hop][1])]

    peer_pack = lax.ppermute(pack, "col", OTHER)

    def prepare(pack, peer_pack, scale, scaled):
        mine = lax.axis_index("col")
        for h, p in ((mine, pack), (1 - mine, peer_pack)):
            degrees = p[rows:, :half].astype(F32)[:blocks]
            for b, column in scale_columns(degrees):
                scale[b, h] = column
                scaled[b, h] = over(column) * p[b * half : (b + 1) * half, :].astype(F32)

    scale_all, scaled_cot = call(
        prepare,
        (array((blocks, 2, half, 128), F32), array((blocks, 2, half, width), F32)),
        [VM] * 2,
        (pack, peer_pack),
        "prepare",
    )
    scale_all = scale_all.reshape(span, 128)
    scaled_cot = scaled_cot.reshape(span, width)

    part = gather([(0, 0, s0), (0, 1, s1)] + long_items(1), None, "gather_near")
    short.append(shift_pair(short[2]))
    part = gather(short_items(1) + long_items(2), part, "gather_two")
    long[3] = (after(long[3][0], part), long[3][1])
    long.append(shift_pair(long[3]))
    part = gather(short_items(2) + long_items(3), after(part, scale_all), "gather_three")

    def turn(dense, fa, ba, part, s0, s1, whole, wide):
        total = part[...] + gather_terms(dense, [(-(far - 1), 1, fa), (far - 1, 0, ba)])
        whole[...] = total.T.reshape(blocks, 2, half, width)
        q = lax.axis_index("col")
        for b in range(blocks):
            at = (b * half) % hrows
            own = s0 if b < blocks // 2 else s1
            whole[b, q] = whole[b, q] + own[at : at + half, :].astype(F32)
        for h in range(2):
            wide[:, h * hrows : (h + 1) * hrows] = dense[half_rows_of(far, h), :].T

    part, turned = call(
        turn,
        (array((blocks, 2, half, width), F32), array((span, rows), BF16)),
        [VM] * 6,
        (dense, *short[3], part, s0, s1),
        "turn",
    )
    part = part.reshape(span, width)

    def node_piece(k):
        return slice(k * rows, (k + 1) * rows)

    def last(k, part, turned, fa, ba, keep, give):
        at = node_piece(k)
        total = part[at, :] + jnp.dot(turned[at, :hrows], fa[...], preferred_element_type=F32)
        total = total + jnp.dot(turned[at, hrows:], ba[...], preferred_element_type=F32)
        keep[...] = total
        give[...] = total.astype(BF16)

    keep, got = [], []
    for k in range(2):
        kept, give = call(
            functools.partial(last, k),
            (array(shape, F32), array(shape, BF16)),
            [VM] * 4,
            (part, turned, *long[far]),
            "gather_last",
        )
        keep.append(kept)
        got.append(lax.ppermute(give, "col", OTHER))

    def mix_back(k, keep, got, scale, scaled, back):
        at = node_piece(k)
        mixed = over(scale[at, :]) * (keep[...] + got[...].astype(F32))
        sig = jax.nn.sigmoid(mixed)
        slope = sig * (1.0 + mixed * (1.0 - sig))
        back[...] = (scaled[at, :] * slope).astype(BF16)

    far_rows = lambda dense, k: dense[pl.ds(half_rows_of(far, 0).start, rows), node_piece(k)]

    def far_first(dense, back, out):
        out[...] = jnp.dot(far_rows(dense, 0), back[...], preferred_element_type=F32)

    def far_second(dense, back, part, c0, c1):
        out = part[...] + jnp.dot(far_rows(dense, 1), back[...], preferred_element_type=F32)
        c0[...] = out[:hrows].astype(BF16)
        c1[...] = out[hrows:].astype(BF16)

    back = []
    for k in range(2):
        back.append(
            call(
                functools.partial(mix_back, k),
                array(shape, BF16),
                [VM] * 4,
                (keep[k], got[k], scale_all, scaled_cot),
                "mix_back",
            )
        )
        if k == 0:
            far_part = call(
                far_first, array(shape, F32), [VM] * 2, (dense, back[0]), "return_far_first"
            )
    up = call(
        far_second,
        (array(hshape, BF16), array(hshape, BF16)),
        [VM] * 3,
        (dense, back[1], far_part),
        "return_far",
    )
    token = up[0]
    up = shift_pair(up)

    def chunk(dense, back, d, h):
        at = half_rows_of(d, h)
        return sum(
            jnp.dot(dense[at, node_piece(k)], back[k][...], preferred_element_type=F32)
            for k in range(2)
        )

    def chunks(which, token, name, dtype=F32):
        def body(dense, *refs):
            for (d, h), out in zip(which, refs[2:]):
                out[...] = chunk(dense, refs[:2], d, h).astype(dtype)

        return call(
            body,
            tuple(array(hshape, dtype) for _ in which),
            [VM] * 3,
            (dense, after(back[0], token), back[1]),
            name,
        )

    def add(total, term, token):
        return (total.astype(F32) + term).astype(BF16)

    def shift(x, h):
        return lax.ppermute(x, "row", (fwd, bwd)[h])

    down = chunks([(far - 1, 1), (1 - far, 0)], token, "return_next", BF16)
    token = down[0]
    down = shift_pair(down)
    a0, a1, c0, c1 = chunks([(3, 0), (-3, 1), (2, 1), (-2, 0)], token, "return_a")
    d0, d1 = chunks([(2, 0), (-2, 1)], a0, "return_b")
    u0 = add(up[0], a0, d0)
    e0, e1 = chunks([(1, 1), (-1, 0)], u0, "return_c")
    u1 = add(up[1], a1, e0)
    f0, f1 = chunks([(1, 0), (-1, 1)], u1, "return_d")
    w0 = add(down[0], c0, f0)

    def own_base(dense, back0, back1, base0, base1):
        q = lax.axis_index("col")
        for h, (back, base) in enumerate(((back0, base0), (back1, base1))):
            mine = back[...].reshape(blocks // 2, 2, half, width)
            mine = jnp.where(q == 0, mine[:, 0], mine[:, 1]).reshape(hshape).astype(F32)
            base[...] = chunk(dense, (back0, back1), 0, h) + mine

    base = call(
        own_base,
        (array(hshape, F32), array(hshape, F32)),
        [VM] * 3,
        (dense, after(back[0], w0), back[1]),
        "own_base",
    )
    w1 = add(down[1], c1, base[0])
    u0, u1, w0, w1 = shift(u0, 0), shift(u1, 1), shift(w0, 0), shift(w1, 1)
    v0 = add(u0, d0, w1)
    v1 = add(u1, d1, v0)
    x0 = add(w0, e0, v1)
    x1 = add(w1, e1, x0)
    u0, u1, w0, w1 = shift(v0, 0), shift(v1, 1), shift(x0, 0), shift(x1, 1)
    v0 = add(u0, f0, x1)
    v1 = add(u1, f1, v0)
    up = (shift(v0, 0), shift(v1, 1))
    down = (w0, w1)

    def mix_out(keep0, keep1, got0, got1, scale, out):
        q = lax.axis_index("col")
        for k, (keep, got) in enumerate(((keep0, got0), (keep1, got1))):
            mixed = over(scale[node_piece(k), :]) * (keep[...] + got[...].astype(F32))
            mixed = mixed.reshape(blocks // 2, 2, half, width)
            mixed = jnp.where(q == 0, mixed[:, 0], mixed[:, 1]).reshape(hshape)
            out[k * hrows : (k + 1) * hrows, :] = (mixed * jax.nn.sigmoid(mixed)).astype(BF16)

    output = call(
        mix_out, array(shape, BF16), [VM] * 5, (*keep, *got, after(scale_all, v1)), "mix_out"
    )

    def finish(base0, base1, g0, r1, g1, r0, sc, w, out_hbm, out, sems):
        copies = []
        step = hrows // 2
        for h, (base, g, r) in enumerate(((base0, g0, r0), (base1, g1, r1))):
            for i in range(2):
                at = slice(i * step, (i + 1) * step)
                whole = slice(h * hrows + i * step, h * hrows + (i + 1) * step)
                total = base[at, :] + g[at, :].astype(F32) + r[at, :].astype(F32)
                comb = (over(sc[whole, :]) * total).astype(BF16)
                out[whole, :] = lax.dot_general(
                    comb, w[...], (((1,), (1,)), ((), ())), preferred_element_type=F32
                ).astype(BF16)
                to = pl.ds(h * hrows + i * step, step)
                copies.append(pltpu.make_async_copy(out.at[to], out_hbm.at[to], sems.at[2 * h + i]))
                copies[-1].start()
        for c in copies:
            c.wait()

    grad = pl.pallas_call(
        finish,
        out_shape=array(shape, BF16),
        in_specs=[VM] * 8,
        out_specs=ANY,
        scratch_shapes=[pltpu.VMEM(shape, BF16), pltpu.SemaphoreType.DMA((4,))],
        cost_estimate=pl.CostEstimate(flops=0, bytes_accessed=0, transcendentals=0),
        compiler_params=pltpu.CompilerParams(vmem_limit_bytes=24 * 2**20),
        name="finish",
    )(*base, *up, *down, scale, weight)
    return output.reshape(feats.shape), grad.reshape(feats.shape)


def shards(feats, weight, degree, tile_cols, adjacency, cotangent):
    n = lax.axis_size("row")
    blocks, half, width = feats.shape
    dense = (
        n * blocks <= blocks * tile_cols.shape[1]
        and n % 2 == 0
        and n == 8
        and blocks % 2 == 0
        and blocks <= 16
        and half % 16 == 0
        and width % 128 == 0
        and adjacency.shape[2] == 2 * half
        and lax.axis_size("col") == 2
    )
    plan = dense_plan if dense else sparse_plan
    return plan(feats, weight, degree, tile_cols, adjacency, cotangent)


def solution(mesh):
    in_specs = (
        P(("grp", "row"), "col", None),
        P(),
        P(("grp", "row"), "col"),
        P(("grp", "row"), None),
        P(("grp", "row"), "col", None),
        P(("grp", "row"), "col", None),
    )
    out_specs = (P(("grp", "row"), "col", None), P(("grp", "row"), "col", None))
    return jax.shard_map(shards, mesh=mesh, in_specs=in_specs, out_specs=out_specs, check_vma=False)
```

time: 61.7 us -> 58.4 us (0.947)
  waiting for transfers between devices: 16.9 us -> 12.3 us
  starting transfers between devices: 30.3 us -> 31.2 us
    ppermute x2 -> x13, starting transfers between devices: 0.27 us -> 11.7 us  [the longest x10 11.1 us: shift(): return lax.ppermute(x, 'row', (fwd, bwd)[h])]
    ppermute x14 -> x9, starting transfers between devices: 8.14 us -> 2.22 us  [shift_pair(): lax.ppermute(pair[1], 'row', bwd)]
    ppermute x14 -> x9, waiting for transfers between devices: 8.48 us -> 3.19 us  [shift_pair(): lax.ppermute(pair[1], 'row', bwd)]
    ppermute x14 -> x9, starting transfers between devices: 21.9 us -> 17.3 us  [shift_pair(): lax.ppermute(pair[0], 'row', fwd)]
    ppermute x2 -> x13, waiting for transfers between devices: 2.32 us -> 5.43 us  [the longest x10 4.75 us: shift(): return lax.ppermute(x, 'row', (fwd, bwd)[h])]
    ppermute x14 -> x9, waiting for transfers between devices: 6.1 us -> 3.7 us  [shift_pair(): lax.ppermute(pair[0], 'row', fwd)]
    pallas_call x1 -> x2, Pallas kernels: 2.35 us -> 3.38 us  [the longest x1 2.38 us: dense_plan(): pl.pallas_call(densify, out_shape=(pltpu.VMEM((n * rows, span), BF16), ar...]
    pallas_call x16 -> x19, Pallas kernels: 10.8 us -> 10.1 us  [call(): pl.pallas_call(body, out_shape=outs, in_specs=ins, out_specs=jax.tree.map...]
  transfers between devices with their start and end apart: 30 -> 31, of which waited for: 15 -> 15; matrix products, arithmetic and copies ran while one was open for 0% -> 0% of each run, Pallas kernels for 16% -> 18%
where the time goes in v3:
time: 58.4 us; the launch traced here: 58.2 us
  starting transfers between devices  31.2 us (53%)
  Pallas kernels  13.5 us (23%)
  waiting for transfers between devices  12.3 us (21%)
  between operations  0.9 us (2%)
    ppermute x9, starting transfers between devices, shift_pair(): lax.ppermute(pair[0], 'row', fwd)  17.3 us
    ppermute x10, starting transfers between devices, shift(): return lax.ppermute(x, 'row', (fwd, bwd)[h])  11.1 us
    pallas_call x19, Pallas kernels, call(): pl.pallas_call(body, out_shape=outs, in_specs=ins, out_specs=jax.tree.map...  10.1 us
    ppermute x10, waiting for transfers between devices, shift(): return lax.ppermute(x, 'row', (fwd, bwd)[h])  4.75 us
    ppermute x9, waiting for transfers between devices, shift_pair(): lax.ppermute(pair[0], 'row', fwd)  3.7 us
    ppermute x9, waiting for transfers between devices, shift_pair(): lax.ppermute(pair[1], 'row', bwd)  3.19 us
    pallas_call x1, Pallas kernels, dense_plan(): pl.pallas_call(densify, out_shape=(pltpu.VMEM((n * rows, span), BF16), ar...  2.38 us
    ppermute x9, starting transfers between devices, shift_pair(): lax.ppermute(pair[1], 'row', bwd)  2.22 us
  transfers between devices with their start and end apart: 31, of which 15 were waited for; matrix products, arithmetic and copies ran while one was open for 0% of the time, Pallas kernels for 18%

profile of v3, /device:TPU:0, one launch (start us, length us, event | category | flops | bytes accessed | tf_op | source)
XLA Modules:
  0.0 58.2 jit_solution(3875112545019044962)
XLA Ops:
  0.6 1.3 %project.1 = (bf16[256,256]{1,0:T(8,128)(2,1)S(1)}, bf16[256,256]{1,0:T(8,128)(2,1)S(1)}, f32[512,128]{1,0:T(8,128)S(1)}) custom-call(s32[8,64]{1,0:T(8,128)} %deg_hbm.3, bf16[512,256]{1,0:T(8,128)(2,1)} %bitcast.16, bf16[256,256]{1,0:T(8,128)(2,1)} %w.1), custom_call_target="tpu_custom_call" | custom-call | tf_op jit(solution)/shard_map/project/pallas_call | solution.py:83
  1.9 3.1 %collective-permute-start.6 = (bf16[256,256]{1,0:T(8,128)(2,1)S(1)}, bf16[256,256]{1,0:T(8,128)(2,1)S(1)}, u32[]{:S(2)}, u32[]{:S(2)}) collective-permute-start(bf16[256,256]{1,0:T(8,128)(2,1)S(1)} %get-tuple-element.44.refs_0_.s0), channel_id=1, source_target_pairs={{0,4},{4,8},{8,12},{12,14},{14,10},{10,6},{6,2},{2,0},{1,5},{5,9},... | collective-permute-start | bytes 393224 | tf_op jit(solution)/shard_map/ppermute | solution.py:230
  5.0 2.0 %collective-permute-start = (bf16[256,256]{1,0:T(8,128)(2,1)S(1)}, bf16[256,256]{1,0:T(8,128)(2,1)S(1)}, u32[]{:S(2)}, u32[]{:S(2)}) collective-permute-start(bf16[256,256]{1,0:T(8,128)(2,1)S(1)} %get-tuple-element.43.refs_1_.s1), channel_id=1, source_target_pairs={{0,4},{4,8},{8,12},{12,14},{14,10},{10,6},{6,2},{2,0},{1,5},{5,9},... | collective-permute-start | bytes 393224 | tf_op jit(solution)/shard_map/ppermute | solution.py:230
  7.0 2.4 %densify.1 = (bf16[4096,1024]{1,0:T(8,128)(2,1)S(1)}, bf16[528,256]{1,0:T(8,128)(2,1)S(1)}) custom-call(s32[8,16]{1,0:T(8,128)} %cols_hbm.1, s32[128,64,128]{2,1,0:T(8,128)} %adj_hbm.1, s32[8,64]{1,0:T(8,128)} %deg_hbm.3, bf16[512,256]{1,0:T(8,128)(2,1)} %bitcast.14), custom_call_target="tpu_custom_call" | custom-call | tf_op jit(solution)/shard_map/densify/pallas_call | solution.py:213
  9.4 2.1 %collective-permute-start.7 = (bf16[256,256]{1,0:T(8,128)(2,1)S(1)}, bf16[256,256]{1,0:T(8,128)(2,1)S(1)}, u32[]{:S(2)}, u32[]{:S(2)}) collective-permute-start(bf16[256,256]{1,0:T(8,128)(2,1)S(1)} %collective-permute-done.6.refs_2_), channel_id=1, source_target_pairs={{0,4},{4,8},{8,12},{12,14},{14,10},{10,6},{6,2},{2,0},{1,5},{5,9},... | collective-permute-start | bytes 393224 | tf_op jit(solution)/shard_map/ppermute | solution.py:230
  11.6 2.0 %collective-permute-start.1 = (bf16[256,256]{1,0:T(8,128)(2,1)S(1)}, bf16[256,256]{1,0:T(8,128)(2,1)S(1)}, u32[]{:S(2)}, u32[]{:S(2)}) collective-permute-start(bf16[256,256]{1,0:T(8,128)(2,1)S(1)} %collective-permute-done.refs_0_), channel_id=1, source_target_pairs={{0,4},{4,8},{8,12},{12,14},{14,10},{10,6},{6,2},{2,0},{1,5},{5,9},... | collective-permute-start | bytes 393224 | tf_op jit(solution)/shard_map/ppermute | solution.py:230
  13.6 0.8 %collective-permute-done.7.refs_2_ = bf16[256,256]{1,0:T(8,128)(2,1)S(1)} collective-permute-done((bf16[256,256]{1,0:T(8,128)(2,1)S(1)}, bf16[256,256]{1,0:T(8,128)(2,1)S(1)}, u32[]{:S(2)}, u32[]{:S(2)}) %collective-permute-start.7) | collective-permute-done | bytes 131104 | tf_op jit(solution)/shard_map/ppermute | solution.py:230
  14.5 2.0 %collective-permute-start.8 = (bf16[256,256]{1,0:T(8,128)(2,1)S(1)}, bf16[256,256]{1,0:T(8,128)(2,1)S(1)}, u32[]{:S(2)}, u32[]{:S(2)}) collective-permute-start(bf16[256,256]{1,0:T(8,128)(2,1)S(1)} %collective-permute-done.7.refs_2_), channel_id=1, source_target_pairs={{0,4},{4,8},{8,12},{12,14},{14,10},{10,6},{6,2},{2,0},{1,5},{5,9},... | collective-permute-start | bytes 393224 | tf_op jit(solution)/shard_map/ppermute | solution.py:230
  16.6 0.7 %gather_near.1.refs_4_ = f32[256,1024]{1,0:T(8,128)S(1)} custom-call(bf16[4096,1024]{1,0:T(8,128)(2,1)S(1)} %get-tuple-element.42.dense, bf16[256,256]{1,0:T(8,128)(2,1)S(1)} %get-tuple-element.44.refs_0_.s0, bf16[256,256]{1,0:T(8,128)(2,1)S(1)} %get-tuple-element.43.refs_1_.s1, bf16[256,256]{1,0:T(8,128)(2,1)S(1)} %collective-permute-done.6.refs_2_, ...), custom_call_target="tpu_custom_call" | custom-call | tf_op jit(solution)/shard_map/gather_near/pallas_call | solution.py:83
  17.3 0.7 %collective-permute-done.1.refs_0_ = bf16[256,256]{1,0:T(8,128)(2,1)S(1)} collective-permute-done((bf16[256,256]{1,0:T(8,128)(2,1)S(1)}, bf16[256,256]{1,0:T(8,128)(2,1)S(1)}, u32[]{:S(2)}, u32[]{:S(2)}) %collective-permute-start.1) | collective-permute-done | bytes 131104 | tf_op jit(solution)/shard_map/ppermute | solution.py:230
  18.0 1.9 %collective-permute-start.2 = (bf16[256,256]{1,0:T(8,128)(2,1)S(1)}, bf16[256,256]{1,0:T(8,128)(2,1)S(1)}, u32[]{:S(2)}, u32[]{:S(2)}) collective-permute-start(bf16[256,256]{1,0:T(8,128)(2,1)S(1)} %collective-permute-done.1.refs_0_), channel_id=1, source_target_pairs={{0,4},{4,8},{8,12},{12,14},{14,10},{10,6},{6,2},{2,0},{1,5},{5,9},... | collective-permute-start | bytes 393224 | tf_op jit(solution)/shard_map/ppermute | solution.py:230
  20.0 0.7 %gather_two.1.refs_4_ = f32[256,1024]{1,0:T(8,128)S(1)} custom-call(bf16[4096,1024]{1,0:T(8,128)(2,1)S(1)} %get-tuple-element.42.dense, bf16[256,256]{1,0:T(8,128)(2,1)S(1)} %collective-permute-done.refs_0_, bf16[256,256]{1,0:T(8,128)(2,1)S(1)} %collective-permute-done.3.refs_1_, bf16[256,256]{1,0:T(8,128)(2,1)S(1)} %collective-permute-done.7.refs_2_, ...), custom_call_target="tpu_custom_call" | custom-call | tf_op jit(solution)/shard_map/gather_two/pallas_call | solution.py:83
  20.8 1.8 %collective-permute-done.11.refs_3_ = bf16[256,256]{1,0:T(8,128)(2,1)S(1)} collective-permute-done((bf16[256,256]{1,0:T(8,128)(2,1)S(1)}, bf16[256,256]{1,0:T(8,128)(2,1)S(1)}, u32[]{:S(2)}, u32[]{:S(2)}) %collective-permute-start.11) | collective-permute-done | bytes 131104 | tf_op jit(solution)/shard_map/ppermute | solution.py:230
  22.7 2.0 %collective-permute-start.13 = (bf16[256,256]{1,0:T(8,128)(2,1)S(1)}, bf16[256,256]{1,0:T(8,128)(2,1)S(1)}, u32[]{:S(2)}, u32[]{:S(2)}) collective-permute-start(bf16[256,256]{1,0:T(8,128)(2,1)S(1)} %collective-permute-done.8.refs_2_), channel_id=1, source_target_pairs={{0,4},{4,8},{8,12},{12,14},{14,10},{10,6},{6,2},{2,0},{1,5},{5,9},... | collective-permute-start | bytes 393224 | tf_op jit(solution)/shard_map/ppermute | solution.py:230
  24.9 0.7 %gather_three.1.part = f32[256,1024]{1,0:T(8,128)S(1)} custom-call(bf16[4096,1024]{1,0:T(8,128)(2,1)S(1)} %get-tuple-element.42.dense, bf16[256,256]{1,0:T(8,128)(2,1)S(1)} %collective-permute-done.1.refs_0_, bf16[256,256]{1,0:T(8,128)(2,1)S(1)} %collective-permute-done.4.refs_1_, bf16[256,256]{1,0:T(8,128)(2,1)S(1)} %collective-permute-done.8.refs_2_, ...), custom_call_target="tpu_custom_call" | custom-call | tf_op jit(solution)/shard_map/gather_three/pallas_call | solution.py:83
  26.0 1.1 %turn.1 = (f32[8,2,64,256]{3,2,1,0:T(8,128)S(1)}, bf16[1024,512]{1,0:T(8,128)(2,1)S(1)}) custom-call(bf16[4096,1024]{1,0:T(8,128)(2,1)S(1)} %get-tuple-element.42.dense, bf16[256,256]{1,0:T(8,128)(2,1)S(1)} %collective-permute-done.2.fa, bf16[256,256]{1,0:T(8,128)(2,1)S(1)} %collective-permute-done.5.ba, f32[256,1024]{1,0:T(8,128)S(1)} %gather_three.1.part, ...), custom_call_target="tpu_custom_call" | custom-call | tf_op jit(solution)/shard_map/turn/pallas_call | solution.py:83
  27.1 0.7 %collective-permute-done.14.ba = bf16[256,256]{1,0:T(8,128)(2,1)S(1)} collective-permute-done((bf16[256,256]{1,0:T(8,128)(2,1)S(1)}, bf16[256,256]{1,0:T(8,128)(2,1)S(1)}, u32[]{:S(2)}, u32[]{:S(2)}) %collective-permute-start.14) | collective-permute-done | bytes 131104 | tf_op jit(solution)/shard_map/ppermute | solution.py:230
  29.0 0.7 %collective-permute-done.15.got.got0 = bf16[512,256]{1,0:T(8,128)(2,1)S(1)} collective-permute-done((bf16[512,256]{1,0:T(8,128)(2,1)S(1)}, bf16[512,256]{1,0:T(8,128)(2,1)S(1)}, u32[]{:S(2)}, u32[]{:S(2)}) %collective-permute-start.15) | collective-permute-done | bytes 262176 | tf_op jit(solution)/shard_map/ppermute | solution.py:337
  30.6 1.9 %collective-permute-start.17 = (bf16[256,256]{1,0:T(8,128)(2,1)S(1)}, bf16[256,256]{1,0:T(8,128)(2,1)S(1)}, u32[]{:S(2)}, u32[]{:S(2)}) collective-permute-start(bf16[256,256]{1,0:T(8,128)(2,1)S(1)} %get-tuple-element.58), channel_id=1, source_target_pairs={{4,0},{8,4},{12,8},{14,12},{10,14},{6,10},{2,6},{0,2},{5,1},{9,5},... | collective-permute-start | bytes 393224 | tf_op jit(solution)/shard_map/ppermute | solution.py:230
  33.2 2.0 %collective-permute-start.20 = (bf16[256,256]{1,0:T(8,128)(2,1)S(1)}, bf16[256,256]{1,0:T(8,128)(2,1)S(1)}, u32[]{:S(2)}, u32[]{:S(2)}) collective-permute-start(bf16[256,256]{1,0:T(8,128)(2,1)S(1)} %get-tuple-element.61), channel_id=1, source_target_pairs={{0,4},{4,8},{8,12},{12,14},{14,10},{10,6},{6,2},{2,0},{1,5},{5,9},... | collective-permute-start | bytes 393224 | tf_op jit(solution)/shard_map/ppermute | solution.py:230
  35.2 0.7 %return_a.1 = (f32[256,256]{1,0:T(8,128)S(1)}, f32[256,256]{1,0:T(8,128)S(1)}, f32[256,256]{1,0:T(8,128)S(1)}, f32[256,256]{1,0:T(8,128)S(1)}) custom-call(bf16[4096,1024]{1,0:T(8,128)(2,1)S(1)} %get-tuple-element.42.dense, bf16[512,256]{1,0:T(8,128)(2,1)S(1)} %mix_back.3.back.refs_0_.back0, bf16[512,256]{1,0:T(8,128)(2,1)S(1)} %mix_back.2.back.refs_1_.back1), custom_call_target="tpu_custom_call" | custom-call | tf_op jit(solution)/shard_map/return_a/pallas_call | solution.py:83
  36.7 2.2 %collective-permute-start.18 = (bf16[256,256]{1,0:T(8,128)(2,1)S(1)}, bf16[256,256]{1,0:T(8,128)(2,1)S(1)}, u32[]{:S(2)}, u32[]{:S(2)}) collective-permute-start(bf16[256,256]{1,0:T(8,128)(2,1)S(1)} %add_convert_fusion.9), channel_id=1, source_target_pairs={{4,0},{8,4},{12,8},{14,12},{10,14},{6,10},{2,6},{0,2},{5,1},{9,5},... | collective-permute-start | bytes 393224 | tf_op jit(solution)/shard_map/ppermute | solution.py:405
  39.1 2.1 %collective-permute-done.20 = bf16[256,256]{1,0:T(8,128)(2,1)S(1)} collective-permute-done((bf16[256,256]{1,0:T(8,128)(2,1)S(1)}, bf16[256,256]{1,0:T(8,128)(2,1)S(1)}, u32[]{:S(2)}, u32[]{:S(2)}) %collective-permute-start.20) | collective-permute-done | bytes 131104 | tf_op jit(solution)/shard_map/ppermute | solution.py:230
  41.6 1.8 %collective-permute-start.29 = (bf16[256,256]{1,0:T(8,128)(2,1)S(1)}, bf16[256,256]{1,0:T(8,128)(2,1)S(1)}, u32[]{:S(2)}, u32[]{:S(2)}) collective-permute-start(bf16[256,256]{1,0:T(8,128)(2,1)S(1)} %add_convert_fusion.1), channel_id=1, source_target_pairs={{4,0},{8,4},{12,8},{14,12},{10,14},{6,10},{2,6},{0,2},{5,1},{9,5},... | collective-permute-start | bytes 393224 | tf_op jit(solution)/shard_map/ppermute | solution.py:405
  44.3 0.9 %collective-permute-done.22 = bf16[256,256]{1,0:T(8,128)(2,1)S(1)} collective-permute-done((bf16[256,256]{1,0:T(8,128)(2,1)S(1)}, bf16[256,256]{1,0:T(8,128)(2,1)S(1)}, u32[]{:S(2)}, u32[]{:S(2)}) %collective-permute-start.22) | collective-permute-done | bytes 131104 | tf_op jit(solution)/shard_map/ppermute | solution.py:405
  45.4 2.1 %collective-permute-start.19 = (bf16[256,256]{1,0:T(8,128)(2,1)S(1)}, bf16[256,256]{1,0:T(8,128)(2,1)S(1)}, u32[]{:S(2)}, u32[]{:S(2)}) collective-permute-start(bf16[256,256]{1,0:T(8,128)(2,1)S(1)} %add_convert_fusion.8), channel_id=1, source_target_pairs={{4,0},{8,4},{12,8},{14,12},{10,14},{6,10},{2,6},{0,2},{5,1},{9,5},... | collective-permute-start | bytes 393224 | tf_op jit(solution)/shard_map/ppermute | solution.py:405
  47.6 2.1 %collective-permute-start.30 = (bf16[256,256]{1,0:T(8,128)(2,1)S(1)}, bf16[256,256]{1,0:T(8,128)(2,1)S(1)}, u32[]{:S(2)}, u32[]{:S(2)}) collective-permute-start(bf16[256,256]{1,0:T(8,128)(2,1)S(1)} %add_convert_fusion), channel_id=1, source_target_pairs={{4,0},{8,4},{12,8},{14,12},{10,14},{6,10},{2,6},{0,2},{5,1},{9,5},... | collective-permute-start | bytes 393224 | tf_op jit(solution)/shard_map/ppermute | solution.py:405
  50.0 1.7 %collective-permute-done.23 = bf16[256,256]{1,0:T(8,128)(2,1)S(1)} collective-permute-done((bf16[256,256]{1,0:T(8,128)(2,1)S(1)}, bf16[256,256]{1,0:T(8,128)(2,1)S(1)}, u32[]{:S(2)}, u32[]{:S(2)}) %collective-permute-start.23) | collective-permute-done | bytes 131104 | tf_op jit(solution)/shard_map/ppermute | solution.py:405
  52.1 1.7 %collective-permute-start.25 = (bf16[256,256]{1,0:T(8,128)(2,1)S(1)}, bf16[256,256]{1,0:T(8,128)(2,1)S(1)}, u32[]{:S(2)}, u32[]{:S(2)}) collective-permute-start(bf16[256,256]{1,0:T(8,128)(2,1)S(1)} %add_convert_fusion.7), channel_id=1, source_target_pairs={{4,0},{8,4},{12,8},{14,12},{10,14},{6,10},{2,6},{0,2},{5,1},{9,5},... | collective-permute-start | bytes 393224 | tf_op jit(solution)/shard_map/ppermute | solution.py:405
  54.3 0.9 %mix_out.1 = bf16[512,256]{1,0:T(8,128)(2,1)} custom-call(f32[512,256]{1,0:T(8,128)S(1)} %get-tuple-element.53.keep.keep0, f32[512,256]{1,0:T(8,128)S(1)} %get-tuple-element.54.keep.keep1, bf16[512,256]{1,0:T(8,128)(2,1)S(1)} %collective-permute-done.15.got.got0, bf16[512,256]{1,0:T(8,128)(2,1)S(1)} %collective-permute-done.16.got.got1, f32[1024,128]{1,0:T(8,128)S(1)} %bitcast.9), custom_call_target="tpu_custom_call" | custom-call | tf_op jit(solution)/shard_map/mix_out/pallas_call | solution.py:83
  55.2 1.5 %collective-permute-done.24.g0 = bf16[256,256]{1,0:T(8,128)(2,1)S(1)} collective-permute-done((bf16[256,256]{1,0:T(8,128)(2,1)S(1)}, bf16[256,256]{1,0:T(8,128)(2,1)S(1)}, u32[]{:S(2)}, u32[]{:S(2)}) %collective-permute-start.24) | collective-permute-done | bytes 131104 | tf_op jit(solution)/shard_map/ppermute | solution.py:405
  57.2 1.0 %finish.1 = bf16[512,256]{1,0:T(8,128)(2,1)} custom-call(f32[256,256]{1,0:T(8,128)S(1)} %get-tuple-element.72.base0, f32[256,256]{1,0:T(8,128)S(1)} %get-tuple-element.73.base1, bf16[256,256]{1,0:T(8,128)(2,1)S(1)} %collective-permute-done.24.g0, bf16[256,256]{1,0:T(8,128)(2,1)S(1)} %collective-permute-done.25.r1, ...), custom_call_target="tpu_custom_call" | custom-call | tf_op jit(solution)/shard_map/finish/pallas_call | solution.py:474
  (63 shorter events, 8.0 us)
Async XLA Ops:
  1.9 7.5 %collective-permute-start.6 = (bf16[256,256]{1,0:T(8,128)(2,1)S(1)}, bf16[256,256]{1,0:T(8,128)(2,1)S(1)}, u32[]{:S(2)}, u32[]{:S(2)}) collective-permute-start(bf16[256,256]{1,0:T(8,128)(2,1)S(1)} %get-tuple-element.44.refs_0_.s0), channel_id=1, source_target_pairs={{0,4},{4,8},{8,12},{12,14},{14,10},{10,6},{6,2},{2,0},{1,5},{5,9},... | collective-permute-start | bytes 393224 | tf_op jit(solution)/shard_map/ppermute | solution.py:230
  5.0 6.5 %collective-permute-start.9 = (bf16[256,256]{1,0:T(8,128)(2,1)S(1)}, bf16[256,256]{1,0:T(8,128)(2,1)S(1)}, u32[]{:S(2)}, u32[]{:S(2)}) collective-permute-start(bf16[256,256]{1,0:T(8,128)(2,1)S(1)} %get-tuple-element.43.refs_1_.s1), channel_id=1, source_target_pairs={{4,0},{8,4},{12,8},{14,12},{10,14},{6,10},{2,6},{0,2},{5,1},{9,5},... | collective-permute-start | bytes 393224 | tf_op jit(solution)/shard_map/ppermute | solution.py:230
  5.0 6.5 %collective-permute-start = (bf16[256,256]{1,0:T(8,128)(2,1)S(1)}, bf16[256,256]{1,0:T(8,128)(2,1)S(1)}, u32[]{:S(2)}, u32[]{:S(2)}) collective-permute-start(bf16[256,256]{1,0:T(8,128)(2,1)S(1)} %get-tuple-element.43.refs_1_.s1), channel_id=1, source_target_pairs={{0,4},{4,8},{8,12},{12,14},{14,10},{10,6},{6,2},{2,0},{1,5},{5,9},... | collective-permute-start | bytes 393224 | tf_op jit(solution)/shard_map/ppermute | solution.py:230
  7.0 6.5 %collective-permute-start.3 = (bf16[256,256]{1,0:T(8,128)(2,1)S(1)}, bf16[256,256]{1,0:T(8,128)(2,1)S(1)}, u32[]{:S(2)}, u32[]{:S(2)}) collective-permute-start(bf16[256,256]{1,0:T(8,128)(2,1)S(1)} %get-tuple-element.44.refs_0_.s0), channel_id=1, source_target_pairs={{4,0},{8,4},{12,8},{14,12},{10,14},{6,10},{2,6},{0,2},{5,1},{9,5},... | collective-permute-start | bytes 393224 | tf_op jit(solution)/shard_map/ppermute | solution.py:230
  9.4 5.0 %collective-permute-start.7 = (bf16[256,256]{1,0:T(8,128)(2,1)S(1)}, bf16[256,256]{1,0:T(8,128)(2,1)S(1)}, u32[]{:S(2)}, u32[]{:S(2)}) collective-permute-start(bf16[256,256]{1,0:T(8,128)(2,1)S(1)} %collective-permute-done.6.refs_2_), channel_id=1, source_target_pairs={{0,4},{4,8},{8,12},{12,14},{14,10},{10,6},{6,2},{2,0},{1,5},{5,9},... | collective-permute-start | bytes 393224 | tf_op jit(solution)/shard_map/ppermute | solution.py:230
  11.5 5.0 %collective-permute-start.10 = (bf16[256,256]{1,0:T(8,128)(2,1)S(1)}, bf16[256,256]{1,0:T(8,128)(2,1)S(1)}, u32[]{:S(2)}, u32[]{:S(2)}) collective-permute-start(bf16[256,256]{1,0:T(8,128)(2,1)S(1)} %collective-permute-done.9.refs_3_), channel_id=1, source_target_pairs={{4,0},{8,4},{12,8},{14,12},{10,14},{6,10},{2,6},{0,2},{5,1},{9,5},... | collective-permute-start | bytes 393224 | tf_op jit(solution)/shard_map/ppermute | solution.py:230
  11.5 13.2 %collective-permute-start.12 = (bf16[528,256]{1,0:T(8,128)(2,1)S(1)}, bf16[528,256]{1,0:T(8,128)(2,1)S(1)}, u32[]{:S(2)}, u32[]{:S(2)}) collective-permute-start(bf16[528,256]{1,0:T(8,128)(2,1)S(1)} %get-tuple-element.48.pack), channel_id=1, source_target_pairs={{0,1},{1,0},{2,3},{3,2},{4,5},{5,4},{6,7},{7,6},{8,9},{9,8},{10,11... | collective-permute-start | bytes 811016 | tf_op jit(solution)/shard_map/ppermute | solution.py:270
  11.6 6.4 %collective-permute-start.1 = (bf16[256,256]{1,0:T(8,128)(2,1)S(1)}, bf16[256,256]{1,0:T(8,128)(2,1)S(1)}, u32[]{:S(2)}, u32[]{:S(2)}) collective-permute-start(bf16[256,256]{1,0:T(8,128)(2,1)S(1)} %collective-permute-done.refs_0_), channel_id=1, source_target_pairs={{0,4},{4,8},{8,12},{12,14},{14,10},{10,6},{6,2},{2,0},{1,5},{5,9},... | collective-permute-start | bytes 393224 | tf_op jit(solution)/shard_map/ppermute | solution.py:230
  13.6 6.3 %collective-permute-start.4 = (bf16[256,256]{1,0:T(8,128)(2,1)S(1)}, bf16[256,256]{1,0:T(8,128)(2,1)S(1)}, u32[]{:S(2)}, u32[]{:S(2)}) collective-permute-start(bf16[256,256]{1,0:T(8,128)(2,1)S(1)} %collective-permute-done.3.refs_1_), channel_id=1, source_target_pairs={{4,0},{8,4},{12,8},{14,12},{10,14},{6,10},{2,6},{0,2},{5,1},{9,5},... | collective-permute-start | bytes 393224 | tf_op jit(solution)/shard_map/ppermute | solution.py:230
  14.5 6.3 %collective-permute-start.8 = (bf16[256,256]{1,0:T(8,128)(2,1)S(1)}, bf16[256,256]{1,0:T(8,128)(2,1)S(1)}, u32[]{:S(2)}, u32[]{:S(2)}) collective-permute-start(bf16[256,256]{1,0:T(8,128)(2,1)S(1)} %collective-permute-done.7.refs_2_), channel_id=1, source_target_pairs={{0,4},{4,8},{8,12},{12,14},{14,10},{10,6},{6,2},{2,0},{1,5},{5,9},... | collective-permute-start | bytes 393224 | tf_op jit(solution)/shard_map/ppermute | solution.py:230
  16.6 6.1 %collective-permute-start.11 = (bf16[256,256]{1,0:T(8,128)(2,1)S(1)}, bf16[256,256]{1,0:T(8,128)(2,1)S(1)}, u32[]{:S(2)}, u32[]{:S(2)}) collective-permute-start(bf16[256,256]{1,0:T(8,128)(2,1)S(1)} %collective-permute-done.10.refs_3_), channel_id=1, source_target_pairs={{4,0},{8,4},{12,8},{14,12},{10,14},{6,10},{2,6},{0,2},{5,1},{9,5},... | collective-permute-start | bytes 393224 | tf_op jit(solution)/shard_map/ppermute | solution.py:230
  18.0 7.7 %collective-permute-start.2 = (bf16[256,256]{1,0:T(8,128)(2,1)S(1)}, bf16[256,256]{1,0:T(8,128)(2,1)S(1)}, u32[]{:S(2)}, u32[]{:S(2)}) collective-permute-start(bf16[256,256]{1,0:T(8,128)(2,1)S(1)} %collective-permute-done.1.refs_0_), channel_id=1, source_target_pairs={{0,4},{4,8},{8,12},{12,14},{14,10},{10,6},{6,2},{2,0},{1,5},{5,9},... | collective-permute-start | bytes 393224 | tf_op jit(solution)/shard_map/ppermute | solution.py:230
  19.9 6.1 %collective-permute-start.5 = (bf16[256,256]{1,0:T(8,128)(2,1)S(1)}, bf16[256,256]{1,0:T(8,128)(2,1)S(1)}, u32[]{:S(2)}, u32[]{:S(2)}) collective-permute-start(bf16[256,256]{1,0:T(8,128)(2,1)S(1)} %collective-permute-done.4.refs_1_), channel_id=1, source_target_pairs={{4,0},{8,4},{12,8},{14,12},{10,14},{6,10},{2,6},{0,2},{5,1},{9,5},... | collective-permute-start | bytes 393224 | tf_op jit(solution)/shard_map/ppermute | solution.py:230
  22.7 5.1 %collective-permute-start.14 = (bf16[256,256]{1,0:T(8,128)(2,1)S(1)}, bf16[256,256]{1,0:T(8,128)(2,1)S(1)}, u32[]{:S(2)}, u32[]{:S(2)}) collective-permute-start(bf16[256,256]{1,0:T(8,128)(2,1)S(1)} %collective-permute-done.11.refs_3_), channel_id=1, source_target_pairs={{4,0},{8,4},{12,8},{14,12},{10,14},{6,10},{2,6},{0,2},{5,1},{9,5},... | collective-permute-start | bytes 393224 | tf_op jit(solution)/shard_map/ppermute | solution.py:230
  22.7 5.0 %collective-permute-start.13 = (bf16[256,256]{1,0:T(8,128)(2,1)S(1)}, bf16[256,256]{1,0:T(8,128)(2,1)S(1)}, u32[]{:S(2)}, u32[]{:S(2)}) collective-permute-start(bf16[256,256]{1,0:T(8,128)(2,1)S(1)} %collective-permute-done.8.refs_2_), channel_id=1, source_target_pairs={{0,4},{4,8},{8,12},{12,14},{14,10},{10,6},{6,2},{2,0},{1,5},{5,9},... | collective-permute-start | bytes 393224 | tf_op jit(solution)/shard_map/ppermute | solution.py:230
  28.0 1.6 %collective-permute-start.15 = (bf16[512,256]{1,0:T(8,128)(2,1)S(1)}, bf16[512,256]{1,0:T(8,128)(2,1)S(1)}, u32[]{:S(2)}, u32[]{:S(2)}) collective-permute-start(bf16[512,256]{1,0:T(8,128)(2,1)S(1)} %get-tuple-element.55), channel_id=1, source_target_pairs={{0,1},{1,0},{2,3},{3,2},{4,5},{5,4},{6,7},{7,6},{8,9},{9,8},{10,11... | collective-permute-start | bytes 786440 | tf_op jit(solution)/shard_map/ppermute | solution.py:337
  28.4 1.7 %collective-permute-start.16 = (bf16[512,256]{1,0:T(8,128)(2,1)S(1)}, bf16[512,256]{1,0:T(8,128)(2,1)S(1)}, u32[]{:S(2)}, u32[]{:S(2)}) collective-permute-start(bf16[512,256]{1,0:T(8,128)(2,1)S(1)} %get-tuple-element.56), channel_id=1, source_target_pairs={{0,1},{1,0},{2,3},{3,2},{4,5},{5,4},{6,7},{7,6},{8,9},{9,8},{10,11... | collective-permute-start | bytes 786440 | tf_op jit(solution)/shard_map/ppermute | solution.py:337
  30.6 6.0 %collective-permute-start.17 = (bf16[256,256]{1,0:T(8,128)(2,1)S(1)}, bf16[256,256]{1,0:T(8,128)(2,1)S(1)}, u32[]{:S(2)}, u32[]{:S(2)}) collective-permute-start(bf16[256,256]{1,0:T(8,128)(2,1)S(1)} %get-tuple-element.58), channel_id=1, source_target_pairs={{4,0},{8,4},{12,8},{14,12},{10,14},{6,10},{2,6},{0,2},{5,1},{9,5},... | collective-permute-start | bytes 393224 | tf_op jit(solution)/shard_map/ppermute | solution.py:230
  32.5 6.4 %collective-permute-start.21 = (bf16[256,256]{1,0:T(8,128)(2,1)S(1)}, bf16[256,256]{1,0:T(8,128)(2,1)S(1)}, u32[]{:S(2)}, u32[]{:S(2)}) collective-permute-start(bf16[256,256]{1,0:T(8,128)(2,1)S(1)} %get-tuple-element.59), channel_id=1, source_target_pairs={{0,4},{4,8},{8,12},{12,14},{14,10},{10,6},{6,2},{2,0},{1,5},{5,9},... | collective-permute-start | bytes 393224 | tf_op jit(solution)/shard_map/ppermute | solution.py:230
  33.2 8.1 %collective-permute-start.20 = (bf16[256,256]{1,0:T(8,128)(2,1)S(1)}, bf16[256,256]{1,0:T(8,128)(2,1)S(1)}, u32[]{:S(2)}, u32[]{:S(2)}) collective-permute-start(bf16[256,256]{1,0:T(8,128)(2,1)S(1)} %get-tuple-element.61), channel_id=1, source_target_pairs={{0,4},{4,8},{8,12},{12,14},{14,10},{10,6},{6,2},{2,0},{1,5},{5,9},... | collective-permute-start | bytes 393224 | tf_op jit(solution)/shard_map/ppermute | solution.py:230
  35.1 6.5 %collective-permute-start.28 = (bf16[256,256]{1,0:T(8,128)(2,1)S(1)}, bf16[256,256]{1,0:T(8,128)(2,1)S(1)}, u32[]{:S(2)}, u32[]{:S(2)}) collective-permute-start(bf16[256,256]{1,0:T(8,128)(2,1)S(1)} %get-tuple-element.78), channel_id=1, source_target_pairs={{4,0},{8,4},{12,8},{14,12},{10,14},{6,10},{2,6},{0,2},{5,1},{9,5},... | collective-permute-start | bytes 393224 | tf_op jit(solution)/shard_map/ppermute | solution.py:230
  36.7 8.7 %collective-permute-start.18 = (bf16[256,256]{1,0:T(8,128)(2,1)S(1)}, bf16[256,256]{1,0:T(8,128)(2,1)S(1)}, u32[]{:S(2)}, u32[]{:S(2)}) collective-permute-start(bf16[256,256]{1,0:T(8,128)(2,1)S(1)} %add_convert_fusion.9), channel_id=1, source_target_pairs={{4,0},{8,4},{12,8},{14,12},{10,14},{6,10},{2,6},{0,2},{5,1},{9,5},... | collective-permute-start | bytes 393224 | tf_op jit(solution)/shard_map/ppermute | solution.py:405
  39.0 6.3 %collective-permute-start.22 = (bf16[256,256]{1,0:T(8,128)(2,1)S(1)}, bf16[256,256]{1,0:T(8,128)(2,1)S(1)}, u32[]{:S(2)}, u32[]{:S(2)}) collective-permute-start(bf16[256,256]{1,0:T(8,128)(2,1)S(1)} %add_convert_fusion.5), channel_id=1, source_target_pairs={{0,4},{4,8},{8,12},{12,14},{14,10},{10,6},{6,2},{2,0},{1,5},{5,9},... | collective-permute-start | bytes 393224 | tf_op jit(solution)/shard_map/ppermute | solution.py:405
  41.3 8.5 %collective-permute-start.26 = (bf16[256,256]{1,0:T(8,128)(2,1)S(1)}, bf16[256,256]{1,0:T(8,128)(2,1)S(1)}, u32[]{:S(2)}, u32[]{:S(2)}) collective-permute-start(bf16[256,256]{1,0:T(8,128)(2,1)S(1)} %add_convert_fusion.6), channel_id=1, source_target_pairs={{0,4},{4,8},{8,12},{12,14},{14,10},{10,6},{6,2},{2,0},{1,5},{5,9},... | collective-permute-start | bytes 393224 | tf_op jit(solution)/shard_map/ppermute | solution.py:405
  41.6 6.0 %collective-permute-start.29 = (bf16[256,256]{1,0:T(8,128)(2,1)S(1)}, bf16[256,256]{1,0:T(8,128)(2,1)S(1)}, u32[]{:S(2)}, u32[]{:S(2)}) collective-permute-start(bf16[256,256]{1,0:T(8,128)(2,1)S(1)} %add_convert_fusion.1), channel_id=1, source_target_pairs={{4,0},{8,4},{12,8},{14,12},{10,14},{6,10},{2,6},{0,2},{5,1},{9,5},... | collective-permute-start | bytes 393224 | tf_op jit(solution)/shard_map/ppermute | solution.py:405
  44.3 12.9 %copy-start = (bf16[256,256]{1,0:T(8,128)(2,1)S(1)}, bf16[256,256]{1,0:T(8,128)(2,1)}, u32[]{:S(2)}) copy-start(bf16[256,256]{1,0:T(8,128)(2,1)} %w.1) | copy-start | bytes 393220
  45.3 6.4 %collective-permute-start.23 = (bf16[256,256]{1,0:T(8,128)(2,1)S(1)}, bf16[256,256]{1,0:T(8,128)(2,1)S(1)}, u32[]{:S(2)}, u32[]{:S(2)}) collective-permute-start(bf16[256,256]{1,0:T(8,128)(2,1)S(1)} %add_convert_fusion.4), channel_id=1, source_target_pairs={{0,4},{4,8},{8,12},{12,14},{14,10},{10,6},{6,2},{2,0},{1,5},{5,9},... | collective-permute-start | bytes 393224 | tf_op jit(solution)/shard_map/ppermute | solution.py:405
  45.4 6.7 %collective-permute-start.19 = (bf16[256,256]{1,0:T(8,128)(2,1)S(1)}, bf16[256,256]{1,0:T(8,128)(2,1)S(1)}, u32[]{:S(2)}, u32[]{:S(2)}) collective-permute-start(bf16[256,256]{1,0:T(8,128)(2,1)S(1)} %add_convert_fusion.8), channel_id=1, source_target_pairs={{4,0},{8,4},{12,8},{14,12},{10,14},{6,10},{2,6},{0,2},{5,1},{9,5},... | collective-permute-start | bytes 393224 | tf_op jit(solution)/shard_map/ppermute | solution.py:405
  47.6 7.6 %collective-permute-start.30 = (bf16[256,256]{1,0:T(8,128)(2,1)S(1)}, bf16[256,256]{1,0:T(8,128)(2,1)S(1)}, u32[]{:S(2)}, u32[]{:S(2)}) collective-permute-start(bf16[256,256]{1,0:T(8,128)(2,1)S(1)} %add_convert_fusion), channel_id=1, source_target_pairs={{4,0},{8,4},{12,8},{14,12},{10,14},{6,10},{2,6},{0,2},{5,1},{9,5},... | collective-permute-start | bytes 393224 | tf_op jit(solution)/shard_map/ppermute | solution.py:405
  49.8 5.4 %collective-permute-start.27 = (bf16[256,256]{1,0:T(8,128)(2,1)S(1)}, bf16[256,256]{1,0:T(8,128)(2,1)S(1)}, u32[]{:S(2)}, u32[]{:S(2)}) collective-permute-start(bf16[256,256]{1,0:T(8,128)(2,1)S(1)} %add_convert_fusion.2), channel_id=1, source_target_pairs={{0,4},{4,8},{8,12},{12,14},{14,10},{10,6},{6,2},{2,0},{1,5},{5,9},... | collective-permute-start | bytes 393224 | tf_op jit(solution)/shard_map/ppermute | solution.py:405
  51.7 5.0 %collective-permute-start.24 = (bf16[256,256]{1,0:T(8,128)(2,1)S(1)}, bf16[256,256]{1,0:T(8,128)(2,1)S(1)}, u32[]{:S(2)}, u32[]{:S(2)}) collective-permute-start(bf16[256,256]{1,0:T(8,128)(2,1)S(1)} %add_convert_fusion.3), channel_id=1, source_target_pairs={{0,4},{4,8},{8,12},{12,14},{14,10},{10,6},{6,2},{2,0},{1,5},{5,9},... | collective-permute-start | bytes 393224 | tf_op jit(solution)/shard_map/ppermute | solution.py:405
  52.1 5.0 %collective-permute-start.25 = (bf16[256,256]{1,0:T(8,128)(2,1)S(1)}, bf16[256,256]{1,0:T(8,128)(2,1)S(1)}, u32[]{:S(2)}, u32[]{:S(2)}) collective-permute-start(bf16[256,256]{1,0:T(8,128)(2,1)S(1)} %add_convert_fusion.7), channel_id=1, source_target_pairs={{4,0},{8,4},{12,8},{14,12},{10,14},{6,10},{2,6},{0,2},{5,1},{9,5},... | collective-permute-start | bytes 393224 | tf_op jit(solution)/shard_map/ppermute | solution.py:405

commit v4 on v3

--- a/solution.py
+++ b/solution.py
@@ -257,7 +257,7 @@
     long.append(shift_pair(long[0]))
     short.append(shift_pair(short[0]))
 
-    long[1] = tuple(after(x, dense) for x in long[1])
+    long[1] = (after(long[1][0], dense), after(long[1][1], dense))
     long.append(shift_pair(long[1]))
     short.append(shift_pair(short[1]))
     long.append(shift_pair(long[2]))
@@ -289,8 +289,9 @@
 
     part = gather([(0, 0, s0), (0, 1, s1)] + long_items(1), None, "gather_near")
     short.append(shift_pair(short[2]))
+    long[3] = (after(long[3][0], part), long[3][1])
     part = gather(short_items(1) + long_items(2), part, "gather_two")
-    long[3] = (after(long[3][0], part), long[3][1])
+    long[3] = (long[3][0], after(long[3][1], part))
     long.append(shift_pair(long[3]))
     part = gather(short_items(2) + long_items(3), after(part, scale_all), "gather_three")
 
@@ -409,12 +410,11 @@
     down = shift_pair(down)
     a0, a1, c0, c1 = chunks([(3, 0), (-3, 1), (2, 1), (-2, 0)], token, "return_a")
     d0, d1 = chunks([(2, 0), (-2, 1)], a0, "return_b")
-    u0 = add(up[0], a0, d0)
+    u0 = (up[0].astype(F32) + a0).astype(BF16)
     e0, e1 = chunks([(1, 1), (-1, 0)], u0, "return_c")
-    u1 = add(up[1], a1, e0)
+    u1 = (up[1].astype(F32) + a1).astype(BF16)
     f0, f1 = chunks([(1, 0), (-1, 1)], u1, "return_d")
-    w0 = add(down[0], c0, f0)
-
+    w0 = (down[0].astype(F32) + c0).astype(BF16)
     def own_base(dense, back0, back1, base0, base1):
         q = lax.axis_index("col")
         for h, (back, base) in enumerate(((back0, base0), (back1, base1))):
@@ -429,15 +429,15 @@
         (dense, after(back[0], w0), back[1]),
         "own_base",
     )
-    w1 = add(down[1], c1, base[0])
+    w1 = (down[1].astype(F32) + c1).astype(BF16)
     u0, u1, w0, w1 = shift(u0, 0), shift(u1, 1), shift(w0, 0), shift(w1, 1)
-    v0 = add(u0, d0, w1)
-    v1 = add(u1, d1, v0)
-    x0 = add(w0, e0, v1)
-    x1 = add(w1, e1, x0)
+    v0 = (u0.astype(F32) + d0).astype(BF16)
+    v1 = (u1.astype(F32) + d1).astype(BF16)
+    x0 = (w0.astype(F32) + e0).astype(BF16)
+    x1 = (w1.astype(F32) + after(e1, x0)).astype(BF16)
     u0, u1, w0, w1 = shift(v0, 0), shift(v1, 1), shift(x0, 0), shift(x1, 1)
-    v0 = add(u0, f0, x1)
-    v1 = add(u1, f1, v0)
+    v0 = (u0.astype(F32) + f0).astype(BF16)
+    v1 = (u1.astype(F32) + f1).astype(BF16)
     up = (shift(v0, 0), shift(v1, 1))
     down = (w0, w1)
 

time: 58.4 us -> 57.8 us (0.990)
    ppermute x9, starting transfers between devices: 17.3 us -> 18.5 us  [shift_pair(): lax.ppermute(pair[0], 'row', fwd)]
    ppermute x9, starting transfers between devices: 2.22 us -> 1 us  [shift_pair(): lax.ppermute(pair[1], 'row', bwd)]
    ppermute x9, waiting for transfers between devices: 3.7 us -> 2.51 us  [shift_pair(): lax.ppermute(pair[0], 'row', fwd)]
    ppermute x10, waiting for transfers between devices: 4.75 us -> 5.72 us  [shift(): return lax.ppermute(x, 'row', (fwd, bwd)[h])]
  transfers between devices with their start and end apart: 31 -> 31, of which waited for: 15 -> 16; matrix products, arithmetic and copies ran while one was open for 0% -> 0% of each run, Pallas kernels for 18% -> 18%
where the time goes in v4:
time: 57.8 us; the launch traced here: 57.6 us
  starting transfers between devices  31.1 us (54%)
  Pallas kernels  13.5 us (23%)
  waiting for transfers between devices  11.9 us (21%)
  between operations  0.88 us (2%)
    ppermute x9, starting transfers between devices, shift_pair(): lax.ppermute(pair[0], 'row', fwd)  18.5 us
    ppermute x10, starting transfers between devices, shift(): return lax.ppermute(x, 'row', (fwd, bwd)[h])  11 us
    pallas_call x19, Pallas kernels, call(): pl.pallas_call(body, out_shape=outs, in_specs=ins, out_specs=jax.tree.map...  10.1 us
    ppermute x10, waiting for transfers between devices, shift(): return lax.ppermute(x, 'row', (fwd, bwd)[h])  5.72 us
    ppermute x9, waiting for transfers between devices, shift_pair(): lax.ppermute(pair[1], 'row', bwd)  2.99 us
    ppermute x9, waiting for transfers between devices, shift_pair(): lax.ppermute(pair[0], 'row', fwd)  2.51 us
    pallas_call x1, Pallas kernels, dense_plan(): pl.pallas_call(densify, out_shape=(pltpu.VMEM((n * rows, span), BF16), ar...  2.38 us
  transfers between devices with their start and end apart: 31, of which 16 were waited for; matrix products, arithmetic and copies ran while one was open for 0% of the time, Pallas kernels for 18%

profile of v4, /device:TPU:0, one launch (start us, length us, event | category | flops | bytes accessed | tf_op | source)
XLA Modules:
  0.0 57.6 jit_solution(6211119388873422818)
XLA Ops:
  0.6 1.3 %project.1 = (bf16[256,256]{1,0:T(8,128)(2,1)S(1)}, bf16[256,256]{1,0:T(8,128)(2,1)S(1)}, f32[512,128]{1,0:T(8,128)S(1)}) custom-call(s32[8,64]{1,0:T(8,128)} %deg_hbm.3, bf16[512,256]{1,0:T(8,128)(2,1)} %bitcast.16, bf16[256,256]{1,0:T(8,128)(2,1)} %w.1), custom_call_target="tpu_custom_call" | custom-call | tf_op jit(solution)/shard_map/project/pallas_call | solution.py:83
  1.9 3.1 %collective-permute-start.6 = (bf16[256,256]{1,0:T(8,128)(2,1)S(1)}, bf16[256,256]{1,0:T(8,128)(2,1)S(1)}, u32[]{:S(2)}, u32[]{:S(2)}) collective-permute-start(bf16[256,256]{1,0:T(8,128)(2,1)S(1)} %get-tuple-element.46.refs_0_.s0), channel_id=1, source_target_pairs={{0,4},{4,8},{8,12},{12,14},{14,10},{10,6},{6,2},{2,0},{1,5},{5,9},... | collective-permute-start | bytes 393224 | tf_op jit(solution)/shard_map/ppermute | solution.py:230
  5.0 2.0 %collective-permute-start = (bf16[256,256]{1,0:T(8,128)(2,1)S(1)}, bf16[256,256]{1,0:T(8,128)(2,1)S(1)}, u32[]{:S(2)}, u32[]{:S(2)}) collective-permute-start(bf16[256,256]{1,0:T(8,128)(2,1)S(1)} %get-tuple-element.45.refs_1_.s1), channel_id=1, source_target_pairs={{0,4},{4,8},{8,12},{12,14},{14,10},{10,6},{6,2},{2,0},{1,5},{5,9},... | collective-permute-start | bytes 393224 | tf_op jit(solution)/shard_map/ppermute | solution.py:230
  7.0 2.4 %densify.1 = (bf16[4096,1024]{1,0:T(8,128)(2,1)S(1)}, bf16[528,256]{1,0:T(8,128)(2,1)S(1)}) custom-call(s32[8,16]{1,0:T(8,128)} %cols_hbm.1, s32[128,64,128]{2,1,0:T(8,128)} %adj_hbm.1, s32[8,64]{1,0:T(8,128)} %deg_hbm.3, bf16[512,256]{1,0:T(8,128)(2,1)} %bitcast.14), custom_call_target="tpu_custom_call" | custom-call | tf_op jit(solution)/shard_map/densify/pallas_call | solution.py:213
  9.4 2.1 %collective-permute-start.7 = (bf16[256,256]{1,0:T(8,128)(2,1)S(1)}, bf16[256,256]{1,0:T(8,128)(2,1)S(1)}, u32[]{:S(2)}, u32[]{:S(2)}) collective-permute-start(bf16[256,256]{1,0:T(8,128)(2,1)S(1)} %collective-permute-done.6.refs_2_), channel_id=1, source_target_pairs={{0,4},{4,8},{8,12},{12,14},{14,10},{10,6},{6,2},{2,0},{1,5},{5,9},... | collective-permute-start | bytes 393224 | tf_op jit(solution)/shard_map/ppermute | solution.py:230
  11.6 2.0 %collective-permute-start.1 = (bf16[256,256]{1,0:T(8,128)(2,1)S(1)}, bf16[256,256]{1,0:T(8,128)(2,1)S(1)}, u32[]{:S(2)}, u32[]{:S(2)}) collective-permute-start(bf16[256,256]{1,0:T(8,128)(2,1)S(1)} %collective-permute-done.refs_0_), channel_id=1, source_target_pairs={{0,4},{4,8},{8,12},{12,14},{14,10},{10,6},{6,2},{2,0},{1,5},{5,9},... | collective-permute-start | bytes 393224 | tf_op jit(solution)/shard_map/ppermute | solution.py:230
  13.6 0.8 %collective-permute-done.7.refs_2_ = bf16[256,256]{1,0:T(8,128)(2,1)S(1)} collective-permute-done((bf16[256,256]{1,0:T(8,128)(2,1)S(1)}, bf16[256,256]{1,0:T(8,128)(2,1)S(1)}, u32[]{:S(2)}, u32[]{:S(2)}) %collective-permute-start.7) | collective-permute-done | bytes 131104 | tf_op jit(solution)/shard_map/ppermute | solution.py:230
  14.5 2.0 %collective-permute-start.8 = (bf16[256,256]{1,0:T(8,128)(2,1)S(1)}, bf16[256,256]{1,0:T(8,128)(2,1)S(1)}, u32[]{:S(2)}, u32[]{:S(2)}) collective-permute-start(bf16[256,256]{1,0:T(8,128)(2,1)S(1)} %collective-permute-done.7.refs_2_), channel_id=1, source_target_pairs={{0,4},{4,8},{8,12},{12,14},{14,10},{10,6},{6,2},{2,0},{1,5},{5,9},... | collective-permute-start | bytes 393224 | tf_op jit(solution)/shard_map/ppermute | solution.py:230
  16.6 0.7 %gather_near.1.refs_4_ = f32[256,1024]{1,0:T(8,128)S(1)} custom-call(bf16[4096,1024]{1,0:T(8,128)(2,1)S(1)} %get-tuple-element.44.dense, bf16[256,256]{1,0:T(8,128)(2,1)S(1)} %get-tuple-element.46.refs_0_.s0, bf16[256,256]{1,0:T(8,128)(2,1)S(1)} %get-tuple-element.45.refs_1_.s1, bf16[256,256]{1,0:T(8,128)(2,1)S(1)} %collective-permute-done.6.refs_2_, ...), custom_call_target="tpu_custom_call" | custom-call | tf_op jit(solution)/shard_map/gather_near/pallas_call | solution.py:83
  17.3 0.7 %collective-permute-done.1.refs_0_ = bf16[256,256]{1,0:T(8,128)(2,1)S(1)} collective-permute-done((bf16[256,256]{1,0:T(8,128)(2,1)S(1)}, bf16[256,256]{1,0:T(8,128)(2,1)S(1)}, u32[]{:S(2)}, u32[]{:S(2)}) %collective-permute-start.1) | collective-permute-done | bytes 131104 | tf_op jit(solution)/shard_map/ppermute | solution.py:230
  18.0 1.9 %collective-permute-start.2 = (bf16[256,256]{1,0:T(8,128)(2,1)S(1)}, bf16[256,256]{1,0:T(8,128)(2,1)S(1)}, u32[]{:S(2)}, u32[]{:S(2)}) collective-permute-start(bf16[256,256]{1,0:T(8,128)(2,1)S(1)} %collective-permute-done.1.refs_0_), channel_id=1, source_target_pairs={{0,4},{4,8},{8,12},{12,14},{14,10},{10,6},{6,2},{2,0},{1,5},{5,9},... | collective-permute-start | bytes 393224 | tf_op jit(solution)/shard_map/ppermute | solution.py:230
  20.0 0.7 %gather_two.1.refs_4_ = f32[256,1024]{1,0:T(8,128)S(1)} custom-call(bf16[4096,1024]{1,0:T(8,128)(2,1)S(1)} %get-tuple-element.44.dense, bf16[256,256]{1,0:T(8,128)(2,1)S(1)} %collective-permute-done.refs_0_, bf16[256,256]{1,0:T(8,128)(2,1)S(1)} %collective-permute-done.3.refs_1_, bf16[256,256]{1,0:T(8,128)(2,1)S(1)} %collective-permute-done.7.refs_2_, ...), custom_call_target="tpu_custom_call" | custom-call | tf_op jit(solution)/shard_map/gather_two/pallas_call | solution.py:83
  20.8 1.9 %collective-permute-start.13 = (bf16[256,256]{1,0:T(8,128)(2,1)S(1)}, bf16[256,256]{1,0:T(8,128)(2,1)S(1)}, u32[]{:S(2)}, u32[]{:S(2)}) collective-permute-start(bf16[256,256]{1,0:T(8,128)(2,1)S(1)} %collective-permute-done.8.refs_2_), channel_id=1, source_target_pairs={{0,4},{4,8},{8,12},{12,14},{14,10},{10,6},{6,2},{2,0},{1,5},{5,9},... | collective-permute-start | bytes 393224 | tf_op jit(solution)/shard_map/ppermute | solution.py:230
  23.1 0.7 %gather_three.1.part = f32[256,1024]{1,0:T(8,128)S(1)} custom-call(bf16[4096,1024]{1,0:T(8,128)(2,1)S(1)} %get-tuple-element.44.dense, bf16[256,256]{1,0:T(8,128)(2,1)S(1)} %collective-permute-done.1.refs_0_, bf16[256,256]{1,0:T(8,128)(2,1)S(1)} %collective-permute-done.4.refs_1_, bf16[256,256]{1,0:T(8,128)(2,1)S(1)} %collective-permute-done.8.refs_2_, ...), custom_call_target="tpu_custom_call" | custom-call | tf_op jit(solution)/shard_map/gather_three/pallas_call | solution.py:83
  23.8 2.0 %collective-permute-done.5.ba = bf16[256,256]{1,0:T(8,128)(2,1)S(1)} collective-permute-done((bf16[256,256]{1,0:T(8,128)(2,1)S(1)}, bf16[256,256]{1,0:T(8,128)(2,1)S(1)}, u32[]{:S(2)}, u32[]{:S(2)}) %collective-permute-start.5) | collective-permute-done | bytes 131104 | tf_op jit(solution)/shard_map/ppermute | solution.py:230
  25.8 1.1 %turn.1 = (f32[8,2,64,256]{3,2,1,0:T(8,128)S(1)}, bf16[1024,512]{1,0:T(8,128)(2,1)S(1)}) custom-call(bf16[4096,1024]{1,0:T(8,128)(2,1)S(1)} %get-tuple-element.44.dense, bf16[256,256]{1,0:T(8,128)(2,1)S(1)} %collective-permute-done.2.fa, bf16[256,256]{1,0:T(8,128)(2,1)S(1)} %collective-permute-done.5.ba, f32[256,1024]{1,0:T(8,128)S(1)} %gather_three.1.part, ...), custom_call_target="tpu_custom_call" | custom-call | tf_op jit(solution)/shard_map/turn/pallas_call | solution.py:83
  26.9 0.8 %collective-permute-done.14.ba = bf16[256,256]{1,0:T(8,128)(2,1)S(1)} collective-permute-done((bf16[256,256]{1,0:T(8,128)(2,1)S(1)}, bf16[256,256]{1,0:T(8,128)(2,1)S(1)}, u32[]{:S(2)}, u32[]{:S(2)}) %collective-permute-start.14) | collective-permute-done | bytes 131104 | tf_op jit(solution)/shard_map/ppermute | solution.py:230
  29.0 0.7 %collective-permute-done.15.got.got0 = bf16[512,256]{1,0:T(8,128)(2,1)S(1)} collective-permute-done((bf16[512,256]{1,0:T(8,128)(2,1)S(1)}, bf16[512,256]{1,0:T(8,128)(2,1)S(1)}, u32[]{:S(2)}, u32[]{:S(2)}) %collective-permute-start.15) | collective-permute-done | bytes 262176 | tf_op jit(solution)/shard_map/ppermute | solution.py:338
  30.9 1.9 %collective-permute-start.21 = (bf16[256,256]{1,0:T(8,128)(2,1)S(1)}, bf16[256,256]{1,0:T(8,128)(2,1)S(1)}, u32[]{:S(2)}, u32[]{:S(2)}) collective-permute-start(bf16[256,256]{1,0:T(8,128)(2,1)S(1)} %get-tuple-element.62), channel_id=1, source_target_pairs={{0,4},{4,8},{8,12},{12,14},{14,10},{10,6},{6,2},{2,0},{1,5},{5,9},... | collective-permute-start | bytes 393224 | tf_op jit(solution)/shard_map/ppermute | solution.py:230
  33.2 1.6 %collective-permute-start.20 = (bf16[256,256]{1,0:T(8,128)(2,1)S(1)}, bf16[256,256]{1,0:T(8,128)(2,1)S(1)}, u32[]{:S(2)}, u32[]{:S(2)}) collective-permute-start(bf16[256,256]{1,0:T(8,128)(2,1)S(1)} %get-tuple-element.64), channel_id=1, source_target_pairs={{0,4},{4,8},{8,12},{12,14},{14,10},{10,6},{6,2},{2,0},{1,5},{5,9},... | collective-permute-start | bytes 393224 | tf_op jit(solution)/shard_map/ppermute | solution.py:230
  35.2 0.7 %return_a.1 = (f32[256,256]{1,0:T(8,128)S(1)}, f32[256,256]{1,0:T(8,128)S(1)}, f32[256,256]{1,0:T(8,128)S(1)}, f32[256,256]{1,0:T(8,128)S(1)}) custom-call(bf16[4096,1024]{1,0:T(8,128)(2,1)S(1)} %get-tuple-element.44.dense, bf16[512,256]{1,0:T(8,128)(2,1)S(1)} %mix_back.3.back.refs_0_.back0, bf16[512,256]{1,0:T(8,128)(2,1)S(1)} %mix_back.2.back.refs_1_.back1), custom_call_target="tpu_custom_call" | custom-call | tf_op jit(solution)/shard_map/return_a/pallas_call | solution.py:83
  37.2 1.9 %collective-permute-start.22 = (bf16[256,256]{1,0:T(8,128)(2,1)S(1)}, bf16[256,256]{1,0:T(8,128)(2,1)S(1)}, u32[]{:S(2)}, u32[]{:S(2)}) collective-permute-start(bf16[256,256]{1,0:T(8,128)(2,1)S(1)} %add_convert_fusion.5), channel_id=1, source_target_pairs={{0,4},{4,8},{8,12},{12,14},{14,10},{10,6},{6,2},{2,0},{1,5},{5,9},... | collective-permute-start | bytes 393224 | tf_op jit(solution)/shard_map/ppermute | solution.py:406
  39.7 1.8 %collective-permute-start.26 = (bf16[256,256]{1,0:T(8,128)(2,1)S(1)}, bf16[256,256]{1,0:T(8,128)(2,1)S(1)}, u32[]{:S(2)}, u32[]{:S(2)}) collective-permute-start(bf16[256,256]{1,0:T(8,128)(2,1)S(1)} %add_convert_fusion.6), channel_id=1, source_target_pairs={{0,4},{4,8},{8,12},{12,14},{14,10},{10,6},{6,2},{2,0},{1,5},{5,9},... | collective-permute-start | bytes 393224 | tf_op jit(solution)/shard_map/ppermute | solution.py:406
  43.2 2.2 %collective-permute-start.23 = (bf16[256,256]{1,0:T(8,128)(2,1)S(1)}, bf16[256,256]{1,0:T(8,128)(2,1)S(1)}, u32[]{:S(2)}, u32[]{:S(2)}) collective-permute-start(bf16[256,256]{1,0:T(8,128)(2,1)S(1)} %add_convert_fusion.4), channel_id=1, source_target_pairs={{0,4},{4,8},{8,12},{12,14},{14,10},{10,6},{6,2},{2,0},{1,5},{5,9},... | collective-permute-start | bytes 393224 | tf_op jit(solution)/shard_map/ppermute | solution.py:406
  46.2 2.0 %collective-permute-start.27 = (bf16[256,256]{1,0:T(8,128)(2,1)S(1)}, bf16[256,256]{1,0:T(8,128)(2,1)S(1)}, u32[]{:S(2)}, u32[]{:S(2)}) collective-permute-start(bf16[256,256]{1,0:T(8,128)(2,1)S(1)} %add_convert_fusion.2), channel_id=1, source_target_pairs={{0,4},{4,8},{8,12},{12,14},{14,10},{10,6},{6,2},{2,0},{1,5},{5,9},... | collective-permute-start | bytes 393224 | tf_op jit(solution)/shard_map/ppermute | solution.py:406
  48.4 1.3 %collective-permute-done.23 = bf16[256,256]{1,0:T(8,128)(2,1)S(1)} collective-permute-done((bf16[256,256]{1,0:T(8,128)(2,1)S(1)}, bf16[256,256]{1,0:T(8,128)(2,1)S(1)}, u32[]{:S(2)}, u32[]{:S(2)}) %collective-permute-start.23) | collective-permute-done | bytes 131104 | tf_op jit(solution)/shard_map/ppermute | solution.py:406
  49.7 1.8 %collective-permute-start.24 = (bf16[256,256]{1,0:T(8,128)(2,1)S(1)}, bf16[256,256]{1,0:T(8,128)(2,1)S(1)}, u32[]{:S(2)}, u32[]{:S(2)}) collective-permute-start(bf16[256,256]{1,0:T(8,128)(2,1)S(1)} %add_convert_fusion.3), channel_id=1, source_target_pairs={{0,4},{4,8},{8,12},{12,14},{14,10},{10,6},{6,2},{2,0},{1,5},{5,9},... | collective-permute-start | bytes 393224 | tf_op jit(solution)/shard_map/ppermute | solution.py:406
  52.3 0.9 %mix_out.1 = bf16[512,256]{1,0:T(8,128)(2,1)} custom-call(f32[512,256]{1,0:T(8,128)S(1)} %get-tuple-element.56.keep.keep0, f32[512,256]{1,0:T(8,128)S(1)} %get-tuple-element.57.keep.keep1, bf16[512,256]{1,0:T(8,128)(2,1)S(1)} %collective-permute-done.15.got.got0, bf16[512,256]{1,0:T(8,128)(2,1)S(1)} %collective-permute-done.16.got.got1, f32[1024,128]{1,0:T(8,128)S(1)} %bitcast.9), custom_call_target="tpu_custom_call" | custom-call | tf_op jit(solution)/shard_map/mix_out/pallas_call | solution.py:83
  53.2 0.7 %collective-permute-done.30.r0 = bf16[256,256]{1,0:T(8,128)(2,1)S(1)} collective-permute-done((bf16[256,256]{1,0:T(8,128)(2,1)S(1)}, bf16[256,256]{1,0:T(8,128)(2,1)S(1)}, u32[]{:S(2)}, u32[]{:S(2)}) %collective-permute-start.30) | collective-permute-done | bytes 131104 | tf_op jit(solution)/shard_map/ppermute | solution.py:406
  54.0 0.8 %collective-permute-done.24.g0 = bf16[256,256]{1,0:T(8,128)(2,1)S(1)} collective-permute-done((bf16[256,256]{1,0:T(8,128)(2,1)S(1)}, bf16[256,256]{1,0:T(8,128)(2,1)S(1)}, u32[]{:S(2)}, u32[]{:S(2)}) %collective-permute-start.24) | collective-permute-done | bytes 131104 | tf_op jit(solution)/shard_map/ppermute | solution.py:406
  54.7 1.9 %collective-permute-done.25.r1 = bf16[256,256]{1,0:T(8,128)(2,1)S(1)} collective-permute-done((bf16[256,256]{1,0:T(8,128)(2,1)S(1)}, bf16[256,256]{1,0:T(8,128)(2,1)S(1)}, u32[]{:S(2)}, u32[]{:S(2)}) %collective-permute-start.25) | collective-permute-done | bytes 131104 | tf_op jit(solution)/shard_map/ppermute | solution.py:406
  56.6 1.0 %finish.1 = bf16[512,256]{1,0:T(8,128)(2,1)} custom-call(f32[256,256]{1,0:T(8,128)S(1)} %get-tuple-element.75.base0, f32[256,256]{1,0:T(8,128)S(1)} %get-tuple-element.76.base1, bf16[256,256]{1,0:T(8,128)(2,1)S(1)} %collective-permute-done.24.g0, bf16[256,256]{1,0:T(8,128)(2,1)S(1)} %collective-permute-done.25.r1, ...), custom_call_target="tpu_custom_call" | custom-call | tf_op jit(solution)/shard_map/finish/pallas_call | solution.py:474
  (63 shorter events, 9.2 us)
Async XLA Ops:
  1.9 7.5 %collective-permute-start.6 = (bf16[256,256]{1,0:T(8,128)(2,1)S(1)}, bf16[256,256]{1,0:T(8,128)(2,1)S(1)}, u32[]{:S(2)}, u32[]{:S(2)}) collective-permute-start(bf16[256,256]{1,0:T(8,128)(2,1)S(1)} %get-tuple-element.46.refs_0_.s0), channel_id=1, source_target_pairs={{0,4},{4,8},{8,12},{12,14},{14,10},{10,6},{6,2},{2,0},{1,5},{5,9},... | collective-permute-start | bytes 393224 | tf_op jit(solution)/shard_map/ppermute | solution.py:230
  5.0 6.5 %collective-permute-start.9 = (bf16[256,256]{1,0:T(8,128)(2,1)S(1)}, bf16[256,256]{1,0:T(8,128)(2,1)S(1)}, u32[]{:S(2)}, u32[]{:S(2)}) collective-permute-start(bf16[256,256]{1,0:T(8,128)(2,1)S(1)} %get-tuple-element.45.refs_1_.s1), channel_id=1, source_target_pairs={{4,0},{8,4},{12,8},{14,12},{10,14},{6,10},{2,6},{0,2},{5,1},{9,5},... | collective-permute-start | bytes 393224 | tf_op jit(solution)/shard_map/ppermute | solution.py:230
  5.0 6.5 %collective-permute-start = (bf16[256,256]{1,0:T(8,128)(2,1)S(1)}, bf16[256,256]{1,0:T(8,128)(2,1)S(1)}, u32[]{:S(2)}, u32[]{:S(2)}) collective-permute-start(bf16[256,256]{1,0:T(8,128)(2,1)S(1)} %get-tuple-element.45.refs_1_.s1), channel_id=1, source_target_pairs={{0,4},{4,8},{8,12},{12,14},{14,10},{10,6},{6,2},{2,0},{1,5},{5,9},... | collective-permute-start | bytes 393224 | tf_op jit(solution)/shard_map/ppermute | solution.py:230
  7.0 6.5 %collective-permute-start.3 = (bf16[256,256]{1,0:T(8,128)(2,1)S(1)}, bf16[256,256]{1,0:T(8,128)(2,1)S(1)}, u32[]{:S(2)}, u32[]{:S(2)}) collective-permute-start(bf16[256,256]{1,0:T(8,128)(2,1)S(1)} %get-tuple-element.46.refs_0_.s0), channel_id=1, source_target_pairs={{4,0},{8,4},{12,8},{14,12},{10,14},{6,10},{2,6},{0,2},{5,1},{9,5},... | collective-permute-start | bytes 393224 | tf_op jit(solution)/shard_map/ppermute | solution.py:230
  9.4 5.0 %collective-permute-start.7 = (bf16[256,256]{1,0:T(8,128)(2,1)S(1)}, bf16[256,256]{1,0:T(8,128)(2,1)S(1)}, u32[]{:S(2)}, u32[]{:S(2)}) collective-permute-start(bf16[256,256]{1,0:T(8,128)(2,1)S(1)} %collective-permute-done.6.refs_2_), channel_id=1, source_target_pairs={{0,4},{4,8},{8,12},{12,14},{14,10},{10,6},{6,2},{2,0},{1,5},{5,9},... | collective-permute-start | bytes 393224 | tf_op jit(solution)/shard_map/ppermute | solution.py:230
  11.5 5.0 %collective-permute-start.10 = (bf16[256,256]{1,0:T(8,128)(2,1)S(1)}, bf16[256,256]{1,0:T(8,128)(2,1)S(1)}, u32[]{:S(2)}, u32[]{:S(2)}) collective-permute-start(bf16[256,256]{1,0:T(8,128)(2,1)S(1)} %collective-permute-done.9.refs_3_), channel_id=1, source_target_pairs={{4,0},{8,4},{12,8},{14,12},{10,14},{6,10},{2,6},{0,2},{5,1},{9,5},... | collective-permute-start | bytes 393224 | tf_op jit(solution)/shard_map/ppermute | solution.py:230
  11.5 11.3 %collective-permute-start.12 = (bf16[528,256]{1,0:T(8,128)(2,1)S(1)}, bf16[528,256]{1,0:T(8,128)(2,1)S(1)}, u32[]{:S(2)}, u32[]{:S(2)}) collective-permute-start(bf16[528,256]{1,0:T(8,128)(2,1)S(1)} %get-tuple-element.51.pack), channel_id=1, source_target_pairs={{0,1},{1,0},{2,3},{3,2},{4,5},{5,4},{6,7},{7,6},{8,9},{9,8},{10,11... | collective-permute-start | bytes 811016 | tf_op jit(solution)/shard_map/ppermute | solution.py:270
  11.6 6.4 %collective-permute-start.1 = (bf16[256,256]{1,0:T(8,128)(2,1)S(1)}, bf16[256,256]{1,0:T(8,128)(2,1)S(1)}, u32[]{:S(2)}, u32[]{:S(2)}) collective-permute-start(bf16[256,256]{1,0:T(8,128)(2,1)S(1)} %collective-permute-done.refs_0_), channel_id=1, source_target_pairs={{0,4},{4,8},{8,12},{12,14},{14,10},{10,6},{6,2},{2,0},{1,5},{5,9},... | collective-permute-start | bytes 393224 | tf_op jit(solution)/shard_map/ppermute | solution.py:230
  13.6 6.3 %collective-permute-start.4 = (bf16[256,256]{1,0:T(8,128)(2,1)S(1)}, bf16[256,256]{1,0:T(8,128)(2,1)S(1)}, u32[]{:S(2)}, u32[]{:S(2)}) collective-permute-start(bf16[256,256]{1,0:T(8,128)(2,1)S(1)} %collective-permute-done.3.refs_1_), channel_id=1, source_target_pairs={{4,0},{8,4},{12,8},{14,12},{10,14},{6,10},{2,6},{0,2},{5,1},{9,5},... | collective-permute-start | bytes 393224 | tf_op jit(solution)/shard_map/ppermute | solution.py:230
  14.5 6.3 %collective-permute-start.8 = (bf16[256,256]{1,0:T(8,128)(2,1)S(1)}, bf16[256,256]{1,0:T(8,128)(2,1)S(1)}, u32[]{:S(2)}, u32[]{:S(2)}) collective-permute-start(bf16[256,256]{1,0:T(8,128)(2,1)S(1)} %collective-permute-done.7.refs_2_), channel_id=1, source_target_pairs={{0,4},{4,8},{8,12},{12,14},{14,10},{10,6},{6,2},{2,0},{1,5},{5,9},... | collective-permute-start | bytes 393224 | tf_op jit(solution)/shard_map/ppermute | solution.py:230
  16.6 6.2 %collective-permute-start.11 = (bf16[256,256]{1,0:T(8,128)(2,1)S(1)}, bf16[256,256]{1,0:T(8,128)(2,1)S(1)}, u32[]{:S(2)}, u32[]{:S(2)}) collective-permute-start(bf16[256,256]{1,0:T(8,128)(2,1)S(1)} %collective-permute-done.10.refs_3_), channel_id=1, source_target_pairs={{4,0},{8,4},{12,8},{14,12},{10,14},{6,10},{2,6},{0,2},{5,1},{9,5},... | collective-permute-start | bytes 393224 | tf_op jit(solution)/shard_map/ppermute | solution.py:230
  18.0 5.8 %collective-permute-start.2 = (bf16[256,256]{1,0:T(8,128)(2,1)S(1)}, bf16[256,256]{1,0:T(8,128)(2,1)S(1)}, u32[]{:S(2)}, u32[]{:S(2)}) collective-permute-start(bf16[256,256]{1,0:T(8,128)(2,1)S(1)} %collective-permute-done.1.refs_0_), channel_id=1, source_target_pairs={{0,4},{4,8},{8,12},{12,14},{14,10},{10,6},{6,2},{2,0},{1,5},{5,9},... | collective-permute-start | bytes 393224 | tf_op jit(solution)/shard_map/ppermute | solution.py:230
  19.9 5.9 %collective-permute-start.5 = (bf16[256,256]{1,0:T(8,128)(2,1)S(1)}, bf16[256,256]{1,0:T(8,128)(2,1)S(1)}, u32[]{:S(2)}, u32[]{:S(2)}) collective-permute-start(bf16[256,256]{1,0:T(8,128)(2,1)S(1)} %collective-permute-done.4.refs_1_), channel_id=1, source_target_pairs={{4,0},{8,4},{12,8},{14,12},{10,14},{6,10},{2,6},{0,2},{5,1},{9,5},... | collective-permute-start | bytes 393224 | tf_op jit(solution)/shard_map/ppermute | solution.py:230
  20.8 6.1 %collective-permute-start.13 = (bf16[256,256]{1,0:T(8,128)(2,1)S(1)}, bf16[256,256]{1,0:T(8,128)(2,1)S(1)}, u32[]{:S(2)}, u32[]{:S(2)}) collective-permute-start(bf16[256,256]{1,0:T(8,128)(2,1)S(1)} %collective-permute-done.8.refs_2_), channel_id=1, source_target_pairs={{0,4},{4,8},{8,12},{12,14},{14,10},{10,6},{6,2},{2,0},{1,5},{5,9},... | collective-permute-start | bytes 393224 | tf_op jit(solution)/shard_map/ppermute | solution.py:230
  22.7 5.0 %collective-permute-start.14 = (bf16[256,256]{1,0:T(8,128)(2,1)S(1)}, bf16[256,256]{1,0:T(8,128)(2,1)S(1)}, u32[]{:S(2)}, u32[]{:S(2)}) collective-permute-start(bf16[256,256]{1,0:T(8,128)(2,1)S(1)} %collective-permute-done.11.refs_3_), channel_id=1, source_target_pairs={{4,0},{8,4},{12,8},{14,12},{10,14},{6,10},{2,6},{0,2},{5,1},{9,5},... | collective-permute-start | bytes 393224 | tf_op jit(solution)/shard_map/ppermute | solution.py:230
  28.0 1.6 %collective-permute-start.15 = (bf16[512,256]{1,0:T(8,128)(2,1)S(1)}, bf16[512,256]{1,0:T(8,128)(2,1)S(1)}, u32[]{:S(2)}, u32[]{:S(2)}) collective-permute-start(bf16[512,256]{1,0:T(8,128)(2,1)S(1)} %get-tuple-element.58), channel_id=1, source_target_pairs={{0,1},{1,0},{2,3},{3,2},{4,5},{5,4},{6,7},{7,6},{8,9},{9,8},{10,11... | collective-permute-start | bytes 786440 | tf_op jit(solution)/shard_map/ppermute | solution.py:338
  28.4 1.7 %collective-permute-start.16 = (bf16[512,256]{1,0:T(8,128)(2,1)S(1)}, bf16[512,256]{1,0:T(8,128)(2,1)S(1)}, u32[]{:S(2)}, u32[]{:S(2)}) collective-permute-start(bf16[512,256]{1,0:T(8,128)(2,1)S(1)} %get-tuple-element.59), channel_id=1, source_target_pairs={{0,1},{1,0},{2,3},{3,2},{4,5},{5,4},{6,7},{7,6},{8,9},{9,8},{10,11... | collective-permute-start | bytes 786440 | tf_op jit(solution)/shard_map/ppermute | solution.py:338
  30.6 5.8 %collective-permute-start.17 = (bf16[256,256]{1,0:T(8,128)(2,1)S(1)}, bf16[256,256]{1,0:T(8,128)(2,1)S(1)}, u32[]{:S(2)}, u32[]{:S(2)}) collective-permute-start(bf16[256,256]{1,0:T(8,128)(2,1)S(1)} %get-tuple-element.61), channel_id=1, source_target_pairs={{4,0},{8,4},{12,8},{14,12},{10,14},{6,10},{2,6},{0,2},{5,1},{9,5},... | collective-permute-start | bytes 393224 | tf_op jit(solution)/shard_map/ppermute | solution.py:230
  30.9 6.3 %collective-permute-start.21 = (bf16[256,256]{1,0:T(8,128)(2,1)S(1)}, bf16[256,256]{1,0:T(8,128)(2,1)S(1)}, u32[]{:S(2)}, u32[]{:S(2)}) collective-permute-start(bf16[256,256]{1,0:T(8,128)(2,1)S(1)} %get-tuple-element.62), channel_id=1, source_target_pairs={{0,4},{4,8},{8,12},{12,14},{14,10},{10,6},{6,2},{2,0},{1,5},{5,9},... | collective-permute-start | bytes 393224 | tf_op jit(solution)/shard_map/ppermute | solution.py:230
  33.2 6.5 %collective-permute-start.20 = (bf16[256,256]{1,0:T(8,128)(2,1)S(1)}, bf16[256,256]{1,0:T(8,128)(2,1)S(1)}, u32[]{:S(2)}, u32[]{:S(2)}) collective-permute-start(bf16[256,256]{1,0:T(8,128)(2,1)S(1)} %get-tuple-element.64), channel_id=1, source_target_pairs={{0,4},{4,8},{8,12},{12,14},{14,10},{10,6},{6,2},{2,0},{1,5},{5,9},... | collective-permute-start | bytes 393224 | tf_op jit(solution)/shard_map/ppermute | solution.py:230
  34.8 6.7 %collective-permute-start.28 = (bf16[256,256]{1,0:T(8,128)(2,1)S(1)}, bf16[256,256]{1,0:T(8,128)(2,1)S(1)}, u32[]{:S(2)}, u32[]{:S(2)}) collective-permute-start(bf16[256,256]{1,0:T(8,128)(2,1)S(1)} %get-tuple-element.81), channel_id=1, source_target_pairs={{4,0},{8,4},{12,8},{14,12},{10,14},{6,10},{2,6},{0,2},{5,1},{9,5},... | collective-permute-start | bytes 393224 | tf_op jit(solution)/shard_map/ppermute | solution.py:230
  36.5 8.9 %collective-permute-start.18 = (bf16[256,256]{1,0:T(8,128)(2,1)S(1)}, bf16[256,256]{1,0:T(8,128)(2,1)S(1)}, u32[]{:S(2)}, u32[]{:S(2)}) collective-permute-start(bf16[256,256]{1,0:T(8,128)(2,1)S(1)} %add_convert_fusion.9), channel_id=1, source_target_pairs={{4,0},{8,4},{12,8},{14,12},{10,14},{6,10},{2,6},{0,2},{5,1},{9,5},... | collective-permute-start | bytes 393224 | tf_op jit(solution)/shard_map/ppermute | solution.py:406
  37.2 5.9 %collective-permute-start.22 = (bf16[256,256]{1,0:T(8,128)(2,1)S(1)}, bf16[256,256]{1,0:T(8,128)(2,1)S(1)}, u32[]{:S(2)}, u32[]{:S(2)}) collective-permute-start(bf16[256,256]{1,0:T(8,128)(2,1)S(1)} %add_convert_fusion.5), channel_id=1, source_target_pairs={{0,4},{4,8},{8,12},{12,14},{14,10},{10,6},{6,2},{2,0},{1,5},{5,9},... | collective-permute-start | bytes 393224 | tf_op jit(solution)/shard_map/ppermute | solution.py:406
  39.7 6.4 %collective-permute-start.26 = (bf16[256,256]{1,0:T(8,128)(2,1)S(1)}, bf16[256,256]{1,0:T(8,128)(2,1)S(1)}, u32[]{:S(2)}, u32[]{:S(2)}) collective-permute-start(bf16[256,256]{1,0:T(8,128)(2,1)S(1)} %add_convert_fusion.6), channel_id=1, source_target_pairs={{0,4},{4,8},{8,12},{12,14},{14,10},{10,6},{6,2},{2,0},{1,5},{5,9},... | collective-permute-start | bytes 393224 | tf_op jit(solution)/shard_map/ppermute | solution.py:406
  41.6 6.7 %collective-permute-start.29 = (bf16[256,256]{1,0:T(8,128)(2,1)S(1)}, bf16[256,256]{1,0:T(8,128)(2,1)S(1)}, u32[]{:S(2)}, u32[]{:S(2)}) collective-permute-start(bf16[256,256]{1,0:T(8,128)(2,1)S(1)} %add_convert_fusion.1), channel_id=1, source_target_pairs={{4,0},{8,4},{12,8},{14,12},{10,14},{6,10},{2,6},{0,2},{5,1},{9,5},... | collective-permute-start | bytes 393224 | tf_op jit(solution)/shard_map/ppermute | solution.py:406
  42.8 13.9 %copy-start = (bf16[256,256]{1,0:T(8,128)(2,1)S(1)}, bf16[256,256]{1,0:T(8,128)(2,1)}, u32[]{:S(2)}) copy-start(bf16[256,256]{1,0:T(8,128)(2,1)} %w.1) | copy-start | bytes 393220
  43.2 6.5 %collective-permute-start.23 = (bf16[256,256]{1,0:T(8,128)(2,1)S(1)}, bf16[256,256]{1,0:T(8,128)(2,1)S(1)}, u32[]{:S(2)}, u32[]{:S(2)}) collective-permute-start(bf16[256,256]{1,0:T(8,128)(2,1)S(1)} %add_convert_fusion.4), channel_id=1, source_target_pairs={{0,4},{4,8},{8,12},{12,14},{14,10},{10,6},{6,2},{2,0},{1,5},{5,9},... | collective-permute-start | bytes 393224 | tf_op jit(solution)/shard_map/ppermute | solution.py:406
  45.4 6.1 %collective-permute-start.19 = (bf16[256,256]{1,0:T(8,128)(2,1)S(1)}, bf16[256,256]{1,0:T(8,128)(2,1)S(1)}, u32[]{:S(2)}, u32[]{:S(2)}) collective-permute-start(bf16[256,256]{1,0:T(8,128)(2,1)S(1)} %add_convert_fusion.8), channel_id=1, source_target_pairs={{4,0},{8,4},{12,8},{14,12},{10,14},{6,10},{2,6},{0,2},{5,1},{9,5},... | collective-permute-start | bytes 393224 | tf_op jit(solution)/shard_map/ppermute | solution.py:406
  46.2 7.8 %collective-permute-start.27 = (bf16[256,256]{1,0:T(8,128)(2,1)S(1)}, bf16[256,256]{1,0:T(8,128)(2,1)S(1)}, u32[]{:S(2)}, u32[]{:S(2)}) collective-permute-start(bf16[256,256]{1,0:T(8,128)(2,1)S(1)} %add_convert_fusion.2), channel_id=1, source_target_pairs={{0,4},{4,8},{8,12},{12,14},{14,10},{10,6},{6,2},{2,0},{1,5},{5,9},... | collective-permute-start | bytes 393224 | tf_op jit(solution)/shard_map/ppermute | solution.py:406
  48.3 5.7 %collective-permute-start.30 = (bf16[256,256]{1,0:T(8,128)(2,1)S(1)}, bf16[256,256]{1,0:T(8,128)(2,1)S(1)}, u32[]{:S(2)}, u32[]{:S(2)}) collective-permute-start(bf16[256,256]{1,0:T(8,128)(2,1)S(1)} %add_convert_fusion), channel_id=1, source_target_pairs={{4,0},{8,4},{12,8},{14,12},{10,14},{6,10},{2,6},{0,2},{5,1},{9,5},... | collective-permute-start | bytes 393224 | tf_op jit(solution)/shard_map/ppermute | solution.py:406
  49.7 5.0 %collective-permute-start.24 = (bf16[256,256]{1,0:T(8,128)(2,1)S(1)}, bf16[256,256]{1,0:T(8,128)(2,1)S(1)}, u32[]{:S(2)}, u32[]{:S(2)}) collective-permute-start(bf16[256,256]{1,0:T(8,128)(2,1)S(1)} %add_convert_fusion.3), channel_id=1, source_target_pairs={{0,4},{4,8},{8,12},{12,14},{14,10},{10,6},{6,2},{2,0},{1,5},{5,9},... | collective-permute-start | bytes 393224 | tf_op jit(solution)/shard_map/ppermute | solution.py:406
  51.6 5.0 %collective-permute-start.25 = (bf16[256,256]{1,0:T(8,128)(2,1)S(1)}, bf16[256,256]{1,0:T(8,128)(2,1)S(1)}, u32[]{:S(2)}, u32[]{:S(2)}) collective-permute-start(bf16[256,256]{1,0:T(8,128)(2,1)S(1)} %add_convert_fusion.7), channel_id=1, source_target_pairs={{4,0},{8,4},{12,8},{14,12},{10,14},{6,10},{2,6},{0,2},{5,1},{9,5},... | collective-permute-start | bytes 393224 | tf_op jit(solution)/shard_map/ppermute | solution.py:406

commit v5 on v4

--- a/solution.py
+++ b/solution.py
@@ -337,45 +337,44 @@
         keep.append(kept)
         got.append(lax.ppermute(give, "col", OTHER))
 
-    def mix_back(k, keep, got, scale, scaled, back):
+    def back_of(k, keep, got, scale, scaled):
         at = node_piece(k)
         mixed = over(scale[at, :]) * (keep[...] + got[...].astype(F32))
         sig = jax.nn.sigmoid(mixed)
         slope = sig * (1.0 + mixed * (1.0 - sig))
-        back[...] = (scaled[at, :] * slope).astype(BF16)
-
-    far_rows = lambda dense, k: dense[pl.ds(half_rows_of(far, 0).start, rows), node_piece(k)]
-
-    def far_first(dense, back, out):
-        out[...] = jnp.dot(far_rows(dense, 0), back[...], preferred_element_type=F32)
-
-    def far_second(dense, back, part, c0, c1):
-        out = part[...] + jnp.dot(far_rows(dense, 1), back[...], preferred_element_type=F32)
+        return (scaled[at, :] * slope).astype(BF16)
+
+    def far_term(k, dense, back):
+        at = pl.ds(half_rows_of(far, 0).start, rows)
+        return jnp.dot(dense[at, node_piece(k)], back, preferred_element_type=F32)
+
+    def mix_first(keep, got, scale, scaled, dense, back, far_part):
+        value = back_of(0, keep, got, scale, scaled)
+        back[...] = value
+        far_part[...] = far_term(0, dense, value)
+
+    def mix_second(keep, got, scale, scaled, dense, far_part, back, c0, c1):
+        value = back_of(1, keep, got, scale, scaled)
+        back[...] = value
+        out = far_part[...] + far_term(1, dense, value)
         c0[...] = out[:hrows].astype(BF16)
         c1[...] = out[hrows:].astype(BF16)
 
-    back = []
-    for k in range(2):
-        back.append(
-            call(
-                functools.partial(mix_back, k),
-                array(shape, BF16),
-                [VM] * 4,
-                (keep[k], got[k], scale_all, scaled_cot),
-                "mix_back",
-            )
-        )
-        if k == 0:
-            far_part = call(
-                far_first, array(shape, F32), [VM] * 2, (dense, back[0]), "return_far_first"
-            )
-    up = call(
-        far_second,
-        (array(hshape, BF16), array(hshape, BF16)),
-        [VM] * 3,
-        (dense, back[1], far_part),
-        "return_far",
-    )
+    back0, far_part = call(
+        mix_first,
+        (array(shape, BF16), array(shape, F32)),
+        [VM] * 5,
+        (keep[0], got[0], scale_all, scaled_cot, dense),
+        "mix_first",
+    )
+    back1, *up = call(
+        mix_second,
+        (array(shape, BF16), array(hshape, BF16), array(hshape, BF16)),
+        [VM] * 6,
+        (keep[1], got[1], scale_all, scaled_cot, dense, far_part),
+        "mix_second",
+    )
+    back = [back0, back1]
     token = up[0]
     up = shift_pair(up)
 
@@ -408,13 +407,10 @@
     down = chunks([(far - 1, 1), (1 - far, 0)], token, "return_next", BF16)
     token = down[0]
     down = shift_pair(down)
-    a0, a1, c0, c1 = chunks([(3, 0), (-3, 1), (2, 1), (-2, 0)], token, "return_a")
-    d0, d1 = chunks([(2, 0), (-2, 1)], a0, "return_b")
+    a0, a1, c0, c1, d0, d1 = chunks([(3, 0), (-3, 1), (2, 1), (-2, 0), (2, 0), (-2, 1)], token, "return_ab")
     u0 = (up[0].astype(F32) + a0).astype(BF16)
-    e0, e1 = chunks([(1, 1), (-1, 0)], u0, "return_c")
     u1 = (up[1].astype(F32) + a1).astype(BF16)
-    f0, f1 = chunks([(1, 0), (-1, 1)], u1, "return_d")
-    w0 = (down[0].astype(F32) + c0).astype(BF16)
+    w0 = (down[0].astype(F32) + after(c0, u0, u1)).astype(BF16)
     def own_base(dense, back0, back1, base0, base1):
         q = lax.axis_index("col")
         for h, (back, base) in enumerate(((back0, base0), (back1, base1))):
@@ -433,7 +429,9 @@
     u0, u1, w0, w1 = shift(u0, 0), shift(u1, 1), shift(w0, 0), shift(w1, 1)
     v0 = (u0.astype(F32) + d0).astype(BF16)
     v1 = (u1.astype(F32) + d1).astype(BF16)
+    e0, e1 = chunks([(1, 1), (-1, 0)], v0, "return_c")
     x0 = (w0.astype(F32) + e0).astype(BF16)
+    f0, f1 = chunks([(1, 0), (-1, 1)], v1, "return_d")
     x1 = (w1.astype(F32) + after(e1, x0)).astype(BF16)
     u0, u1, w0, w1 = shift(v0, 0), shift(v1, 1), shift(x0, 0), shift(x1, 1)
     v0 = (u0.astype(F32) + f0).astype(BF16)

time: 57.8 us -> 57.8 us (level)
    pallas_call x19 -> x16, Pallas kernels: 10.1 us -> 9.89 us  [call(): pl.pallas_call(body, out_shape=outs, in_specs=ins, out_specs=jax.tree.map...]
  transfers between devices with their start and end apart: 31 -> 31, of which waited for: 16 -> 15; matrix products, arithmetic and copies ran while one was open for 0% -> 0% of each run, Pallas kernels for 18% -> 18%
where the time goes in v5:
time: 57.8 us; the launch traced here: 57.6 us
  starting transfers between devices  31.5 us (54%)
  Pallas kernels  13.3 us (23%)
  waiting for transfers between devices  11.6 us (20%)
  between operations  0.88 us (2%)
    ppermute x9, starting transfers between devices, shift_pair(): lax.ppermute(pair[0], 'row', fwd)  18.5 us
    ppermute x10, starting transfers between devices, shift(): return lax.ppermute(x, 'row', (fwd, bwd)[h])  11.4 us
    pallas_call x16, Pallas kernels, call(): pl.pallas_call(body, out_shape=outs, in_specs=ins, out_specs=jax.tree.map...  9.89 us
    ppermute x10, waiting for transfers between devices, shift(): return lax.ppermute(x, 'row', (fwd, bwd)[h])  5.26 us
    ppermute x9, waiting for transfers between devices, shift_pair(): lax.ppermute(pair[1], 'row', bwd)  3.16 us
    ppermute x9, waiting for transfers between devices, shift_pair(): lax.ppermute(pair[0], 'row', fwd)  2.5 us
    pallas_call x1, Pallas kernels, dense_plan(): pl.pallas_call(densify, out_shape=(pltpu.VMEM((n * rows, span), BF16), ar...  2.38 us
  transfers between devices with their start and end apart: 31, of which 15 were waited for; matrix products, arithmetic and copies ran while one was open for 0% of the time, Pallas kernels for 18%

profile of v5, /device:TPU:0, one launch (start us, length us, event | category | flops | bytes accessed | tf_op | source)
XLA Modules:
  0.0 57.6 jit_solution(3997755961071408356)
XLA Ops:
  0.6 1.3 %project.1 = (bf16[256,256]{1,0:T(8,128)(2,1)S(1)}, bf16[256,256]{1,0:T(8,128)(2,1)S(1)}, f32[512,128]{1,0:T(8,128)S(1)}) custom-call(s32[8,64]{1,0:T(8,128)} %deg_hbm.3, bf16[512,256]{1,0:T(8,128)(2,1)} %bitcast.16, bf16[256,256]{1,0:T(8,128)(2,1)} %w.1), custom_call_target="tpu_custom_call" | custom-call | tf_op jit(solution)/shard_map/project/pallas_call | solution.py:83
  1.9 3.1 %collective-permute-start.6 = (bf16[256,256]{1,0:T(8,128)(2,1)S(1)}, bf16[256,256]{1,0:T(8,128)(2,1)S(1)}, u32[]{:S(2)}, u32[]{:S(2)}) collective-permute-start(bf16[256,256]{1,0:T(8,128)(2,1)S(1)} %get-tuple-element.49.refs_0_.s0), channel_id=1, source_target_pairs={{0,4},{4,8},{8,12},{12,14},{14,10},{10,6},{6,2},{2,0},{1,5},{5,9},... | collective-permute-start | bytes 393224 | tf_op jit(solution)/shard_map/ppermute | solution.py:230
  5.0 2.0 %collective-permute-start = (bf16[256,256]{1,0:T(8,128)(2,1)S(1)}, bf16[256,256]{1,0:T(8,128)(2,1)S(1)}, u32[]{:S(2)}, u32[]{:S(2)}) collective-permute-start(bf16[256,256]{1,0:T(8,128)(2,1)S(1)} %get-tuple-element.48.refs_1_.s1), channel_id=1, source_target_pairs={{0,4},{4,8},{8,12},{12,14},{14,10},{10,6},{6,2},{2,0},{1,5},{5,9},... | collective-permute-start | bytes 393224 | tf_op jit(solution)/shard_map/ppermute | solution.py:230
  7.0 2.4 %densify.1 = (bf16[4096,1024]{1,0:T(8,128)(2,1)S(1)}, bf16[528,256]{1,0:T(8,128)(2,1)S(1)}) custom-call(s32[8,16]{1,0:T(8,128)} %cols_hbm.1, s32[128,64,128]{2,1,0:T(8,128)} %adj_hbm.1, s32[8,64]{1,0:T(8,128)} %deg_hbm.3, bf16[512,256]{1,0:T(8,128)(2,1)} %bitcast.14), custom_call_target="tpu_custom_call" | custom-call | tf_op jit(solution)/shard_map/densify/pallas_call | solution.py:213
  9.4 2.1 %collective-permute-start.7 = (bf16[256,256]{1,0:T(8,128)(2,1)S(1)}, bf16[256,256]{1,0:T(8,128)(2,1)S(1)}, u32[]{:S(2)}, u32[]{:S(2)}) collective-permute-start(bf16[256,256]{1,0:T(8,128)(2,1)S(1)} %collective-permute-done.6.refs_2_), channel_id=1, source_target_pairs={{0,4},{4,8},{8,12},{12,14},{14,10},{10,6},{6,2},{2,0},{1,5},{5,9},... | collective-permute-start | bytes 393224 | tf_op jit(solution)/shard_map/ppermute | solution.py:230
  11.5 2.0 %collective-permute-start.1 = (bf16[256,256]{1,0:T(8,128)(2,1)S(1)}, bf16[256,256]{1,0:T(8,128)(2,1)S(1)}, u32[]{:S(2)}, u32[]{:S(2)}) collective-permute-start(bf16[256,256]{1,0:T(8,128)(2,1)S(1)} %collective-permute-done.refs_0_), channel_id=1, source_target_pairs={{0,4},{4,8},{8,12},{12,14},{14,10},{10,6},{6,2},{2,0},{1,5},{5,9},... | collective-permute-start | bytes 393224 | tf_op jit(solution)/shard_map/ppermute | solution.py:230
  13.6 0.8 %collective-permute-done.7.refs_2_ = bf16[256,256]{1,0:T(8,128)(2,1)S(1)} collective-permute-done((bf16[256,256]{1,0:T(8,128)(2,1)S(1)}, bf16[256,256]{1,0:T(8,128)(2,1)S(1)}, u32[]{:S(2)}, u32[]{:S(2)}) %collective-permute-start.7) | collective-permute-done | bytes 131104 | tf_op jit(solution)/shard_map/ppermute | solution.py:230
  14.5 2.0 %collective-permute-start.8 = (bf16[256,256]{1,0:T(8,128)(2,1)S(1)}, bf16[256,256]{1,0:T(8,128)(2,1)S(1)}, u32[]{:S(2)}, u32[]{:S(2)}) collective-permute-start(bf16[256,256]{1,0:T(8,128)(2,1)S(1)} %collective-permute-done.7.refs_2_), channel_id=1, source_target_pairs={{0,4},{4,8},{8,12},{12,14},{14,10},{10,6},{6,2},{2,0},{1,5},{5,9},... | collective-permute-start | bytes 393224 | tf_op jit(solution)/shard_map/ppermute | solution.py:230
  16.6 0.7 %gather_near.1.refs_4_ = f32[256,1024]{1,0:T(8,128)S(1)} custom-call(bf16[4096,1024]{1,0:T(8,128)(2,1)S(1)} %get-tuple-element.47.dense, bf16[256,256]{1,0:T(8,128)(2,1)S(1)} %get-tuple-element.49.refs_0_.s0, bf16[256,256]{1,0:T(8,128)(2,1)S(1)} %get-tuple-element.48.refs_1_.s1, bf16[256,256]{1,0:T(8,128)(2,1)S(1)} %collective-permute-done.6.refs_2_, ...), custom_call_target="tpu_custom_call" | custom-call | tf_op jit(solution)/shard_map/gather_near/pallas_call | solution.py:83
  17.3 0.7 %collective-permute-done.1.refs_0_ = bf16[256,256]{1,0:T(8,128)(2,1)S(1)} collective-permute-done((bf16[256,256]{1,0:T(8,128)(2,1)S(1)}, bf16[256,256]{1,0:T(8,128)(2,1)S(1)}, u32[]{:S(2)}, u32[]{:S(2)}) %collective-permute-start.1) | collective-permute-done | bytes 131104 | tf_op jit(solution)/shard_map/ppermute | solution.py:230
  18.0 1.9 %collective-permute-start.2 = (bf16[256,256]{1,0:T(8,128)(2,1)S(1)}, bf16[256,256]{1,0:T(8,128)(2,1)S(1)}, u32[]{:S(2)}, u32[]{:S(2)}) collective-permute-start(bf16[256,256]{1,0:T(8,128)(2,1)S(1)} %collective-permute-done.1.refs_0_), channel_id=1, source_target_pairs={{0,4},{4,8},{8,12},{12,14},{14,10},{10,6},{6,2},{2,0},{1,5},{5,9},... | collective-permute-start | bytes 393224 | tf_op jit(solution)/shard_map/ppermute | solution.py:230
  20.0 0.7 %gather_two.1.refs_4_ = f32[256,1024]{1,0:T(8,128)S(1)} custom-call(bf16[4096,1024]{1,0:T(8,128)(2,1)S(1)} %get-tuple-element.47.dense, bf16[256,256]{1,0:T(8,128)(2,1)S(1)} %collective-permute-done.refs_0_, bf16[256,256]{1,0:T(8,128)(2,1)S(1)} %collective-permute-done.3.refs_1_, bf16[256,256]{1,0:T(8,128)(2,1)S(1)} %collective-permute-done.7.refs_2_, ...), custom_call_target="tpu_custom_call" | custom-call | tf_op jit(solution)/shard_map/gather_two/pallas_call | solution.py:83
  20.8 1.9 %collective-permute-start.13 = (bf16[256,256]{1,0:T(8,128)(2,1)S(1)}, bf16[256,256]{1,0:T(8,128)(2,1)S(1)}, u32[]{:S(2)}, u32[]{:S(2)}) collective-permute-start(bf16[256,256]{1,0:T(8,128)(2,1)S(1)} %collective-permute-done.8.refs_2_), channel_id=1, source_target_pairs={{0,4},{4,8},{8,12},{12,14},{14,10},{10,6},{6,2},{2,0},{1,5},{5,9},... | collective-permute-start | bytes 393224 | tf_op jit(solution)/shard_map/ppermute | solution.py:230
  23.1 0.7 %gather_three.1.part = f32[256,1024]{1,0:T(8,128)S(1)} custom-call(bf16[4096,1024]{1,0:T(8,128)(2,1)S(1)} %get-tuple-element.47.dense, bf16[256,256]{1,0:T(8,128)(2,1)S(1)} %collective-permute-done.1.refs_0_, bf16[256,256]{1,0:T(8,128)(2,1)S(1)} %collective-permute-done.4.refs_1_, bf16[256,256]{1,0:T(8,128)(2,1)S(1)} %collective-permute-done.8.refs_2_, ...), custom_call_target="tpu_custom_call" | custom-call | tf_op jit(solution)/shard_map/gather_three/pallas_call | solution.py:83
  23.8 2.0 %collective-permute-done.5.ba = bf16[256,256]{1,0:T(8,128)(2,1)S(1)} collective-permute-done((bf16[256,256]{1,0:T(8,128)(2,1)S(1)}, bf16[256,256]{1,0:T(8,128)(2,1)S(1)}, u32[]{:S(2)}, u32[]{:S(2)}) %collective-permute-start.5) | collective-permute-done | bytes 131104 | tf_op jit(solution)/shard_map/ppermute | solution.py:230
  25.8 1.1 %turn.1 = (f32[8,2,64,256]{3,2,1,0:T(8,128)S(1)}, bf16[1024,512]{1,0:T(8,128)(2,1)S(1)}) custom-call(bf16[4096,1024]{1,0:T(8,128)(2,1)S(1)} %get-tuple-element.47.dense, bf16[256,256]{1,0:T(8,128)(2,1)S(1)} %collective-permute-done.2.fa, bf16[256,256]{1,0:T(8,128)(2,1)S(1)} %collective-permute-done.5.ba, f32[256,1024]{1,0:T(8,128)S(1)} %gather_three.1.part, ...), custom_call_target="tpu_custom_call" | custom-call | tf_op jit(solution)/shard_map/turn/pallas_call | solution.py:83
  26.9 0.8 %collective-permute-done.14.ba = bf16[256,256]{1,0:T(8,128)(2,1)S(1)} collective-permute-done((bf16[256,256]{1,0:T(8,128)(2,1)S(1)}, bf16[256,256]{1,0:T(8,128)(2,1)S(1)}, u32[]{:S(2)}, u32[]{:S(2)}) %collective-permute-start.14) | collective-permute-done | bytes 131104 | tf_op jit(solution)/shard_map/ppermute | solution.py:230
  30.8 1.9 %collective-permute-start.21 = (bf16[256,256]{1,0:T(8,128)(2,1)S(1)}, bf16[256,256]{1,0:T(8,128)(2,1)S(1)}, u32[]{:S(2)}, u32[]{:S(2)}) collective-permute-start(bf16[256,256]{1,0:T(8,128)(2,1)S(1)} %get-tuple-element.67), channel_id=1, source_target_pairs={{0,4},{4,8},{8,12},{12,14},{14,10},{10,6},{6,2},{2,0},{1,5},{5,9},... | collective-permute-start | bytes 393224 | tf_op jit(solution)/shard_map/ppermute | solution.py:230
  33.1 1.6 %collective-permute-start.20 = (bf16[256,256]{1,0:T(8,128)(2,1)S(1)}, bf16[256,256]{1,0:T(8,128)(2,1)S(1)}, u32[]{:S(2)}, u32[]{:S(2)}) collective-permute-start(bf16[256,256]{1,0:T(8,128)(2,1)S(1)} %get-tuple-element.70), channel_id=1, source_target_pairs={{0,4},{4,8},{8,12},{12,14},{14,10},{10,6},{6,2},{2,0},{1,5},{5,9},... | collective-permute-start | bytes 393224 | tf_op jit(solution)/shard_map/ppermute | solution.py:230
  35.2 1.0 %return_ab.1 = (f32[256,256]{1,0:T(8,128)S(1)}, f32[256,256]{1,0:T(8,128)S(1)}, f32[256,256]{1,0:T(8,128)S(1)}, f32[256,256]{1,0:T(8,128)S(1)}, f32[256,256]{1,0:T(8,128)S(1)}, /*index=5*/f32[256,256]{1,0:T(8,128)S(1)}) custom-call(bf16[4096,1024]{1,0:T(8,128)(2,1)S(1)} %get-tuple-element.47.dense, bf16[512,256]{1,0:T(8,128)(2,1)S(1)} %get-tuple-element.85.refs_0_.back0, ...), custom_call_target="tpu_custom_call" | custom-call | tf_op jit(solution)/shard_map/return_ab/pallas_call | solution.py:83
  37.2 1.9 %collective-permute-start.22 = (bf16[256,256]{1,0:T(8,128)(2,1)S(1)}, bf16[256,256]{1,0:T(8,128)(2,1)S(1)}, u32[]{:S(2)}, u32[]{:S(2)}) collective-permute-start(bf16[256,256]{1,0:T(8,128)(2,1)S(1)} %add_convert_fusion.6), channel_id=1, source_target_pairs={{0,4},{4,8},{8,12},{12,14},{14,10},{10,6},{6,2},{2,0},{1,5},{5,9},... | collective-permute-start | bytes 393224 | tf_op jit(solution)/shard_map/ppermute | solution.py:405
  39.7 1.8 %collective-permute-start.26 = (bf16[256,256]{1,0:T(8,128)(2,1)S(1)}, bf16[256,256]{1,0:T(8,128)(2,1)S(1)}, u32[]{:S(2)}, u32[]{:S(2)}) collective-permute-start(bf16[256,256]{1,0:T(8,128)(2,1)S(1)} %add_convert_fusion.5), channel_id=1, source_target_pairs={{0,4},{4,8},{8,12},{12,14},{14,10},{10,6},{6,2},{2,0},{1,5},{5,9},... | collective-permute-start | bytes 393224 | tf_op jit(solution)/shard_map/ppermute | solution.py:405
  41.9 0.7 %collective-permute-done.18 = bf16[256,256]{1,0:T(8,128)(2,1)S(1)} collective-permute-done((bf16[256,256]{1,0:T(8,128)(2,1)S(1)}, bf16[256,256]{1,0:T(8,128)(2,1)S(1)}, u32[]{:S(2)}, u32[]{:S(2)}) %collective-permute-start.18) | collective-permute-done | bytes 131104 | tf_op jit(solution)/shard_map/ppermute | solution.py:405
  42.6 1.0 %collective-permute-start.19 = (bf16[256,256]{1,0:T(8,128)(2,1)S(1)}, bf16[256,256]{1,0:T(8,128)(2,1)S(1)}, u32[]{:S(2)}, u32[]{:S(2)}) collective-permute-start(bf16[256,256]{1,0:T(8,128)(2,1)S(1)} %add_convert_fusion.8), channel_id=1, source_target_pairs={{4,0},{8,4},{12,8},{14,12},{10,14},{6,10},{2,6},{0,2},{5,1},{9,5},... | collective-permute-start | bytes 393224 | tf_op jit(solution)/shard_map/ppermute | solution.py:405
  43.6 1.8 %collective-permute-start.23 = (bf16[256,256]{1,0:T(8,128)(2,1)S(1)}, bf16[256,256]{1,0:T(8,128)(2,1)S(1)}, u32[]{:S(2)}, u32[]{:S(2)}) collective-permute-start(bf16[256,256]{1,0:T(8,128)(2,1)S(1)} %add_convert_fusion.4), channel_id=1, source_target_pairs={{0,4},{4,8},{8,12},{12,14},{14,10},{10,6},{6,2},{2,0},{1,5},{5,9},... | collective-permute-start | bytes 393224 | tf_op jit(solution)/shard_map/ppermute | solution.py:405
  45.9 1.9 %collective-permute-start.27 = (bf16[256,256]{1,0:T(8,128)(2,1)S(1)}, bf16[256,256]{1,0:T(8,128)(2,1)S(1)}, u32[]{:S(2)}, u32[]{:S(2)}) collective-permute-start(bf16[256,256]{1,0:T(8,128)(2,1)S(1)} %add_convert_fusion.2), channel_id=1, source_target_pairs={{0,4},{4,8},{8,12},{12,14},{14,10},{10,6},{6,2},{2,0},{1,5},{5,9},... | collective-permute-start | bytes 393224 | tf_op jit(solution)/shard_map/ppermute | solution.py:405
  48.5 1.1 %collective-permute-done.23 = bf16[256,256]{1,0:T(8,128)(2,1)S(1)} collective-permute-done((bf16[256,256]{1,0:T(8,128)(2,1)S(1)}, bf16[256,256]{1,0:T(8,128)(2,1)S(1)}, u32[]{:S(2)}, u32[]{:S(2)}) %collective-permute-start.23) | collective-permute-done | bytes 131104 | tf_op jit(solution)/shard_map/ppermute | solution.py:405
  49.6 1.9 %collective-permute-start.24 = (bf16[256,256]{1,0:T(8,128)(2,1)S(1)}, bf16[256,256]{1,0:T(8,128)(2,1)S(1)}, u32[]{:S(2)}, u32[]{:S(2)}) collective-permute-start(bf16[256,256]{1,0:T(8,128)(2,1)S(1)} %add_convert_fusion.3), channel_id=1, source_target_pairs={{0,4},{4,8},{8,12},{12,14},{14,10},{10,6},{6,2},{2,0},{1,5},{5,9},... | collective-permute-start | bytes 393224 | tf_op jit(solution)/shard_map/ppermute | solution.py:405
  52.2 0.9 %mix_out.1 = bf16[512,256]{1,0:T(8,128)(2,1)} custom-call(f32[512,256]{1,0:T(8,128)S(1)} %get-tuple-element.59.keep.keep0, f32[512,256]{1,0:T(8,128)S(1)} %get-tuple-element.60.keep.keep1, bf16[512,256]{1,0:T(8,128)(2,1)S(1)} %collective-permute-done.15.got.got0, bf16[512,256]{1,0:T(8,128)(2,1)S(1)} %collective-permute-done.16.got.got1, f32[1024,128]{1,0:T(8,128)S(1)} %bitcast.9), custom_call_target="tpu_custom_call" | custom-call | tf_op jit(solution)/shard_map/mix_out/pallas_call | solution.py:83
  53.7 0.9 %collective-permute-done.24.g0 = bf16[256,256]{1,0:T(8,128)(2,1)S(1)} collective-permute-done((bf16[256,256]{1,0:T(8,128)(2,1)S(1)}, bf16[256,256]{1,0:T(8,128)(2,1)S(1)}, u32[]{:S(2)}, u32[]{:S(2)}) %collective-permute-start.24) | collective-permute-done | bytes 131104 | tf_op jit(solution)/shard_map/ppermute | solution.py:405
  54.6 2.0 %collective-permute-done.25.r1 = bf16[256,256]{1,0:T(8,128)(2,1)S(1)} collective-permute-done((bf16[256,256]{1,0:T(8,128)(2,1)S(1)}, bf16[256,256]{1,0:T(8,128)(2,1)S(1)}, u32[]{:S(2)}, u32[]{:S(2)}) %collective-permute-start.25) | collective-permute-done | bytes 131104 | tf_op jit(solution)/shard_map/ppermute | solution.py:405
  56.6 1.0 %finish.1 = bf16[512,256]{1,0:T(8,128)(2,1)} custom-call(f32[256,256]{1,0:T(8,128)S(1)} %get-tuple-element.81.base0, f32[256,256]{1,0:T(8,128)S(1)} %get-tuple-element.82.base1, bf16[256,256]{1,0:T(8,128)(2,1)S(1)} %collective-permute-done.24.g0, bf16[256,256]{1,0:T(8,128)(2,1)S(1)} %collective-permute-done.25.r1, ...), custom_call_target="tpu_custom_call" | custom-call | tf_op jit(solution)/shard_map/finish/pallas_call | solution.py:472
  (60 shorter events, 9.2 us)
Async XLA Ops:
  1.9 7.5 %collective-permute-start.6 = (bf16[256,256]{1,0:T(8,128)(2,1)S(1)}, bf16[256,256]{1,0:T(8,128)(2,1)S(1)}, u32[]{:S(2)}, u32[]{:S(2)}) collective-permute-start(bf16[256,256]{1,0:T(8,128)(2,1)S(1)} %get-tuple-element.49.refs_0_.s0), channel_id=1, source_target_pairs={{0,4},{4,8},{8,12},{12,14},{14,10},{10,6},{6,2},{2,0},{1,5},{5,9},... | collective-permute-start | bytes 393224 | tf_op jit(solution)/shard_map/ppermute | solution.py:230
  5.0 6.5 %collective-permute-start.9 = (bf16[256,256]{1,0:T(8,128)(2,1)S(1)}, bf16[256,256]{1,0:T(8,128)(2,1)S(1)}, u32[]{:S(2)}, u32[]{:S(2)}) collective-permute-start(bf16[256,256]{1,0:T(8,128)(2,1)S(1)} %get-tuple-element.48.refs_1_.s1), channel_id=1, source_target_pairs={{4,0},{8,4},{12,8},{14,12},{10,14},{6,10},{2,6},{0,2},{5,1},{9,5},... | collective-permute-start | bytes 393224 | tf_op jit(solution)/shard_map/ppermute | solution.py:230
  5.0 6.5 %collective-permute-start = (bf16[256,256]{1,0:T(8,128)(2,1)S(1)}, bf16[256,256]{1,0:T(8,128)(2,1)S(1)}, u32[]{:S(2)}, u32[]{:S(2)}) collective-permute-start(bf16[256,256]{1,0:T(8,128)(2,1)S(1)} %get-tuple-element.48.refs_1_.s1), channel_id=1, source_target_pairs={{0,4},{4,8},{8,12},{12,14},{14,10},{10,6},{6,2},{2,0},{1,5},{5,9},... | collective-permute-start | bytes 393224 | tf_op jit(solution)/shard_map/ppermute | solution.py:230
  7.0 6.5 %collective-permute-start.3 = (bf16[256,256]{1,0:T(8,128)(2,1)S(1)}, bf16[256,256]{1,0:T(8,128)(2,1)S(1)}, u32[]{:S(2)}, u32[]{:S(2)}) collective-permute-start(bf16[256,256]{1,0:T(8,128)(2,1)S(1)} %get-tuple-element.49.refs_0_.s0), channel_id=1, source_target_pairs={{4,0},{8,4},{12,8},{14,12},{10,14},{6,10},{2,6},{0,2},{5,1},{9,5},... | collective-permute-start | bytes 393224 | tf_op jit(solution)/shard_map/ppermute | solution.py:230
  9.4 5.0 %collective-permute-start.7 = (bf16[256,256]{1,0:T(8,128)(2,1)S(1)}, bf16[256,256]{1,0:T(8,128)(2,1)S(1)}, u32[]{:S(2)}, u32[]{:S(2)}) collective-permute-start(bf16[256,256]{1,0:T(8,128)(2,1)S(1)} %collective-permute-done.6.refs_2_), channel_id=1, source_target_pairs={{0,4},{4,8},{8,12},{12,14},{14,10},{10,6},{6,2},{2,0},{1,5},{5,9},... | collective-permute-start | bytes 393224 | tf_op jit(solution)/shard_map/ppermute | solution.py:230
  11.5 5.0 %collective-permute-start.10 = (bf16[256,256]{1,0:T(8,128)(2,1)S(1)}, bf16[256,256]{1,0:T(8,128)(2,1)S(1)}, u32[]{:S(2)}, u32[]{:S(2)}) collective-permute-start(bf16[256,256]{1,0:T(8,128)(2,1)S(1)} %collective-permute-done.9.refs_3_), channel_id=1, source_target_pairs={{4,0},{8,4},{12,8},{14,12},{10,14},{6,10},{2,6},{0,2},{5,1},{9,5},... | collective-permute-start | bytes 393224 | tf_op jit(solution)/shard_map/ppermute | solution.py:230
  11.5 11.3 %collective-permute-start.12 = (bf16[528,256]{1,0:T(8,128)(2,1)S(1)}, bf16[528,256]{1,0:T(8,128)(2,1)S(1)}, u32[]{:S(2)}, u32[]{:S(2)}) collective-permute-start(bf16[528,256]{1,0:T(8,128)(2,1)S(1)} %get-tuple-element.54.pack), channel_id=1, source_target_pairs={{0,1},{1,0},{2,3},{3,2},{4,5},{5,4},{6,7},{7,6},{8,9},{9,8},{10,11... | collective-permute-start | bytes 811016 | tf_op jit(solution)/shard_map/ppermute | solution.py:270
  11.5 6.4 %collective-permute-start.1 = (bf16[256,256]{1,0:T(8,128)(2,1)S(1)}, bf16[256,256]{1,0:T(8,128)(2,1)S(1)}, u32[]{:S(2)}, u32[]{:S(2)}) collective-permute-start(bf16[256,256]{1,0:T(8,128)(2,1)S(1)} %collective-permute-done.refs_0_), channel_id=1, source_target_pairs={{0,4},{4,8},{8,12},{12,14},{14,10},{10,6},{6,2},{2,0},{1,5},{5,9},... | collective-permute-start | bytes 393224 | tf_op jit(solution)/shard_map/ppermute | solution.py:230
  13.6 6.3 %collective-permute-start.4 = (bf16[256,256]{1,0:T(8,128)(2,1)S(1)}, bf16[256,256]{1,0:T(8,128)(2,1)S(1)}, u32[]{:S(2)}, u32[]{:S(2)}) collective-permute-start(bf16[256,256]{1,0:T(8,128)(2,1)S(1)} %collective-permute-done.3.refs_1_), channel_id=1, source_target_pairs={{4,0},{8,4},{12,8},{14,12},{10,14},{6,10},{2,6},{0,2},{5,1},{9,5},... | collective-permute-start | bytes 393224 | tf_op jit(solution)/shard_map/ppermute | solution.py:230
  14.5 6.3 %collective-permute-start.8 = (bf16[256,256]{1,0:T(8,128)(2,1)S(1)}, bf16[256,256]{1,0:T(8,128)(2,1)S(1)}, u32[]{:S(2)}, u32[]{:S(2)}) collective-permute-start(bf16[256,256]{1,0:T(8,128)(2,1)S(1)} %collective-permute-done.7.refs_2_), channel_id=1, source_target_pairs={{0,4},{4,8},{8,12},{12,14},{14,10},{10,6},{6,2},{2,0},{1,5},{5,9},... | collective-permute-start | bytes 393224 | tf_op jit(solution)/shard_map/ppermute | solution.py:230
  16.6 6.2 %collective-permute-start.11 = (bf16[256,256]{1,0:T(8,128)(2,1)S(1)}, bf16[256,256]{1,0:T(8,128)(2,1)S(1)}, u32[]{:S(2)}, u32[]{:S(2)}) collective-permute-start(bf16[256,256]{1,0:T(8,128)(2,1)S(1)} %collective-permute-done.10.refs_3_), channel_id=1, source_target_pairs={{4,0},{8,4},{12,8},{14,12},{10,14},{6,10},{2,6},{0,2},{5,1},{9,5},... | collective-permute-start | bytes 393224 | tf_op jit(solution)/shard_map/ppermute | solution.py:230
  18.0 5.8 %collective-permute-start.2 = (bf16[256,256]{1,0:T(8,128)(2,1)S(1)}, bf16[256,256]{1,0:T(8,128)(2,1)S(1)}, u32[]{:S(2)}, u32[]{:S(2)}) collective-permute-start(bf16[256,256]{1,0:T(8,128)(2,1)S(1)} %collective-permute-done.1.refs_0_), channel_id=1, source_target_pairs={{0,4},{4,8},{8,12},{12,14},{14,10},{10,6},{6,2},{2,0},{1,5},{5,9},... | collective-permute-start | bytes 393224 | tf_op jit(solution)/shard_map/ppermute | solution.py:230
  19.9 5.9 %collective-permute-start.5 = (bf16[256,256]{1,0:T(8,128)(2,1)S(1)}, bf16[256,256]{1,0:T(8,128)(2,1)S(1)}, u32[]{:S(2)}, u32[]{:S(2)}) collective-permute-start(bf16[256,256]{1,0:T(8,128)(2,1)S(1)} %collective-permute-done.4.refs_1_), channel_id=1, source_target_pairs={{4,0},{8,4},{12,8},{14,12},{10,14},{6,10},{2,6},{0,2},{5,1},{9,5},... | collective-permute-start | bytes 393224 | tf_op jit(solution)/shard_map/ppermute | solution.py:230
  20.8 6.1 %collective-permute-start.13 = (bf16[256,256]{1,0:T(8,128)(2,1)S(1)}, bf16[256,256]{1,0:T(8,128)(2,1)S(1)}, u32[]{:S(2)}, u32[]{:S(2)}) collective-permute-start(bf16[256,256]{1,0:T(8,128)(2,1)S(1)} %collective-permute-done.8.refs_2_), channel_id=1, source_target_pairs={{0,4},{4,8},{8,12},{12,14},{14,10},{10,6},{6,2},{2,0},{1,5},{5,9},... | collective-permute-start | bytes 393224 | tf_op jit(solution)/shard_map/ppermute | solution.py:230
  22.7 5.0 %collective-permute-start.14 = (bf16[256,256]{1,0:T(8,128)(2,1)S(1)}, bf16[256,256]{1,0:T(8,128)(2,1)S(1)}, u32[]{:S(2)}, u32[]{:S(2)}) collective-permute-start(bf16[256,256]{1,0:T(8,128)(2,1)S(1)} %collective-permute-done.11.refs_3_), channel_id=1, source_target_pairs={{4,0},{8,4},{12,8},{14,12},{10,14},{6,10},{2,6},{0,2},{5,1},{9,5},... | collective-permute-start | bytes 393224 | tf_op jit(solution)/shard_map/ppermute | solution.py:230
  28.0 1.6 %collective-permute-start.15 = (bf16[512,256]{1,0:T(8,128)(2,1)S(1)}, bf16[512,256]{1,0:T(8,128)(2,1)S(1)}, u32[]{:S(2)}, u32[]{:S(2)}) collective-permute-start(bf16[512,256]{1,0:T(8,128)(2,1)S(1)} %get-tuple-element.61), channel_id=1, source_target_pairs={{0,1},{1,0},{2,3},{3,2},{4,5},{5,4},{6,7},{7,6},{8,9},{9,8},{10,11... | collective-permute-start | bytes 786440 | tf_op jit(solution)/shard_map/ppermute | solution.py:338
  28.4 1.7 %collective-permute-start.16 = (bf16[512,256]{1,0:T(8,128)(2,1)S(1)}, bf16[512,256]{1,0:T(8,128)(2,1)S(1)}, u32[]{:S(2)}, u32[]{:S(2)}) collective-permute-start(bf16[512,256]{1,0:T(8,128)(2,1)S(1)} %get-tuple-element.62), channel_id=1, source_target_pairs={{0,1},{1,0},{2,3},{3,2},{4,5},{5,4},{6,7},{7,6},{8,9},{9,8},{10,11... | collective-permute-start | bytes 786440 | tf_op jit(solution)/shard_map/ppermute | solution.py:338
  30.6 5.8 %collective-permute-start.17 = (bf16[256,256]{1,0:T(8,128)(2,1)S(1)}, bf16[256,256]{1,0:T(8,128)(2,1)S(1)}, u32[]{:S(2)}, u32[]{:S(2)}) collective-permute-start(bf16[256,256]{1,0:T(8,128)(2,1)S(1)} %get-tuple-element.65), channel_id=1, source_target_pairs={{4,0},{8,4},{12,8},{14,12},{10,14},{6,10},{2,6},{0,2},{5,1},{9,5},... | collective-permute-start | bytes 393224 | tf_op jit(solution)/shard_map/ppermute | solution.py:230
  30.8 6.3 %collective-permute-start.21 = (bf16[256,256]{1,0:T(8,128)(2,1)S(1)}, bf16[256,256]{1,0:T(8,128)(2,1)S(1)}, u32[]{:S(2)}, u32[]{:S(2)}) collective-permute-start(bf16[256,256]{1,0:T(8,128)(2,1)S(1)} %get-tuple-element.67), channel_id=1, source_target_pairs={{0,4},{4,8},{8,12},{12,14},{14,10},{10,6},{6,2},{2,0},{1,5},{5,9},... | collective-permute-start | bytes 393224 | tf_op jit(solution)/shard_map/ppermute | solution.py:230
  33.1 6.5 %collective-permute-start.20 = (bf16[256,256]{1,0:T(8,128)(2,1)S(1)}, bf16[256,256]{1,0:T(8,128)(2,1)S(1)}, u32[]{:S(2)}, u32[]{:S(2)}) collective-permute-start(bf16[256,256]{1,0:T(8,128)(2,1)S(1)} %get-tuple-element.70), channel_id=1, source_target_pairs={{0,4},{4,8},{8,12},{12,14},{14,10},{10,6},{6,2},{2,0},{1,5},{5,9},... | collective-permute-start | bytes 393224 | tf_op jit(solution)/shard_map/ppermute | solution.py:230
  34.8 6.7 %collective-permute-start.28 = (bf16[256,256]{1,0:T(8,128)(2,1)S(1)}, bf16[256,256]{1,0:T(8,128)(2,1)S(1)}, u32[]{:S(2)}, u32[]{:S(2)}) collective-permute-start(bf16[256,256]{1,0:T(8,128)(2,1)S(1)} %get-tuple-element.87), channel_id=1, source_target_pairs={{4,0},{8,4},{12,8},{14,12},{10,14},{6,10},{2,6},{0,2},{5,1},{9,5},... | collective-permute-start | bytes 393224 | tf_op jit(solution)/shard_map/ppermute | solution.py:230
  36.5 6.1 %collective-permute-start.18 = (bf16[256,256]{1,0:T(8,128)(2,1)S(1)}, bf16[256,256]{1,0:T(8,128)(2,1)S(1)}, u32[]{:S(2)}, u32[]{:S(2)}) collective-permute-start(bf16[256,256]{1,0:T(8,128)(2,1)S(1)} %add_convert_fusion.9), channel_id=1, source_target_pairs={{4,0},{8,4},{12,8},{14,12},{10,14},{6,10},{2,6},{0,2},{5,1},{9,5},... | collective-permute-start | bytes 393224 | tf_op jit(solution)/shard_map/ppermute | solution.py:405
  37.2 6.4 %collective-permute-start.22 = (bf16[256,256]{1,0:T(8,128)(2,1)S(1)}, bf16[256,256]{1,0:T(8,128)(2,1)S(1)}, u32[]{:S(2)}, u32[]{:S(2)}) collective-permute-start(bf16[256,256]{1,0:T(8,128)(2,1)S(1)} %add_convert_fusion.6), channel_id=1, source_target_pairs={{0,4},{4,8},{8,12},{12,14},{14,10},{10,6},{6,2},{2,0},{1,5},{5,9},... | collective-permute-start | bytes 393224 | tf_op jit(solution)/shard_map/ppermute | solution.py:405
  39.7 6.1 %collective-permute-start.26 = (bf16[256,256]{1,0:T(8,128)(2,1)S(1)}, bf16[256,256]{1,0:T(8,128)(2,1)S(1)}, u32[]{:S(2)}, u32[]{:S(2)}) collective-permute-start(bf16[256,256]{1,0:T(8,128)(2,1)S(1)} %add_convert_fusion.5), channel_id=1, source_target_pairs={{0,4},{4,8},{8,12},{12,14},{14,10},{10,6},{6,2},{2,0},{1,5},{5,9},... | collective-permute-start | bytes 393224 | tf_op jit(solution)/shard_map/ppermute | solution.py:405
  41.5 6.2 %collective-permute-start.29 = (bf16[256,256]{1,0:T(8,128)(2,1)S(1)}, bf16[256,256]{1,0:T(8,128)(2,1)S(1)}, u32[]{:S(2)}, u32[]{:S(2)}) collective-permute-start(bf16[256,256]{1,0:T(8,128)(2,1)S(1)} %add_convert_fusion.1), channel_id=1, source_target_pairs={{4,0},{8,4},{12,8},{14,12},{10,14},{6,10},{2,6},{0,2},{5,1},{9,5},... | collective-permute-start | bytes 393224 | tf_op jit(solution)/shard_map/ppermute | solution.py:405
  42.6 9.0 %collective-permute-start.19 = (bf16[256,256]{1,0:T(8,128)(2,1)S(1)}, bf16[256,256]{1,0:T(8,128)(2,1)S(1)}, u32[]{:S(2)}, u32[]{:S(2)}) collective-permute-start(bf16[256,256]{1,0:T(8,128)(2,1)S(1)} %add_convert_fusion.8), channel_id=1, source_target_pairs={{4,0},{8,4},{12,8},{14,12},{10,14},{6,10},{2,6},{0,2},{5,1},{9,5},... | collective-permute-start | bytes 393224 | tf_op jit(solution)/shard_map/ppermute | solution.py:405
  43.6 5.9 %collective-permute-start.23 = (bf16[256,256]{1,0:T(8,128)(2,1)S(1)}, bf16[256,256]{1,0:T(8,128)(2,1)S(1)}, u32[]{:S(2)}, u32[]{:S(2)}) collective-permute-start(bf16[256,256]{1,0:T(8,128)(2,1)S(1)} %add_convert_fusion.4), channel_id=1, source_target_pairs={{0,4},{4,8},{8,12},{12,14},{14,10},{10,6},{6,2},{2,0},{1,5},{5,9},... | collective-permute-start | bytes 393224 | tf_op jit(solution)/shard_map/ppermute | solution.py:405
  45.9 7.9 %collective-permute-start.27 = (bf16[256,256]{1,0:T(8,128)(2,1)S(1)}, bf16[256,256]{1,0:T(8,128)(2,1)S(1)}, u32[]{:S(2)}, u32[]{:S(2)}) collective-permute-start(bf16[256,256]{1,0:T(8,128)(2,1)S(1)} %add_convert_fusion.2), channel_id=1, source_target_pairs={{0,4},{4,8},{8,12},{12,14},{14,10},{10,6},{6,2},{2,0},{1,5},{5,9},... | collective-permute-start | bytes 393224 | tf_op jit(solution)/shard_map/ppermute | solution.py:405
  47.8 5.9 %collective-permute-start.30 = (bf16[256,256]{1,0:T(8,128)(2,1)S(1)}, bf16[256,256]{1,0:T(8,128)(2,1)S(1)}, u32[]{:S(2)}, u32[]{:S(2)}) collective-permute-start(bf16[256,256]{1,0:T(8,128)(2,1)S(1)} %add_convert_fusion), channel_id=1, source_target_pairs={{4,0},{8,4},{12,8},{14,12},{10,14},{6,10},{2,6},{0,2},{5,1},{9,5},... | collective-permute-start | bytes 393224 | tf_op jit(solution)/shard_map/ppermute | solution.py:405
  48.5 8.1 %copy-start = (bf16[256,256]{1,0:T(8,128)(2,1)S(1)}, bf16[256,256]{1,0:T(8,128)(2,1)}, u32[]{:S(2)}) copy-start(bf16[256,256]{1,0:T(8,128)(2,1)} %w.1) | copy-start | bytes 393220
  49.6 5.0 %collective-permute-start.24 = (bf16[256,256]{1,0:T(8,128)(2,1)S(1)}, bf16[256,256]{1,0:T(8,128)(2,1)S(1)}, u32[]{:S(2)}, u32[]{:S(2)}) collective-permute-start(bf16[256,256]{1,0:T(8,128)(2,1)S(1)} %add_convert_fusion.3), channel_id=1, source_target_pairs={{0,4},{4,8},{8,12},{12,14},{14,10},{10,6},{6,2},{2,0},{1,5},{5,9},... | collective-permute-start | bytes 393224 | tf_op jit(solution)/shard_map/ppermute | solution.py:405
  51.6 5.0 %collective-permute-start.25 = (bf16[256,256]{1,0:T(8,128)(2,1)S(1)}, bf16[256,256]{1,0:T(8,128)(2,1)S(1)}, u32[]{:S(2)}, u32[]{:S(2)}) collective-permute-start(bf16[256,256]{1,0:T(8,128)(2,1)S(1)} %add_convert_fusion.7), channel_id=1, source_target_pairs={{4,0},{8,4},{12,8},{14,12},{10,14},{6,10},{2,6},{0,2},{5,1},{9,5},... | collective-permute-start | bytes 393224 | tf_op jit(solution)/shard_map/ppermute | solution.py:405

commit v6 on v5

--- a/solution.py
+++ b/solution.py
@@ -318,28 +318,26 @@
     def node_piece(k):
         return slice(k * rows, (k + 1) * rows)
 
-    def last(k, part, turned, fa, ba, keep, give):
-        at = node_piece(k)
-        total = part[at, :] + jnp.dot(turned[at, :hrows], fa[...], preferred_element_type=F32)
-        total = total + jnp.dot(turned[at, hrows:], ba[...], preferred_element_type=F32)
+    everyone = (span, width)
+
+    def last(part, turned, fa, ba, keep, give):
+        total = part[...] + jnp.dot(turned[:, :hrows], fa[...], preferred_element_type=F32)
+        total = total + jnp.dot(turned[:, hrows:], ba[...], preferred_element_type=F32)
+        give[...] = total.astype(BF16)
         keep[...] = total
-        give[...] = total.astype(BF16)
-
-    keep, got = [], []
-    for k in range(2):
-        kept, give = call(
-            functools.partial(last, k),
-            (array(shape, F32), array(shape, BF16)),
-            [VM] * 4,
-            (part, turned, *long[far]),
-            "gather_last",
-        )
-        keep.append(kept)
-        got.append(lax.ppermute(give, "col", OTHER))
+
+    keep, give = call(
+        last,
+        (array(everyone, F32), array(everyone, BF16)),
+        [VM] * 4,
+        (part, turned, *long[far]),
+        "gather_last",
+    )
+    got = lax.ppermute(give, "col", OTHER)
 
     def back_of(k, keep, got, scale, scaled):
         at = node_piece(k)
-        mixed = over(scale[at, :]) * (keep[...] + got[...].astype(F32))
+        mixed = over(scale[at, :]) * (keep[at, :] + got[at, :].astype(F32))
         sig = jax.nn.sigmoid(mixed)
         slope = sig * (1.0 + mixed * (1.0 - sig))
         return (scaled[at, :] * slope).astype(BF16)
@@ -348,31 +346,22 @@
         at = pl.ds(half_rows_of(far, 0).start, rows)
         return jnp.dot(dense[at, node_piece(k)], back, preferred_element_type=F32)
 
-    def mix_first(keep, got, scale, scaled, dense, back, far_part):
-        value = back_of(0, keep, got, scale, scaled)
-        back[...] = value
-        far_part[...] = far_term(0, dense, value)
-
-    def mix_second(keep, got, scale, scaled, dense, far_part, back, c0, c1):
-        value = back_of(1, keep, got, scale, scaled)
-        back[...] = value
-        out = far_part[...] + far_term(1, dense, value)
+    def mix(keep, got, scale, scaled, dense, back0, back1, c0, c1):
+        out = None
+        for k, back in enumerate((back0, back1)):
+            value = back_of(k, keep, got, scale, scaled)
+            back[...] = value
+            term = far_term(k, dense, value)
+            out = term if out is None else out + term
         c0[...] = out[:hrows].astype(BF16)
         c1[...] = out[hrows:].astype(BF16)
 
-    back0, far_part = call(
-        mix_first,
-        (array(shape, BF16), array(shape, F32)),
+    back0, back1, *up = call(
+        mix,
+        (array(shape, BF16),) * 2 + (array(hshape, BF16),) * 2,
         [VM] * 5,
-        (keep[0], got[0], scale_all, scaled_cot, dense),
-        "mix_first",
-    )
-    back1, *up = call(
-        mix_second,
-        (array(shape, BF16), array(hshape, BF16), array(hshape, BF16)),
-        [VM] * 6,
-        (keep[1], got[1], scale_all, scaled_cot, dense, far_part),
-        "mix_second",
+        (keep, got, scale_all, scaled_cot, dense),
+        "mix",
     )
     back = [back0, back1]
     token = up[0]
@@ -439,16 +428,17 @@
     up = (shift(v0, 0), shift(v1, 1))
     down = (w0, w1)
 
-    def mix_out(keep0, keep1, got0, got1, scale, out):
+    def mix_out(keep, got, scale, out):
         q = lax.axis_index("col")
-        for k, (keep, got) in enumerate(((keep0, got0), (keep1, got1))):
-            mixed = over(scale[node_piece(k), :]) * (keep[...] + got[...].astype(F32))
+        for k in range(2):
+            at = node_piece(k)
+            mixed = over(scale[at, :]) * (keep[at, :] + got[at, :].astype(F32))
             mixed = mixed.reshape(blocks // 2, 2, half, width)
             mixed = jnp.where(q == 0, mixed[:, 0], mixed[:, 1]).reshape(hshape)
             out[k * hrows : (k + 1) * hrows, :] = (mixed * jax.nn.sigmoid(mixed)).astype(BF16)
 
     output = call(
-        mix_out, array(shape, BF16), [VM] * 5, (*keep, *got, after(scale_all, v1)), "mix_out"
+        mix_out, array(shape, BF16), [VM] * 3, (keep, got, after(scale_all, v1)), "mix_out"
     )
 
     def finish(base0, base1, g0, r1, g1, r0, sc, w, out_hbm, out, sems):

time: 57.8 us -> 57.4 us (level)
  waiting for transfers between devices: 11.6 us -> 12.3 us
    ppermute x2 -> x1, waiting for transfers between devices: 0.7 us -> 1.9 us  [dense_plan(): got = lax.ppermute(give, 'col', OTHER)]
    ppermute x10, waiting for transfers between devices: 5.26 us -> 4.62 us  [shift(): return lax.ppermute(x, 'row', (fwd, bwd)[h])]
    pallas_call x16 -> x14, Pallas kernels: 9.89 us -> 9.48 us  [call(): pl.pallas_call(body, out_shape=outs, in_specs=ins, out_specs=jax.tree.map...]
  transfers between devices with their start and end apart: 31 -> 30, of which waited for: 15 -> 15; matrix products, arithmetic and copies ran while one was open for 0% -> 0% of each run, Pallas kernels for 18% -> 17%
where the time goes in v6:
time: 57.4 us; the launch traced here: 57.2 us
  starting transfers between devices  31 us (54%)
  Pallas kernels  12.9 us (22%)
  waiting for transfers between devices  12.3 us (21%)
  between operations  0.85 us (1%)
    ppermute x9, starting transfers between devices, shift_pair(): lax.ppermute(pair[0], 'row', fwd)  18.5 us
    ppermute x10, starting transfers between devices, shift(): return lax.ppermute(x, 'row', (fwd, bwd)[h])  11.5 us
    pallas_call x14, Pallas kernels, call(): pl.pallas_call(body, out_shape=outs, in_specs=ins, out_specs=jax.tree.map...  9.48 us
    ppermute x10, waiting for transfers between devices, shift(): return lax.ppermute(x, 'row', (fwd, bwd)[h])  4.62 us
    ppermute x9, waiting for transfers between devices, shift_pair(): lax.ppermute(pair[1], 'row', bwd)  2.94 us
    ppermute x9, waiting for transfers between devices, shift_pair(): lax.ppermute(pair[0], 'row', fwd)  2.8 us
    pallas_call x1, Pallas kernels, dense_plan(): pl.pallas_call(densify, out_shape=(pltpu.VMEM((n * rows, span), BF16), ar...  2.38 us
    ppermute x1, waiting for transfers between devices, dense_plan(): got = lax.ppermute(give, 'col', OTHER)  1.9 us
  transfers between devices with their start and end apart: 30, of which 15 were waited for; matrix products, arithmetic and copies ran while one was open for 0% of the time, Pallas kernels for 17%

profile of v6, /device:TPU:0, one launch (start us, length us, event | category | flops | bytes accessed | tf_op | source)
XLA Modules:
  0.0 57.2 jit_solution(12706826378262744373)
XLA Ops:
  0.6 1.3 %project.1 = (bf16[256,256]{1,0:T(8,128)(2,1)S(1)}, bf16[256,256]{1,0:T(8,128)(2,1)S(1)}, f32[512,128]{1,0:T(8,128)S(1)}) custom-call(s32[8,64]{1,0:T(8,128)} %deg_hbm.3, bf16[512,256]{1,0:T(8,128)(2,1)} %bitcast.13, bf16[256,256]{1,0:T(8,128)(2,1)} %w.1), custom_call_target="tpu_custom_call" | custom-call | tf_op jit(solution)/shard_map/project/pallas_call | solution.py:83
  1.9 3.1 %collective-permute-start.6 = (bf16[256,256]{1,0:T(8,128)(2,1)S(1)}, bf16[256,256]{1,0:T(8,128)(2,1)S(1)}, u32[]{:S(2)}, u32[]{:S(2)}) collective-permute-start(bf16[256,256]{1,0:T(8,128)(2,1)S(1)} %get-tuple-element.46.refs_0_.s0), channel_id=1, source_target_pairs={{0,4},{4,8},{8,12},{12,14},{14,10},{10,6},{6,2},{2,0},{1,5},{5,9},... | collective-permute-start | bytes 393224 | tf_op jit(solution)/shard_map/ppermute | solution.py:230
  5.0 2.0 %collective-permute-start = (bf16[256,256]{1,0:T(8,128)(2,1)S(1)}, bf16[256,256]{1,0:T(8,128)(2,1)S(1)}, u32[]{:S(2)}, u32[]{:S(2)}) collective-permute-start(bf16[256,256]{1,0:T(8,128)(2,1)S(1)} %get-tuple-element.45.refs_1_.s1), channel_id=1, source_target_pairs={{0,4},{4,8},{8,12},{12,14},{14,10},{10,6},{6,2},{2,0},{1,5},{5,9},... | collective-permute-start | bytes 393224 | tf_op jit(solution)/shard_map/ppermute | solution.py:230
  7.0 2.4 %densify.1 = (bf16[4096,1024]{1,0:T(8,128)(2,1)S(1)}, bf16[528,256]{1,0:T(8,128)(2,1)S(1)}) custom-call(s32[8,16]{1,0:T(8,128)} %cols_hbm.1, s32[128,64,128]{2,1,0:T(8,128)} %adj_hbm.1, s32[8,64]{1,0:T(8,128)} %deg_hbm.3, bf16[512,256]{1,0:T(8,128)(2,1)} %bitcast.11), custom_call_target="tpu_custom_call" | custom-call | tf_op jit(solution)/shard_map/densify/pallas_call | solution.py:213
  9.4 2.1 %collective-permute-start.7 = (bf16[256,256]{1,0:T(8,128)(2,1)S(1)}, bf16[256,256]{1,0:T(8,128)(2,1)S(1)}, u32[]{:S(2)}, u32[]{:S(2)}) collective-permute-start(bf16[256,256]{1,0:T(8,128)(2,1)S(1)} %collective-permute-done.6.refs_2_), channel_id=1, source_target_pairs={{0,4},{4,8},{8,12},{12,14},{14,10},{10,6},{6,2},{2,0},{1,5},{5,9},... | collective-permute-start | bytes 393224 | tf_op jit(solution)/shard_map/ppermute | solution.py:230
  11.6 2.0 %collective-permute-start.1 = (bf16[256,256]{1,0:T(8,128)(2,1)S(1)}, bf16[256,256]{1,0:T(8,128)(2,1)S(1)}, u32[]{:S(2)}, u32[]{:S(2)}) collective-permute-start(bf16[256,256]{1,0:T(8,128)(2,1)S(1)} %collective-permute-done.refs_0_), channel_id=1, source_target_pairs={{0,4},{4,8},{8,12},{12,14},{14,10},{10,6},{6,2},{2,0},{1,5},{5,9},... | collective-permute-start | bytes 393224 | tf_op jit(solution)/shard_map/ppermute | solution.py:230
  13.6 0.8 %collective-permute-done.7.refs_2_ = bf16[256,256]{1,0:T(8,128)(2,1)S(1)} collective-permute-done((bf16[256,256]{1,0:T(8,128)(2,1)S(1)}, bf16[256,256]{1,0:T(8,128)(2,1)S(1)}, u32[]{:S(2)}, u32[]{:S(2)}) %collective-permute-start.7) | collective-permute-done | bytes 131104 | tf_op jit(solution)/shard_map/ppermute | solution.py:230
  14.5 2.0 %collective-permute-start.8 = (bf16[256,256]{1,0:T(8,128)(2,1)S(1)}, bf16[256,256]{1,0:T(8,128)(2,1)S(1)}, u32[]{:S(2)}, u32[]{:S(2)}) collective-permute-start(bf16[256,256]{1,0:T(8,128)(2,1)S(1)} %collective-permute-done.7.refs_2_), channel_id=1, source_target_pairs={{0,4},{4,8},{8,12},{12,14},{14,10},{10,6},{6,2},{2,0},{1,5},{5,9},... | collective-permute-start | bytes 393224 | tf_op jit(solution)/shard_map/ppermute | solution.py:230
  16.6 0.7 %gather_near.1.refs_4_ = f32[256,1024]{1,0:T(8,128)S(1)} custom-call(bf16[4096,1024]{1,0:T(8,128)(2,1)S(1)} %get-tuple-element.44.dense, bf16[256,256]{1,0:T(8,128)(2,1)S(1)} %get-tuple-element.46.refs_0_.s0, bf16[256,256]{1,0:T(8,128)(2,1)S(1)} %get-tuple-element.45.refs_1_.s1, bf16[256,256]{1,0:T(8,128)(2,1)S(1)} %collective-permute-done.6.refs_2_, ...), custom_call_target="tpu_custom_call" | custom-call | tf_op jit(solution)/shard_map/gather_near/pallas_call | solution.py:83
  17.3 0.7 %collective-permute-done.1.refs_0_ = bf16[256,256]{1,0:T(8,128)(2,1)S(1)} collective-permute-done((bf16[256,256]{1,0:T(8,128)(2,1)S(1)}, bf16[256,256]{1,0:T(8,128)(2,1)S(1)}, u32[]{:S(2)}, u32[]{:S(2)}) %collective-permute-start.1) | collective-permute-done | bytes 131104 | tf_op jit(solution)/shard_map/ppermute | solution.py:230
  18.0 1.9 %collective-permute-start.2 = (bf16[256,256]{1,0:T(8,128)(2,1)S(1)}, bf16[256,256]{1,0:T(8,128)(2,1)S(1)}, u32[]{:S(2)}, u32[]{:S(2)}) collective-permute-start(bf16[256,256]{1,0:T(8,128)(2,1)S(1)} %collective-permute-done.1.refs_0_), channel_id=1, source_target_pairs={{0,4},{4,8},{8,12},{12,14},{14,10},{10,6},{6,2},{2,0},{1,5},{5,9},... | collective-permute-start | bytes 393224 | tf_op jit(solution)/shard_map/ppermute | solution.py:230
  20.0 0.7 %gather_two.1.refs_4_ = f32[256,1024]{1,0:T(8,128)S(1)} custom-call(bf16[4096,1024]{1,0:T(8,128)(2,1)S(1)} %get-tuple-element.44.dense, bf16[256,256]{1,0:T(8,128)(2,1)S(1)} %collective-permute-done.refs_0_, bf16[256,256]{1,0:T(8,128)(2,1)S(1)} %collective-permute-done.3.refs_1_, bf16[256,256]{1,0:T(8,128)(2,1)S(1)} %collective-permute-done.7.refs_2_, ...), custom_call_target="tpu_custom_call" | custom-call | tf_op jit(solution)/shard_map/gather_two/pallas_call | solution.py:83
  20.8 1.9 %collective-permute-start.13 = (bf16[256,256]{1,0:T(8,128)(2,1)S(1)}, bf16[256,256]{1,0:T(8,128)(2,1)S(1)}, u32[]{:S(2)}, u32[]{:S(2)}) collective-permute-start(bf16[256,256]{1,0:T(8,128)(2,1)S(1)} %collective-permute-done.8.refs_2_), channel_id=1, source_target_pairs={{0,4},{4,8},{8,12},{12,14},{14,10},{10,6},{6,2},{2,0},{1,5},{5,9},... | collective-permute-start | bytes 393224 | tf_op jit(solution)/shard_map/ppermute | solution.py:230
  23.1 0.7 %gather_three.1.part = f32[256,1024]{1,0:T(8,128)S(1)} custom-call(bf16[4096,1024]{1,0:T(8,128)(2,1)S(1)} %get-tuple-element.44.dense, bf16[256,256]{1,0:T(8,128)(2,1)S(1)} %collective-permute-done.1.refs_0_, bf16[256,256]{1,0:T(8,128)(2,1)S(1)} %collective-permute-done.4.refs_1_, bf16[256,256]{1,0:T(8,128)(2,1)S(1)} %collective-permute-done.8.refs_2_, ...), custom_call_target="tpu_custom_call" | custom-call | tf_op jit(solution)/shard_map/gather_three/pallas_call | solution.py:83
  23.8 2.0 %collective-permute-done.5.ba = bf16[256,256]{1,0:T(8,128)(2,1)S(1)} collective-permute-done((bf16[256,256]{1,0:T(8,128)(2,1)S(1)}, bf16[256,256]{1,0:T(8,128)(2,1)S(1)}, u32[]{:S(2)}, u32[]{:S(2)}) %collective-permute-start.5) | collective-permute-done | bytes 131104 | tf_op jit(solution)/shard_map/ppermute | solution.py:230
  25.8 1.1 %turn.1 = (f32[8,2,64,256]{3,2,1,0:T(8,128)S(1)}, bf16[1024,512]{1,0:T(8,128)(2,1)S(1)}) custom-call(bf16[4096,1024]{1,0:T(8,128)(2,1)S(1)} %get-tuple-element.44.dense, bf16[256,256]{1,0:T(8,128)(2,1)S(1)} %collective-permute-done.2.fa, bf16[256,256]{1,0:T(8,128)(2,1)S(1)} %collective-permute-done.5.ba, f32[256,1024]{1,0:T(8,128)S(1)} %gather_three.1.part, ...), custom_call_target="tpu_custom_call" | custom-call | tf_op jit(solution)/shard_map/turn/pallas_call | solution.py:83
  26.9 0.8 %collective-permute-done.14.ba = bf16[256,256]{1,0:T(8,128)(2,1)S(1)} collective-permute-done((bf16[256,256]{1,0:T(8,128)(2,1)S(1)}, bf16[256,256]{1,0:T(8,128)(2,1)S(1)}, u32[]{:S(2)}, u32[]{:S(2)}) %collective-permute-start.14) | collective-permute-done | bytes 131104 | tf_op jit(solution)/shard_map/ppermute | solution.py:230
  28.2 1.9 %collective-permute-done.15.got = bf16[1024,256]{1,0:T(8,128)(2,1)S(1)} collective-permute-done((bf16[1024,256]{1,0:T(8,128)(2,1)S(1)}, bf16[1024,256]{1,0:T(8,128)(2,1)S(1)}, u32[]{:S(2)}, u32[]{:S(2)}) %collective-permute-start.15) | collective-permute-done | bytes 524320 | tf_op jit(solution)/shard_map/ppermute | solution.py:336
  30.1 0.7 %mix.1 = (bf16[512,256]{1,0:T(8,128)(2,1)S(1)}, bf16[512,256]{1,0:T(8,128)(2,1)S(1)}, bf16[256,256]{1,0:T(8,128)(2,1)S(1)}, bf16[256,256]{1,0:T(8,128)(2,1)S(1)}) custom-call(f32[1024,256]{1,0:T(8,128)S(1)} %get-tuple-element.56.keep, bf16[1024,256]{1,0:T(8,128)(2,1)S(1)} %collective-permute-done.15.got, f32[1024,128]{1,0:T(8,128)S(1)} %bitcast.7, ...), custom_call_target="tpu_custom_call" | custom-call | tf_op jit(solution)/shard_map/mix/pallas_call | solution.py:83
  31.0 1.9 %collective-permute-start.20 = (bf16[256,256]{1,0:T(8,128)(2,1)S(1)}, bf16[256,256]{1,0:T(8,128)(2,1)S(1)}, u32[]{:S(2)}, u32[]{:S(2)}) collective-permute-start(bf16[256,256]{1,0:T(8,128)(2,1)S(1)} %get-tuple-element.61), channel_id=1, source_target_pairs={{0,4},{4,8},{8,12},{12,14},{14,10},{10,6},{6,2},{2,0},{1,5},{5,9},... | collective-permute-start | bytes 393224 | tf_op jit(solution)/shard_map/ppermute | solution.py:230
  33.3 1.6 %collective-permute-start.19 = (bf16[256,256]{1,0:T(8,128)(2,1)S(1)}, bf16[256,256]{1,0:T(8,128)(2,1)S(1)}, u32[]{:S(2)}, u32[]{:S(2)}) collective-permute-start(bf16[256,256]{1,0:T(8,128)(2,1)S(1)} %get-tuple-element.64), channel_id=1, source_target_pairs={{0,4},{4,8},{8,12},{12,14},{14,10},{10,6},{6,2},{2,0},{1,5},{5,9},... | collective-permute-start | bytes 393224 | tf_op jit(solution)/shard_map/ppermute | solution.py:230
  35.4 1.0 %return_ab.1 = (f32[256,256]{1,0:T(8,128)S(1)}, f32[256,256]{1,0:T(8,128)S(1)}, f32[256,256]{1,0:T(8,128)S(1)}, f32[256,256]{1,0:T(8,128)S(1)}, f32[256,256]{1,0:T(8,128)S(1)}, /*index=5*/f32[256,256]{1,0:T(8,128)S(1)}) custom-call(bf16[4096,1024]{1,0:T(8,128)(2,1)S(1)} %get-tuple-element.44.dense, bf16[512,256]{1,0:T(8,128)(2,1)S(1)} %get-tuple-element.79.refs_0_.back0, ...), custom_call_target="tpu_custom_call" | custom-call | tf_op jit(solution)/shard_map/return_ab/pallas_call | solution.py:83
  37.4 1.9 %collective-permute-start.21 = (bf16[256,256]{1,0:T(8,128)(2,1)S(1)}, bf16[256,256]{1,0:T(8,128)(2,1)S(1)}, u32[]{:S(2)}, u32[]{:S(2)}) collective-permute-start(bf16[256,256]{1,0:T(8,128)(2,1)S(1)} %add_convert_fusion.6), channel_id=1, source_target_pairs={{0,4},{4,8},{8,12},{12,14},{14,10},{10,6},{6,2},{2,0},{1,5},{5,9},... | collective-permute-start | bytes 393224 | tf_op jit(solution)/shard_map/ppermute | solution.py:394
  39.9 1.8 %collective-permute-start.25 = (bf16[256,256]{1,0:T(8,128)(2,1)S(1)}, bf16[256,256]{1,0:T(8,128)(2,1)S(1)}, u32[]{:S(2)}, u32[]{:S(2)}) collective-permute-start(bf16[256,256]{1,0:T(8,128)(2,1)S(1)} %add_convert_fusion.5), channel_id=1, source_target_pairs={{0,4},{4,8},{8,12},{12,14},{14,10},{10,6},{6,2},{2,0},{1,5},{5,9},... | collective-permute-start | bytes 393224 | tf_op jit(solution)/shard_map/ppermute | solution.py:394
  42.7 1.1 %collective-permute-start.18 = (bf16[256,256]{1,0:T(8,128)(2,1)S(1)}, bf16[256,256]{1,0:T(8,128)(2,1)S(1)}, u32[]{:S(2)}, u32[]{:S(2)}) collective-permute-start(bf16[256,256]{1,0:T(8,128)(2,1)S(1)} %add_convert_fusion.8), channel_id=1, source_target_pairs={{4,0},{8,4},{12,8},{14,12},{10,14},{6,10},{2,6},{0,2},{5,1},{9,5},... | collective-permute-start | bytes 393224 | tf_op jit(solution)/shard_map/ppermute | solution.py:394
  43.9 1.7 %collective-permute-start.22 = (bf16[256,256]{1,0:T(8,128)(2,1)S(1)}, bf16[256,256]{1,0:T(8,128)(2,1)S(1)}, u32[]{:S(2)}, u32[]{:S(2)}) collective-permute-start(bf16[256,256]{1,0:T(8,128)(2,1)S(1)} %add_convert_fusion.4), channel_id=1, source_target_pairs={{0,4},{4,8},{8,12},{12,14},{14,10},{10,6},{6,2},{2,0},{1,5},{5,9},... | collective-permute-start | bytes 393224 | tf_op jit(solution)/shard_map/ppermute | solution.py:394
  46.4 1.7 %collective-permute-start.26 = (bf16[256,256]{1,0:T(8,128)(2,1)S(1)}, bf16[256,256]{1,0:T(8,128)(2,1)S(1)}, u32[]{:S(2)}, u32[]{:S(2)}) collective-permute-start(bf16[256,256]{1,0:T(8,128)(2,1)S(1)} %add_convert_fusion.2), channel_id=1, source_target_pairs={{0,4},{4,8},{8,12},{12,14},{14,10},{10,6},{6,2},{2,0},{1,5},{5,9},... | collective-permute-start | bytes 393224 | tf_op jit(solution)/shard_map/ppermute | solution.py:394
  49.6 1.6 %collective-permute-start.23 = (bf16[256,256]{1,0:T(8,128)(2,1)S(1)}, bf16[256,256]{1,0:T(8,128)(2,1)S(1)}, u32[]{:S(2)}, u32[]{:S(2)}) collective-permute-start(bf16[256,256]{1,0:T(8,128)(2,1)S(1)} %add_convert_fusion.3), channel_id=1, source_target_pairs={{0,4},{4,8},{8,12},{12,14},{14,10},{10,6},{6,2},{2,0},{1,5},{5,9},... | collective-permute-start | bytes 393224 | tf_op jit(solution)/shard_map/ppermute | solution.py:394
  52.2 0.9 %mix_out.1 = bf16[512,256]{1,0:T(8,128)(2,1)} custom-call(f32[1024,256]{1,0:T(8,128)S(1)} %get-tuple-element.56.keep, bf16[1024,256]{1,0:T(8,128)(2,1)S(1)} %collective-permute-done.15.got, f32[1024,128]{1,0:T(8,128)S(1)} %bitcast.8), custom_call_target="tpu_custom_call" | custom-call | tf_op jit(solution)/shard_map/mix_out/pallas_call | solution.py:83
  53.7 0.9 %collective-permute-done.23.g0 = bf16[256,256]{1,0:T(8,128)(2,1)S(1)} collective-permute-done((bf16[256,256]{1,0:T(8,128)(2,1)S(1)}, bf16[256,256]{1,0:T(8,128)(2,1)S(1)}, u32[]{:S(2)}, u32[]{:S(2)}) %collective-permute-start.23) | collective-permute-done | bytes 131104 | tf_op jit(solution)/shard_map/ppermute | solution.py:394
  54.6 1.6 %collective-permute-done.24.r1 = bf16[256,256]{1,0:T(8,128)(2,1)S(1)} collective-permute-done((bf16[256,256]{1,0:T(8,128)(2,1)S(1)}, bf16[256,256]{1,0:T(8,128)(2,1)S(1)}, u32[]{:S(2)}, u32[]{:S(2)}) %collective-permute-start.24) | collective-permute-done | bytes 131104 | tf_op jit(solution)/shard_map/ppermute | solution.py:394
  56.2 1.0 %finish.1 = bf16[512,256]{1,0:T(8,128)(2,1)} custom-call(f32[256,256]{1,0:T(8,128)S(1)} %get-tuple-element.75.base0, f32[256,256]{1,0:T(8,128)S(1)} %get-tuple-element.76.base1, bf16[256,256]{1,0:T(8,128)(2,1)S(1)} %collective-permute-done.23.g0, bf16[256,256]{1,0:T(8,128)(2,1)S(1)} %collective-permute-done.24.r1, ...), custom_call_target="tpu_custom_call" | custom-call | tf_op jit(solution)/shard_map/finish/pallas_call | solution.py:462
  (56 shorter events, 8.9 us)
Async XLA Ops:
  1.9 7.5 %collective-permute-start.6 = (bf16[256,256]{1,0:T(8,128)(2,1)S(1)}, bf16[256,256]{1,0:T(8,128)(2,1)S(1)}, u32[]{:S(2)}, u32[]{:S(2)}) collective-permute-start(bf16[256,256]{1,0:T(8,128)(2,1)S(1)} %get-tuple-element.46.refs_0_.s0), channel_id=1, source_target_pairs={{0,4},{4,8},{8,12},{12,14},{14,10},{10,6},{6,2},{2,0},{1,5},{5,9},... | collective-permute-start | bytes 393224 | tf_op jit(solution)/shard_map/ppermute | solution.py:230
  5.0 6.5 %collective-permute-start.9 = (bf16[256,256]{1,0:T(8,128)(2,1)S(1)}, bf16[256,256]{1,0:T(8,128)(2,1)S(1)}, u32[]{:S(2)}, u32[]{:S(2)}) collective-permute-start(bf16[256,256]{1,0:T(8,128)(2,1)S(1)} %get-tuple-element.45.refs_1_.s1), channel_id=1, source_target_pairs={{4,0},{8,4},{12,8},{14,12},{10,14},{6,10},{2,6},{0,2},{5,1},{9,5},... | collective-permute-start | bytes 393224 | tf_op jit(solution)/shard_map/ppermute | solution.py:230
  5.0 6.5 %collective-permute-start = (bf16[256,256]{1,0:T(8,128)(2,1)S(1)}, bf16[256,256]{1,0:T(8,128)(2,1)S(1)}, u32[]{:S(2)}, u32[]{:S(2)}) collective-permute-start(bf16[256,256]{1,0:T(8,128)(2,1)S(1)} %get-tuple-element.45.refs_1_.s1), channel_id=1, source_target_pairs={{0,4},{4,8},{8,12},{12,14},{14,10},{10,6},{6,2},{2,0},{1,5},{5,9},... | collective-permute-start | bytes 393224 | tf_op jit(solution)/shard_map/ppermute | solution.py:230
  7.0 6.5 %collective-permute-start.3 = (bf16[256,256]{1,0:T(8,128)(2,1)S(1)}, bf16[256,256]{1,0:T(8,128)(2,1)S(1)}, u32[]{:S(2)}, u32[]{:S(2)}) collective-permute-start(bf16[256,256]{1,0:T(8,128)(2,1)S(1)} %get-tuple-element.46.refs_0_.s0), channel_id=1, source_target_pairs={{4,0},{8,4},{12,8},{14,12},{10,14},{6,10},{2,6},{0,2},{5,1},{9,5},... | collective-permute-start | bytes 393224 | tf_op jit(solution)/shard_map/ppermute | solution.py:230
  9.4 5.0 %collective-permute-start.7 = (bf16[256,256]{1,0:T(8,128)(2,1)S(1)}, bf16[256,256]{1,0:T(8,128)(2,1)S(1)}, u32[]{:S(2)}, u32[]{:S(2)}) collective-permute-start(bf16[256,256]{1,0:T(8,128)(2,1)S(1)} %collective-permute-done.6.refs_2_), channel_id=1, source_target_pairs={{0,4},{4,8},{8,12},{12,14},{14,10},{10,6},{6,2},{2,0},{1,5},{5,9},... | collective-permute-start | bytes 393224 | tf_op jit(solution)/shard_map/ppermute | solution.py:230
  11.5 5.0 %collective-permute-start.10 = (bf16[256,256]{1,0:T(8,128)(2,1)S(1)}, bf16[256,256]{1,0:T(8,128)(2,1)S(1)}, u32[]{:S(2)}, u32[]{:S(2)}) collective-permute-start(bf16[256,256]{1,0:T(8,128)(2,1)S(1)} %collective-permute-done.9.refs_3_), channel_id=1, source_target_pairs={{4,0},{8,4},{12,8},{14,12},{10,14},{6,10},{2,6},{0,2},{5,1},{9,5},... | collective-permute-start | bytes 393224 | tf_op jit(solution)/shard_map/ppermute | solution.py:230
  11.5 11.3 %collective-permute-start.12 = (bf16[528,256]{1,0:T(8,128)(2,1)S(1)}, bf16[528,256]{1,0:T(8,128)(2,1)S(1)}, u32[]{:S(2)}, u32[]{:S(2)}) collective-permute-start(bf16[528,256]{1,0:T(8,128)(2,1)S(1)} %get-tuple-element.51.pack), channel_id=1, source_target_pairs={{0,1},{1,0},{2,3},{3,2},{4,5},{5,4},{6,7},{7,6},{8,9},{9,8},{10,11... | collective-permute-start | bytes 811016 | tf_op jit(solution)/shard_map/ppermute | solution.py:270
  11.6 6.4 %collective-permute-start.1 = (bf16[256,256]{1,0:T(8,128)(2,1)S(1)}, bf16[256,256]{1,0:T(8,128)(2,1)S(1)}, u32[]{:S(2)}, u32[]{:S(2)}) collective-permute-start(bf16[256,256]{1,0:T(8,128)(2,1)S(1)} %collective-permute-done.refs_0_), channel_id=1, source_target_pairs={{0,4},{4,8},{8,12},{12,14},{14,10},{10,6},{6,2},{2,0},{1,5},{5,9},... | collective-permute-start | bytes 393224 | tf_op jit(solution)/shard_map/ppermute | solution.py:230
  13.6 6.3 %collective-permute-start.4 = (bf16[256,256]{1,0:T(8,128)(2,1)S(1)}, bf16[256,256]{1,0:T(8,128)(2,1)S(1)}, u32[]{:S(2)}, u32[]{:S(2)}) collective-permute-start(bf16[256,256]{1,0:T(8,128)(2,1)S(1)} %collective-permute-done.3.refs_1_), channel_id=1, source_target_pairs={{4,0},{8,4},{12,8},{14,12},{10,14},{6,10},{2,6},{0,2},{5,1},{9,5},... | collective-permute-start | bytes 393224 | tf_op jit(solution)/shard_map/ppermute | solution.py:230
  14.5 6.3 %collective-permute-start.8 = (bf16[256,256]{1,0:T(8,128)(2,1)S(1)}, bf16[256,256]{1,0:T(8,128)(2,1)S(1)}, u32[]{:S(2)}, u32[]{:S(2)}) collective-permute-start(bf16[256,256]{1,0:T(8,128)(2,1)S(1)} %collective-permute-done.7.refs_2_), channel_id=1, source_target_pairs={{0,4},{4,8},{8,12},{12,14},{14,10},{10,6},{6,2},{2,0},{1,5},{5,9},... | collective-permute-start | bytes 393224 | tf_op jit(solution)/shard_map/ppermute | solution.py:230
  16.6 6.2 %collective-permute-start.11 = (bf16[256,256]{1,0:T(8,128)(2,1)S(1)}, bf16[256,256]{1,0:T(8,128)(2,1)S(1)}, u32[]{:S(2)}, u32[]{:S(2)}) collective-permute-start(bf16[256,256]{1,0:T(8,128)(2,1)S(1)} %collective-permute-done.10.refs_3_), channel_id=1, source_target_pairs={{4,0},{8,4},{12,8},{14,12},{10,14},{6,10},{2,6},{0,2},{5,1},{9,5},... | collective-permute-start | bytes 393224 | tf_op jit(solution)/shard_map/ppermute | solution.py:230
  18.0 5.8 %collective-permute-start.2 = (bf16[256,256]{1,0:T(8,128)(2,1)S(1)}, bf16[256,256]{1,0:T(8,128)(2,1)S(1)}, u32[]{:S(2)}, u32[]{:S(2)}) collective-permute-start(bf16[256,256]{1,0:T(8,128)(2,1)S(1)} %collective-permute-done.1.refs_0_), channel_id=1, source_target_pairs={{0,4},{4,8},{8,12},{12,14},{14,10},{10,6},{6,2},{2,0},{1,5},{5,9},... | collective-permute-start | bytes 393224 | tf_op jit(solution)/shard_map/ppermute | solution.py:230
  19.9 5.9 %collective-permute-start.5 = (bf16[256,256]{1,0:T(8,128)(2,1)S(1)}, bf16[256,256]{1,0:T(8,128)(2,1)S(1)}, u32[]{:S(2)}, u32[]{:S(2)}) collective-permute-start(bf16[256,256]{1,0:T(8,128)(2,1)S(1)} %collective-permute-done.4.refs_1_), channel_id=1, source_target_pairs={{4,0},{8,4},{12,8},{14,12},{10,14},{6,10},{2,6},{0,2},{5,1},{9,5},... | collective-permute-start | bytes 393224 | tf_op jit(solution)/shard_map/ppermute | solution.py:230
  20.8 6.1 %collective-permute-start.13 = (bf16[256,256]{1,0:T(8,128)(2,1)S(1)}, bf16[256,256]{1,0:T(8,128)(2,1)S(1)}, u32[]{:S(2)}, u32[]{:S(2)}) collective-permute-start(bf16[256,256]{1,0:T(8,128)(2,1)S(1)} %collective-permute-done.8.refs_2_), channel_id=1, source_target_pairs={{0,4},{4,8},{8,12},{12,14},{14,10},{10,6},{6,2},{2,0},{1,5},{5,9},... | collective-permute-start | bytes 393224 | tf_op jit(solution)/shard_map/ppermute | solution.py:230
  22.7 5.0 %collective-permute-start.14 = (bf16[256,256]{1,0:T(8,128)(2,1)S(1)}, bf16[256,256]{1,0:T(8,128)(2,1)S(1)}, u32[]{:S(2)}, u32[]{:S(2)}) collective-permute-start(bf16[256,256]{1,0:T(8,128)(2,1)S(1)} %collective-permute-done.11.refs_3_), channel_id=1, source_target_pairs={{4,0},{8,4},{12,8},{14,12},{10,14},{6,10},{2,6},{0,2},{5,1},{9,5},... | collective-permute-start | bytes 393224 | tf_op jit(solution)/shard_map/ppermute | solution.py:230
  28.2 2.0 %collective-permute-start.15 = (bf16[1024,256]{1,0:T(8,128)(2,1)S(1)}, bf16[1024,256]{1,0:T(8,128)(2,1)S(1)}, u32[]{:S(2)}, u32[]{:S(2)}) collective-permute-start(bf16[1024,256]{1,0:T(8,128)(2,1)S(1)} %get-tuple-element.57), channel_id=1, source_target_pairs={{0,1},{1,0},{2,3},{3,2},{4,5},{5,4},{6,7},{7,6},{8,9},{9,8},{10,11... | collective-permute-start | bytes 1572872 | tf_op jit(solution)/shard_map/ppermute | solution.py:336
  30.8 5.6 %collective-permute-start.16 = (bf16[256,256]{1,0:T(8,128)(2,1)S(1)}, bf16[256,256]{1,0:T(8,128)(2,1)S(1)}, u32[]{:S(2)}, u32[]{:S(2)}) collective-permute-start(bf16[256,256]{1,0:T(8,128)(2,1)S(1)} %get-tuple-element.59), channel_id=1, source_target_pairs={{4,0},{8,4},{12,8},{14,12},{10,14},{6,10},{2,6},{0,2},{5,1},{9,5},... | collective-permute-start | bytes 393224 | tf_op jit(solution)/shard_map/ppermute | solution.py:230
  31.0 6.3 %collective-permute-start.20 = (bf16[256,256]{1,0:T(8,128)(2,1)S(1)}, bf16[256,256]{1,0:T(8,128)(2,1)S(1)}, u32[]{:S(2)}, u32[]{:S(2)}) collective-permute-start(bf16[256,256]{1,0:T(8,128)(2,1)S(1)} %get-tuple-element.61), channel_id=1, source_target_pairs={{0,4},{4,8},{8,12},{12,14},{14,10},{10,6},{6,2},{2,0},{1,5},{5,9},... | collective-permute-start | bytes 393224 | tf_op jit(solution)/shard_map/ppermute | solution.py:230
  33.3 6.6 %collective-permute-start.19 = (bf16[256,256]{1,0:T(8,128)(2,1)S(1)}, bf16[256,256]{1,0:T(8,128)(2,1)S(1)}, u32[]{:S(2)}, u32[]{:S(2)}) collective-permute-start(bf16[256,256]{1,0:T(8,128)(2,1)S(1)} %get-tuple-element.64), channel_id=1, source_target_pairs={{0,4},{4,8},{8,12},{12,14},{14,10},{10,6},{6,2},{2,0},{1,5},{5,9},... | collective-permute-start | bytes 393224 | tf_op jit(solution)/shard_map/ppermute | solution.py:230
  35.0 6.8 %collective-permute-start.27 = (bf16[256,256]{1,0:T(8,128)(2,1)S(1)}, bf16[256,256]{1,0:T(8,128)(2,1)S(1)}, u32[]{:S(2)}, u32[]{:S(2)}) collective-permute-start(bf16[256,256]{1,0:T(8,128)(2,1)S(1)} %get-tuple-element.81), channel_id=1, source_target_pairs={{4,0},{8,4},{12,8},{14,12},{10,14},{6,10},{2,6},{0,2},{5,1},{9,5},... | collective-permute-start | bytes 393224 | tf_op jit(solution)/shard_map/ppermute | solution.py:230
  36.4 6.2 %collective-permute-start.17 = (bf16[256,256]{1,0:T(8,128)(2,1)S(1)}, bf16[256,256]{1,0:T(8,128)(2,1)S(1)}, u32[]{:S(2)}, u32[]{:S(2)}) collective-permute-start(bf16[256,256]{1,0:T(8,128)(2,1)S(1)} %add_convert_fusion.9), channel_id=1, source_target_pairs={{4,0},{8,4},{12,8},{14,12},{10,14},{6,10},{2,6},{0,2},{5,1},{9,5},... | collective-permute-start | bytes 393224 | tf_op jit(solution)/shard_map/ppermute | solution.py:394
  37.4 6.4 %collective-permute-start.21 = (bf16[256,256]{1,0:T(8,128)(2,1)S(1)}, bf16[256,256]{1,0:T(8,128)(2,1)S(1)}, u32[]{:S(2)}, u32[]{:S(2)}) collective-permute-start(bf16[256,256]{1,0:T(8,128)(2,1)S(1)} %add_convert_fusion.6), channel_id=1, source_target_pairs={{0,4},{4,8},{8,12},{12,14},{14,10},{10,6},{6,2},{2,0},{1,5},{5,9},... | collective-permute-start | bytes 393224 | tf_op jit(solution)/shard_map/ppermute | solution.py:394
  39.9 6.5 %collective-permute-start.25 = (bf16[256,256]{1,0:T(8,128)(2,1)S(1)}, bf16[256,256]{1,0:T(8,128)(2,1)S(1)}, u32[]{:S(2)}, u32[]{:S(2)}) collective-permute-start(bf16[256,256]{1,0:T(8,128)(2,1)S(1)} %add_convert_fusion.5), channel_id=1, source_target_pairs={{0,4},{4,8},{8,12},{12,14},{14,10},{10,6},{6,2},{2,0},{1,5},{5,9},... | collective-permute-start | bytes 393224 | tf_op jit(solution)/shard_map/ppermute | solution.py:394
  41.7 6.4 %collective-permute-start.28 = (bf16[256,256]{1,0:T(8,128)(2,1)S(1)}, bf16[256,256]{1,0:T(8,128)(2,1)S(1)}, u32[]{:S(2)}, u32[]{:S(2)}) collective-permute-start(bf16[256,256]{1,0:T(8,128)(2,1)S(1)} %add_convert_fusion.1), channel_id=1, source_target_pairs={{4,0},{8,4},{12,8},{14,12},{10,14},{6,10},{2,6},{0,2},{5,1},{9,5},... | collective-permute-start | bytes 393224 | tf_op jit(solution)/shard_map/ppermute | solution.py:394
  42.7 8.5 %collective-permute-start.18 = (bf16[256,256]{1,0:T(8,128)(2,1)S(1)}, bf16[256,256]{1,0:T(8,128)(2,1)S(1)}, u32[]{:S(2)}, u32[]{:S(2)}) collective-permute-start(bf16[256,256]{1,0:T(8,128)(2,1)S(1)} %add_convert_fusion.8), channel_id=1, source_target_pairs={{4,0},{8,4},{12,8},{14,12},{10,14},{6,10},{2,6},{0,2},{5,1},{9,5},... | collective-permute-start | bytes 393224 | tf_op jit(solution)/shard_map/ppermute | solution.py:394
  43.9 5.7 %collective-permute-start.22 = (bf16[256,256]{1,0:T(8,128)(2,1)S(1)}, bf16[256,256]{1,0:T(8,128)(2,1)S(1)}, u32[]{:S(2)}, u32[]{:S(2)}) collective-permute-start(bf16[256,256]{1,0:T(8,128)(2,1)S(1)} %add_convert_fusion.4), channel_id=1, source_target_pairs={{0,4},{4,8},{8,12},{12,14},{14,10},{10,6},{6,2},{2,0},{1,5},{5,9},... | collective-permute-start | bytes 393224 | tf_op jit(solution)/shard_map/ppermute | solution.py:394
  46.4 7.3 %collective-permute-start.26 = (bf16[256,256]{1,0:T(8,128)(2,1)S(1)}, bf16[256,256]{1,0:T(8,128)(2,1)S(1)}, u32[]{:S(2)}, u32[]{:S(2)}) collective-permute-start(bf16[256,256]{1,0:T(8,128)(2,1)S(1)} %add_convert_fusion.2), channel_id=1, source_target_pairs={{0,4},{4,8},{8,12},{12,14},{14,10},{10,6},{6,2},{2,0},{1,5},{5,9},... | collective-permute-start | bytes 393224 | tf_op jit(solution)/shard_map/ppermute | solution.py:394
  48.2 5.5 %collective-permute-start.29 = (bf16[256,256]{1,0:T(8,128)(2,1)S(1)}, bf16[256,256]{1,0:T(8,128)(2,1)S(1)}, u32[]{:S(2)}, u32[]{:S(2)}) collective-permute-start(bf16[256,256]{1,0:T(8,128)(2,1)S(1)} %add_convert_fusion), channel_id=1, source_target_pairs={{4,0},{8,4},{12,8},{14,12},{10,14},{6,10},{2,6},{0,2},{5,1},{9,5},... | collective-permute-start | bytes 393224 | tf_op jit(solution)/shard_map/ppermute | solution.py:394
  49.1 7.2 %copy-start = (bf16[256,256]{1,0:T(8,128)(2,1)S(1)}, bf16[256,256]{1,0:T(8,128)(2,1)}, u32[]{:S(2)}) copy-start(bf16[256,256]{1,0:T(8,128)(2,1)} %w.1) | copy-start | bytes 393220
  49.6 5.0 %collective-permute-start.23 = (bf16[256,256]{1,0:T(8,128)(2,1)S(1)}, bf16[256,256]{1,0:T(8,128)(2,1)S(1)}, u32[]{:S(2)}, u32[]{:S(2)}) collective-permute-start(bf16[256,256]{1,0:T(8,128)(2,1)S(1)} %add_convert_fusion.3), channel_id=1, source_target_pairs={{0,4},{4,8},{8,12},{12,14},{14,10},{10,6},{6,2},{2,0},{1,5},{5,9},... | collective-permute-start | bytes 393224 | tf_op jit(solution)/shard_map/ppermute | solution.py:394
  51.2 5.0 %collective-permute-start.24 = (bf16[256,256]{1,0:T(8,128)(2,1)S(1)}, bf16[256,256]{1,0:T(8,128)(2,1)S(1)}, u32[]{:S(2)}, u32[]{:S(2)}) collective-permute-start(bf16[256,256]{1,0:T(8,128)(2,1)S(1)} %add_convert_fusion.7), channel_id=1, source_target_pairs={{4,0},{8,4},{12,8},{14,12},{10,14},{6,10},{2,6},{0,2},{5,1},{9,5},... | collective-permute-start | bytes 393224 | tf_op jit(solution)/shard_map/ppermute | solution.py:394
